TPU v7x, 256 devices: a whole 4x4x8 slice. The times are simulated.
256 devices in a mesh: dp: 2 (over x_lo), col: 32 (over y, z), row: 4 (over x_hi, core).
Axes of the slice: x: 4 (x_hi: 2, x_lo: 2; x = x_hi * 2 + x_lo), y: 4, z: 8, core: 2. Of those that a mesh axis runs over, the one named last changes fastest.
Arguments:
- cotangent: bfloat16 [4096, 7168], P(('dp', 'col'), 'row'), may hold values from -6 to 6
- codes: bfloat16 [7168, 20480], P('row', 'col'), may hold values from -1 to 1, as said below
- weight_scale: float32 [1], replicated, may hold values from 0.008 to 0.03
- rotated: bfloat16 [4096, 20480], P(('dp', 'row'), 'col'), may hold values from -6 to 6
- clip_level: float32 [4096], P(('dp', 'row')), may hold values from 0.5 to 3
Outputs:
- input_grad: bfloat16 [4096, 20480], P(('dp', 'row'), 'col')
- weight_grad: float32 [7168, 20480], P('row', 'col')
Inputs may be any that keep to these rules, and one draw needn't show every extreme that they name: `codes`: every entry is -1, 0 or 1.
All inputs are finite; a program needn't handle non-finite values.
Results may differ from a plain program's by a relative error of at most 0.015.
Values may be sent and summed in bfloat16 or wider, within the bound.
No kernel may reach another device: no remote copies, remote signals or barrier semaphores. Data moves between devices by JAX's collectives and lax.ppermute only.
A program may use at most 64 MiB of HBM per device.

v0:
```python
import jax
import jax.numpy as jnp
from jax import lax
from jax.sharding import PartitionSpec as P

HB = 128


def hadamard_table(length):
    indices = jnp.arange(length, dtype=jnp.int32)
    parity = jnp.zeros((length, length), jnp.int32)
    for bit_place in range(length.bit_length() - 1):
        lower = indices[:, None] // 2**bit_place % 2
        upper = indices[None, :] // 2**bit_place % 2
        parity = parity + lower * upper
    signs = (1 - 2 * (parity % 2)).astype(jnp.float32)
    return signs / jnp.sqrt(jnp.float32(length))


def body(cotangent, codes, weight_scale, rotated, clip_level):
    bound_col = clip_level[:, None]
    rotated_wide = rotated.astype(jnp.float32)
    clipped = jnp.clip(rotated_wide, -bound_col, bound_col).astype(jnp.bfloat16)
    clip_all = lax.all_gather(clipped, "row", axis=0, tiled=True)
    token_total = cotangent.shape[0] * lax.axis_size("col") * lax.axis_size("dp")
    grad_norm = token_total ** (-0.5)
    weight_mult = weight_scale[0]
    gathered = lax.all_gather(cotangent, "col", axis=0, tiled=True)
    weight_part = jnp.dot(gathered.T, clip_all, preferred_element_type=jnp.float32) * grad_norm
    partial_value = jnp.dot(gathered, codes, preferred_element_type=jnp.float32) * weight_mult
    weight_grad = lax.psum(weight_part.astype(jnp.bfloat16), "dp").astype(jnp.float32)
    summed = lax.psum_scatter(
        partial_value.astype(jnp.bfloat16), "row", scatter_dimension=0, tiled=True
    ).astype(jnp.float32)
    masked = jnp.where(jnp.abs(rotated_wide) <= bound_col, summed, jnp.float32(0.0))
    rotation = hadamard_table(HB)
    local_rows = masked.shape[0]
    local_cols = masked.shape[1]
    blocks = masked.reshape(local_rows, local_cols // HB, HB)
    input_grad = (
        jnp.einsum("tbi,ij->tbj", blocks, rotation, precision=lax.Precision.HIGHEST)
        .reshape(local_rows, local_cols)
        .astype(jnp.bfloat16)
    )
    return (input_grad, weight_grad)


def solution(mesh):
    placed = (
        P(("dp", "col"), "row"),
        P("row", "col"),
        P(),
        P(("dp", "row"), "col"),
        P(("dp", "row")),
    )
    return jax.shard_map(
        body,
        mesh=mesh,
        in_specs=placed,
        out_specs=(P(("dp", "row"), "col"), P("row", "col")),
        check_vma=False,
    )
```

profile of v0, /device:TPU:1, one launch (start us, length us, event | category | flops | bytes accessed | tf_op | source)
XLA Modules:
  0.0 294.3 jit_solution(15819114711039269136)
XLA Ops:
  7.2 0.0 copy-start
  7.2 0.0 all-gather.5.cloned.1.call-start
  7.2 0.8 neg.4
  8.1 2.2 fusion.3
  10.3 0.0 all-gather.5.cloned.1.call-update
  10.3 0.0 all-gather.3.cloned.1.call-start
  10.3 0.7 all-gather.3.cloned.1.call-update
  11.0 0.0 all-reduce.2.cloned.1.call-start
  11.1 35.7 %all-gather.5.cloned.1.call-done = bf16[2048,640]{1,0:T(8,128)(2,1)} async-done(((bf16[512,640]{1,0:T(8,128)(2,1)}), bf16[2048,640]{1,0:T(8,128)(2,1)}) %all-gather.5.cloned.1.call-update) | async-done | bytes 2621456 | tf_op jit(solution)/shard_map/all_gather | solution.py:24
  46.8 94.6 %all-gather.3.cloned.1.call-done = bf16[2048,1792]{1,0:T(8,128)(2,1)} async-done(((bf16[64,1792]{1,0:T(8,128)(2,1)}), bf16[2048,1792]{1,0:T(8,128)(2,1)}) %all-gather.3.cloned.1.call-update) | async-done | bytes 7340048 | tf_op jit(solution)/shard_map/all_gather | solution.py:28
  141.4 10.3 %fusion = bf16[1792,640]{0,1:T(8,128)(2,1)} fusion(bf16[2048,640]{1,0:T(8,128)(2,1)} %all-gather.5.cloned.1.call-done, bf16[2048,1792]{1,0:T(8,128)(2,1)} %all-gather.3.cloned.1.call-done), kind=kOutput, calls=%fused_computation.2 | convolution fusion | flops 4699914240 | bytes 12255232 | tf_op jit(solution)/shard_map/dot_general | solution.py:29
  151.6 0.0 all-reduce.2.cloned.1.call-update
  151.7 0.0 reduce-scatter.2.cloned.1.call-start
  152.4 0.0 copy-done
  152.4 9.2 %multiply_convert_fusion = bf16[2048,640]{1,0:T(8,128)(2,1)} fusion(bf16[2048,1792]{1,0:T(8,128)(2,1)} %all-gather.3.cloned.1.call-done, bf16[1792,640]{1,0:T(8,128)(2,1)S(1)} %copy-done, f32[]{:T(128)} %bitcast.13), kind=kOutput, calls=%fused_computation | convolution fusion | flops 4700241920 | bytes 12255236 | tf_op jit(solution)/shard_map/dot_general | solution.py:30
  161.6 0.0 reduce-scatter.2.cloned.1.call-update
  161.6 0.0 copy-start.1
  161.6 0.0 copy-start.2
  161.6 66.6 %all-reduce.2.cloned.1.call-done = bf16[1792,640]{0,1:T(8,128)(2,1)} async-done(((bf16[1792,640]{0,1:T(8,128)(2,1)}), bf16[1792,640]{0,1:T(8,128)(2,1)}) %all-reduce.2.cloned.1.call-update) | async-done | bytes 2293776 | tf_op jit(solution)/shard_map/psum | solution.py:31
  228.2 4.6 %copy.13 = f32[1792,640]{1,0:T(8,128)} copy(bf16[1792,640]{0,1:T(8,128)(2,1)} %all-reduce.2.cloned.1.call-done) | data formatting | bytes 6881280
  232.8 46.0 %reduce-scatter.2.cloned.1.call-done = bf16[512,640]{1,0:T(8,128)(2,1)} async-done(((bf16[2048,640]{1,0:T(8,128)(2,1)}), bf16[512,640]{1,0:T(8,128)(2,1)}) %reduce-scatter.2.cloned.1.call-update) | async-done | bytes 655376 | tf_op jit(solution)/shard_map/reduce_scatter | solution.py:32
  278.8 0.0 copy-done.1
  278.8 0.0 copy-done.2
  278.8 2.4 convert_select_fusion
  281.2 2.8 copy.10
  284.0 2.7 convolution_convert_fusion
  286.7 1.1 copy.12
  (4 shorter events, 0.0 us)
Async XLA Ops:
  7.2 145.2 %copy-start = (bf16[1792,640]{1,0:T(8,128)(2,1)S(1)}, bf16[1792,640]{1,0:T(8,128)(2,1)}, u32[]{:S(2)}) copy-start(bf16[1792,640]{1,0:T(8,128)(2,1)} %param.6) | copy-start | bytes 6881284
  7.2 39.6 %all-gather.5.cloned.1.call-start = ((), (), s32[]{:S(2)}) async-start(), calls=%async_computation.3 | async-start | bytes 3276800 | tf_op jit(solution)/shard_map/all_gather | solution.py:24
  10.3 131.1 %all-gather.3.cloned.1.call-start = ((), (), s32[]{:S(2)}) async-start(), calls=%async_computation.1 | async-start | bytes 7569408 | tf_op jit(solution)/shard_map/all_gather | solution.py:28
  11.0 217.2 %all-reduce.2.cloned.1.call-start = ((), (), s32[]{:S(2)}) async-start(), calls=%async_computation.4 | async-start | bytes 4587520 | tf_op jit(solution)/shard_map/psum | solution.py:31
  151.7 127.1 %reduce-scatter.2.cloned.1.call-start = ((), (), s32[]{:S(2)}) async-start(), calls=%async_computation.2 | async-start | bytes 3276800 | tf_op jit(solution)/shard_map/reduce_scatter | solution.py:32
  161.6 117.2 %copy-start.1 = (bf16[512,640]{1,0:T(8,128)(2,1)S(1)}, bf16[512,640]{1,0:T(8,128)(2,1)}, u32[]{:S(2)}) copy-start(bf16[512,640]{1,0:T(8,128)(2,1)} %param.8) | copy-start | bytes 1966084
  161.6 117.2 %copy-start.2 = (f32[512]{0:T(512)S(1)}, f32[512]{0:T(512)}, u32[]{:S(2)}) copy-start(f32[512]{0:T(512)} %param.9) | copy-start | bytes 6148
Sparse Core Ops, SparseCore 0:
  10.4 36.3 all-gather.4
  49.4 91.9 all-gather.2
  151.8 76.3 all-reduce.1
  231.1 47.6 reduce-scatter.1
where the time goes:
time: 295 us; the launch traced here: 294 us
  waiting for transfers between devices  244 us (83%)
  matrix products  22.1 us (7%)
  between operations  14.5 us (5%)
  local copies, waits for them, and re-layouts  8.44 us (3%)
  other arithmetic  5.46 us (2%)
    all_gather x1, waiting for transfers between devices, body(): gathered = lax.all_gather(cotangent, 'col', axis=0, tiled=True)  94.6 us
    psum x1, waiting for transfers between devices, body(): lax.psum(weight_part.astype(jnp.bfloat16), 'dp').astype(jnp.float32)  66.6 us
    reduce_scatter x1, waiting for transfers between devices, body(): lax.psum_scatter(partial_value.astype(jnp.bfloat16), 'row', scatter_dimen...  46 us
    all_gather x1, waiting for transfers between devices, body(): clip_all = lax.all_gather(clipped, 'row', axis=0, tiled=True)  35.7 us
    dot_general x1, matrix products, body(): jnp.dot(gathered.T, clip_all, preferred_element_type=jnp.float32)  10.3 us
    dot_general x1, matrix products, body(): jnp.dot(gathered, codes, preferred_element_type=jnp.float32) * weight_mult  9.18 us
  transfers between devices with their start and end apart: 4, of which 4 were waited for; matrix products, arithmetic and copies ran while one was open for 5% of the time, Pallas kernels for 0%

commit v1 on v0

v1 whole, which is shorter than its diff:
```python
import functools

import jax
import jax.numpy as jnp
from jax import lax
from jax.experimental import pallas as pl
from jax.experimental.pallas import tpu as pltpu
from jax.sharding import PartitionSpec as P

HB = 128
NY, NZ = 4, 8
SHARD = 64
BF = jnp.bfloat16
F32 = jnp.float32

CHUNKS = (("zy", 1024), ("yz", 768))


def z_pairs(k):
    return [(y * NZ + z, y * NZ + (z + k) % NZ) for y in range(NY) for z in range(NZ)]


def y_pairs(k):
    return [(y * NZ + z, (y + k) % NY * NZ + z) for y in range(NY) for z in range(NZ)]


CORE = [(r, r ^ 1) for r in range(4)]
DP = [(0, 1), (1, 0)]
PARTNER = [(d * 4 + r, (1 - d) * 4 + (r ^ 2)) for d in range(2) for r in range(4)]
SWAP = [
    ((d * 32 + c) * 4 + r, ((d ^ (c // 16 != r // 2)) * 32 + c) * 4 + r)
    for d in range(2)
    for c in range(32)
    for r in range(4)
]


def gather_zy(shard):
    ups, downs = [shard], [shard]
    for _ in range(4):
        ups.append(lax.ppermute(ups[-1], "col", z_pairs(1)))
        if len(downs) < 4:
            downs.append(lax.ppermute(downs[-1], "col", z_pairs(-1)))
    line = jnp.concatenate(ups + downs[1:], axis=0)
    order = [0, -1, -2, -3, -4, 1, 2, 3]
    half = line.shape[0] // 2
    up = lax.ppermute(line, "col", y_pairs(1))
    down = lax.ppermute(line, "col", y_pairs(-1))
    up_far = lax.ppermute(up[:half], "col", y_pairs(1))
    down_far = lax.ppermute(down[half:], "col", y_pairs(-1))
    pieces = [line, up, down, up_far, down_far]
    places = [
        [(0, z) for z in order],
        [(-1, z) for z in order],
        [(1, z) for z in order],
        [(-2, z) for z in order[:4]],
        [(2, z) for z in order[4:]],
    ]
    return pieces, places


def gather_yz(shard):
    line = jnp.concatenate(
        [
            shard,
            lax.ppermute(shard, "col", y_pairs(1)),
            lax.ppermute(shard, "col", y_pairs(-1)),
            lax.ppermute(shard, "col", y_pairs(2)),
        ],
        axis=0,
    )
    order = [0, -1, 1, 2]
    half = line.shape[0] // 2
    pieces, places = [line], [[(y, 0) for y in order]]
    for sign in (1, -1):
        held = line
        for step in range(1, 4):
            held = lax.ppermute(held, "col", z_pairs(sign))
            pieces.append(held)
            places.append([(y, -sign * step) for y in order])
        if sign == 1:
            pieces.append(lax.ppermute(held[:half], "col", z_pairs(sign)))
            places.append([(y, 4) for y in order[:2]])
        else:
            pieces.append(lax.ppermute(held[half:], "col", z_pairs(sign)))
            places.append([(y, 4) for y in order[2:]])
    return pieces, places


def load_tokens(where, refs, places, held, sem):
    copies = []
    for ref, spots in zip(refs, places):
        for at, (dy, dz) in enumerate(spots):
            row = lax.rem(where[0] + dy + NY, NY) * NZ + lax.rem(where[1] + dz + NZ, NZ)
            copies.append(
                pltpu.make_async_copy(
                    ref.at[pl.ds(at * SHARD, SHARD)],
                    held.at[pl.ds(pl.multiple_of(row * SHARD, SHARD), SHARD)],
                    sem,
                )
            )
    return copies


def weight_kernel(places, scale, where, *refs):
    n = len(places)
    piece_refs, clip_refs, out, held, clip_held, sem = (
        refs[:n], refs[n:n + 4], refs[n + 4], refs[n + 5], refs[n + 6], refs[n + 7])
    copies = load_tokens(where, piece_refs, places, held, sem)
    rows = clip_refs[0].shape[0]
    for j, ref in enumerate(clip_refs):
        start = pl.multiple_of((where[2] ^ j) * rows, rows)
        copies.append(pltpu.make_async_copy(ref, clip_held.at[pl.ds(start, rows)], sem))
    for copy in copies:
        copy.start()
    for copy in copies:
        copy.wait()
    width = out.shape[0]
    for lo in range(0, width, 256):
        size = min(256, width - lo)
        out[lo:lo + size, :] = (
            lax.dot_general(
                held[:, lo:lo + size], clip_held[...], (((0,), (0,)), ((), ())),
                preferred_element_type=F32,
            ) * scale
        ).astype(BF)


def weight_term(where, pieces, places, clips, scale):
    width = pieces[0].shape[1]
    tokens = 4 * clips[0].shape[0]
    cols = clips[0].shape[1]
    anywhere = pl.BlockSpec(memory_space=pl.ANY)
    return pl.pallas_call(
        functools.partial(weight_kernel, places, scale),
        out_shape=jax.ShapeDtypeStruct((width, cols), BF),
        in_specs=[pl.BlockSpec(memory_space=pltpu.SMEM)] + [anywhere] * (len(pieces) + 4),
        out_specs=pl.BlockSpec(memory_space=pltpu.VMEM),
        scratch_shapes=[
            pltpu.VMEM((tokens, width), BF),
            pltpu.VMEM((tokens, cols), BF),
            pltpu.SemaphoreType.DMA,
        ],
        compiler_params=pltpu.CompilerParams(vmem_limit_bytes=48 * 2**20),
        cost_estimate=pl.CostEstimate(
            flops=2 * tokens * width * cols,
            bytes_accessed=2 * (tokens * (width + cols) + width * cols),
            transcendentals=0),
        name="weight_term",
    )(where, *pieces, *clips)


def act_kernel(all_places, starts, where, weight_scale, codes, *refs):
    n = sum(len(p) for p in all_places)
    piece_refs = refs[:n]
    outs, held, code_held, sem = refs[n:n + 4], refs[n + 4], refs[n + 5], refs[n + 6]
    copies = [pltpu.make_async_copy(codes, code_held, sem)]
    at = 0
    for places, start in zip(all_places, starts):
        here = piece_refs[at:at + len(places)]
        at += len(places)
        width = here[0].shape[1]
        copies += load_tokens(where, here, places, held.at[:, pl.ds(start, width)], sem)
    for copy in copies:
        copy.start()
    for copy in copies:
        copy.wait()
    rows = outs[0].shape[0]
    for j in (3, 2, 1, 0):
        start = pl.multiple_of((where[2] ^ j) * rows, rows)
        outs[j][...] = (
            jnp.dot(held[pl.ds(start, rows), :], code_held[...], preferred_element_type=F32)
            * weight_scale[0]
        ).astype(BF)


def act_parts(where, weight_scale, codes, gathered, starts):
    depth, cols = codes.shape
    tokens = 2048
    pieces = [p for g in gathered for p in g[0]]
    anywhere = pl.BlockSpec(memory_space=pl.ANY)
    smem = pl.BlockSpec(memory_space=pltpu.SMEM)
    return pl.pallas_call(
        functools.partial(act_kernel, [g[1] for g in gathered], starts),
        out_shape=[jax.ShapeDtypeStruct((tokens // 4, cols), BF)] * 4,
        in_specs=[smem, smem] + [anywhere] * (len(pieces) + 1),
        out_specs=[pl.BlockSpec(memory_space=pltpu.VMEM)] * 4,
        scratch_shapes=[
            pltpu.VMEM((tokens, depth), BF),
            pltpu.VMEM((depth, cols), BF),
            pltpu.SemaphoreType.DMA,
        ],
        compiler_params=pltpu.CompilerParams(vmem_limit_bytes=48 * 2**20),
        cost_estimate=pl.CostEstimate(
            flops=2 * tokens * depth * cols,
            bytes_accessed=2 * (tokens * (depth + cols) + depth * cols),
            transcendentals=0),
        name="act_parts",
    )(where, weight_scale, codes, *pieces)


def finish_kernel(own, sibling, other, rotated, bound, signs, out):
    summed = own[...].astype(F32) + sibling[...].astype(F32) + other[...].astype(F32)
    masked = jnp.where(jnp.abs(rotated[...].astype(F32)) <= bound[...], summed, 0.0)
    high = masked.astype(BF)
    low = (masked - high.astype(F32)).astype(BF)
    table = signs[...]
    for lo in range(0, out.shape[1], HB):
        turned = jnp.dot(high[:, lo:lo + HB], table, preferred_element_type=F32)
        turned += jnp.dot(low[:, lo:lo + HB], table, preferred_element_type=F32)
        out[:, lo:lo + HB] = (turned * (HB ** -0.5)).astype(BF)


def finish(own, sibling, other, rotated, bound, signs):
    vmem = pl.BlockSpec(memory_space=pltpu.VMEM)
    return pl.pallas_call(
        finish_kernel,
        out_shape=jax.ShapeDtypeStruct(own.shape, BF),
        in_specs=[vmem] * 6,
        out_specs=vmem,
        compiler_params=pltpu.CompilerParams(vmem_limit_bytes=48 * 2**20),
        name="finish",
    )(own, sibling, other, rotated, bound, signs)


def hadamard_signs(length):
    indices = jnp.arange(length, dtype=jnp.int32)
    common = indices[:, None] & indices[None, :]
    parity = jnp.zeros((length, length), jnp.int32)
    for bit in range(length.bit_length() - 1):
        parity = parity ^ (common >> bit)
    return (1 - 2 * (parity & 1)).astype(BF)


def body(cotangent, codes, weight_scale, rotated, clip_level):
    col = lax.axis_index("col")
    row = lax.axis_index("row")
    where = jnp.stack([col // NZ, col % NZ, row]).astype(jnp.int32)
    token_total = cotangent.shape[0] * lax.axis_size("col") * lax.axis_size("dp")
    grad_norm = token_total ** (-0.5)

    gathered, starts, lo = [], [], 0
    for kind, width in CHUNKS:
        shard = lax.ppermute(cotangent[:, lo:lo + width], ("dp", "col", "row"), SWAP)
        gathered.append((gather_zy if kind == "zy" else gather_yz)(shard))
        starts.append(lo)
        lo += width

    bound = clip_level[:, None]
    clipped = jnp.clip(rotated.astype(F32), -bound, bound).astype(BF)
    other = lax.ppermute(clipped, ("dp", "row"), PARTNER)
    clips = [
        clipped,
        lax.ppermute(clipped, "row", CORE),
        other,
        lax.ppermute(other, "row", CORE),
    ]

    terms = []
    for pieces, places in gathered:
        mine = weight_term(where, pieces, places, clips, grad_norm)
        theirs = lax.ppermute(mine, "dp", DP)
        terms.append(mine.astype(F32) + theirs.astype(F32))
    weight_grad = jnp.concatenate(terms, axis=0)

    parts = act_parts(where, weight_scale, codes, gathered, starts)
    from_sibling = lax.ppermute(parts[3], "row", CORE)
    outward = (parts[2].astype(F32) + from_sibling.astype(F32)).astype(BF)
    inward = lax.ppermute(outward, ("dp", "row"), PARTNER)
    sibling = lax.ppermute(parts[1], "row", CORE)
    input_grad = finish(parts[0], sibling, inward, rotated, bound, hadamard_signs(HB))
    return (input_grad, weight_grad)


def solution(mesh):
    placed = (
        P(("dp", "col"), "row"),
        P("row", "col"),
        P(),
        P(("dp", "row"), "col"),
        P(("dp", "row")),
    )
    return jax.shard_map(
        body,
        mesh=mesh,
        in_specs=placed,
        out_specs=(P(("dp", "row"), "col"), P("row", "col")),
        check_vma=False,
    )
```

time: 295 us -> 165 us (0.56)
  the two profiles are of different devices: /device:TPU:1 before, /device:TPU:8 now
where the time goes in v1:
time: 165 us; the launch traced here: 164 us
  waiting for transfers between devices  60.2 us (36%)
  starting transfers between devices  49.4 us (30%)
  Pallas kernels  32.6 us (20%)
  local copies, waits for them, and re-layouts  13.1 us (8%)
  other arithmetic  6.95 us (4%)
  between operations  1.74 us (1%)
    ppermute x2, waiting for transfers between devices, body(): theirs = lax.ppermute(mine, 'dp', DP)  24.7 us
    pallas_call x2, Pallas kernels, weight_term(): pl.pallas_call(functools.partial(weight_kernel, places, scale), out_shape...  20.7 us
    ppermute x6, waiting for transfers between devices, gather_yz(): held = lax.ppermute(held, 'col', z_pairs(sign))  18.5 us
    ppermute x4, waiting for transfers between devices, gather_zy(): ups.append(lax.ppermute(ups[-1], 'col', z_pairs(1)))  13.4 us
    ppermute x3, starting transfers between devices, gather_zy(): downs.append(lax.ppermute(downs[-1], 'col', z_pairs(-1)))  12.5 us
    ppermute x6, starting transfers between devices, gather_yz(): held = lax.ppermute(held, 'col', z_pairs(sign))  11.1 us
    pallas_call x1, Pallas kernels, act_parts(): pl.pallas_call(functools.partial(act_kernel, [g[1] for g in gathered], st...  10.2 us
    unnamed x66, local copies, waits for them, and re-layouts  8.59 us
  transfers between devices with their start and end apart: 32, of which 11 were waited for; matrix products, arithmetic and copies ran while one was open for 6% of the time, Pallas kernels for 19%

profile of v1, /device:TPU:8, one launch (start us, length us, event | category | flops | bytes accessed | tf_op | source)
XLA Modules:
  0.0 163.9 jit_solution(9698249336124206480)
XLA Ops:
  0.7 1.0 slice.18
  2.3 0.9 slice.21
  4.6 1.9 %collective-permute-start.1 = (bf16[64,1024]{1,0:T(8,128)(2,1)S(1)}, bf16[64,1024]{1,0:T(8,128)(2,1)S(1)}, u32[]{:S(2)}, u32[]{:S(2)}) collective-permute-start(bf16[64,1024]{1,0:T(8,128)(2,1)S(1)} %collective-permute-done), channel_id=1, source_target_pairs={{0,4},{4,8},{8,12},{12,16},{16,20},{20,24},{24,28},{28,0},{32,36},... | collective-permute-start | bytes 393224 | tf_op jit(solution)/shard_map/ppermute | solution.py:41
  6.5 7.6 %collective-permute-start.13 = (bf16[64,768]{1,0:T(8,128)(2,1)S(1)}, bf16[64,768]{1,0:T(8,128)(2,1)S(1)}, u32[]{:S(2)}, u32[]{:S(2)}) collective-permute-start(bf16[64,768]{1,0:T(8,128)(2,1)S(1)} %collective-permute-done.12), channel_id=1, source_target_pairs={{0,32},{4,36},{8,40},{12,44},{16,48},{20,52},{24,56},{28,60},{32,6... | collective-permute-start | bytes 294920 | tf_op jit(solution)/shard_map/ppermute | solution.py:66
  14.1 2.7 %collective-permute-start.15 = (bf16[64,768]{1,0:T(8,128)(2,1)S(1)}, bf16[64,768]{1,0:T(8,128)(2,1)S(1)}, u32[]{:S(2)}, u32[]{:S(2)}) collective-permute-start(bf16[64,768]{1,0:T(8,128)(2,1)S(1)} %collective-permute-done.12), channel_id=1, source_target_pairs={{0,64},{4,68},{8,72},{12,76},{16,80},{20,84},{24,88},{28,92},{32,9... | collective-permute-start | bytes 294920 | tf_op jit(solution)/shard_map/ppermute | solution.py:68
  16.9 5.9 %collective-permute-start.5 = (bf16[64,1024]{1,0:T(8,128)(2,1)S(1)}, bf16[64,1024]{1,0:T(8,128)(2,1)S(1)}, u32[]{:S(2)}, u32[]{:S(2)}) collective-permute-start(bf16[64,1024]{1,0:T(8,128)(2,1)S(1)} %collective-permute-done), channel_id=1, source_target_pairs={{0,28},{4,0},{8,4},{12,8},{16,12},{20,16},{24,20},{28,24},{32,60},... | collective-permute-start | bytes 393224 | tf_op jit(solution)/shard_map/ppermute | solution.py:43
  22.9 6.1 %collective-permute-done.2 = bf16[64,1024]{1,0:T(8,128)(2,1)S(1)} collective-permute-done((bf16[64,1024]{1,0:T(8,128)(2,1)S(1)}, bf16[64,1024]{1,0:T(8,128)(2,1)S(1)}, u32[]{:S(2)}, u32[]{:S(2)}) %collective-permute-start.2) | collective-permute-done | bytes 131104 | tf_op jit(solution)/shard_map/ppermute | solution.py:41
  29.1 3.3 %collective-permute-start.6 = (bf16[64,1024]{1,0:T(8,128)(2,1)S(1)}, bf16[64,1024]{1,0:T(8,128)(2,1)S(1)}, u32[]{:S(2)}, u32[]{:S(2)}) collective-permute-start(bf16[64,1024]{1,0:T(8,128)(2,1)S(1)} %collective-permute-done.5), channel_id=1, source_target_pairs={{0,28},{4,0},{8,4},{12,8},{16,12},{20,16},{24,20},{28,24},{32,60},... | collective-permute-start | bytes 393224 | tf_op jit(solution)/shard_map/ppermute | solution.py:43
  32.5 4.2 %collective-permute-done.3 = bf16[64,1024]{1,0:T(8,128)(2,1)S(1)} collective-permute-done((bf16[64,1024]{1,0:T(8,128)(2,1)S(1)}, bf16[64,1024]{1,0:T(8,128)(2,1)S(1)}, u32[]{:S(2)}, u32[]{:S(2)}) %collective-permute-start.3) | collective-permute-done | bytes 131104 | tf_op jit(solution)/shard_map/ppermute | solution.py:41
  36.7 3.3 %collective-permute-start.7 = (bf16[64,1024]{1,0:T(8,128)(2,1)S(1)}, bf16[64,1024]{1,0:T(8,128)(2,1)S(1)}, u32[]{:S(2)}, u32[]{:S(2)}) collective-permute-start(bf16[64,1024]{1,0:T(8,128)(2,1)S(1)} %collective-permute-done.6), channel_id=1, source_target_pairs={{0,28},{4,0},{8,4},{12,8},{16,12},{20,16},{24,20},{28,24},{32,60},... | collective-permute-start | bytes 393224 | tf_op jit(solution)/shard_map/ppermute | solution.py:43
  40.0 3.0 %collective-permute-done.4 = bf16[64,1024]{1,0:T(8,128)(2,1)S(1)} collective-permute-done((bf16[64,1024]{1,0:T(8,128)(2,1)S(1)}, bf16[64,1024]{1,0:T(8,128)(2,1)S(1)}, u32[]{:S(2)}, u32[]{:S(2)}) %collective-permute-start.4) | collective-permute-done | bytes 131104 | tf_op jit(solution)/shard_map/ppermute | solution.py:41
  43.1 1.0 collective-permute-start.8
  44.4 2.1 %collective-permute-start.28 = (bf16[512,640]{1,0:T(8,128)(2,1)S(1)}, bf16[512,640]{1,0:T(8,128)(2,1)}, u32[]{:S(2)}, u32[]{:S(2)}) collective-permute-start(bf16[512,640]{1,0:T(8,128)(2,1)S(1)} %minimum_convert_fusion.refs_5_.refs_9_), channel_id=1, source_target_pairs={{0,130},{1,131},{2,128},{3,129},{128,2},{129,3},{130,0},{131,1},{4... | collective-permute-start | bytes 1966088 | tf_op jit(solution)/shard_map/ppermute | solution.py:251
  46.5 3.5 %collective-permute-start.20 = (bf16[256,768]{1,0:T(8,128)(2,1)S(1)}, bf16[256,768]{1,0:T(8,128)(2,1)S(1)}, u32[]{:S(2)}, u32[]{:S(2)}) collective-permute-start(bf16[256,768]{1,0:T(8,128)(2,1)S(1)} %constant_dynamic-update-slice_fusion.8.refs_5_.refs_0_), channel_id=1, source_target_pairs={{0,28},{4,0},{8,4},{12,8},{16,12},{20,16},{24,20},{28,24},{32,60},... | collective-permute-start | bytes 1179656 | tf_op jit(solution)/shard_map/ppermute | solution.py:78
  50.0 0.7 copy-done.14
  50.7 8.4 %collective-permute-done.20.refs_10_.refs_5_ = bf16[256,768]{1,0:T(8,128)(2,1)S(1)} collective-permute-done((bf16[256,768]{1,0:T(8,128)(2,1)S(1)}, bf16[256,768]{1,0:T(8,128)(2,1)S(1)}, u32[]{:S(2)}, u32[]{:S(2)}) %collective-permute-start.20) | collective-permute-done | bytes 393248 | tf_op jit(solution)/shard_map/ppermute | solution.py:78
  59.2 3.7 %collective-permute-start.21 = (bf16[256,768]{1,0:T(8,128)(2,1)S(1)}, bf16[256,768]{1,0:T(8,128)(2,1)S(1)}, u32[]{:S(2)}, u32[]{:S(2)}) collective-permute-start(bf16[256,768]{1,0:T(8,128)(2,1)S(1)} %collective-permute-done.20.refs_10_.refs_5_), channel_id=1, source_target_pairs={{0,28},{4,0},{8,4},{12,8},{16,12},{20,16},{24,20},{28,24},{32,60},... | collective-permute-start | bytes 1179656 | tf_op jit(solution)/shard_map/ppermute | solution.py:78
  63.0 5.2 %collective-permute-done.21.refs_11_.refs_6_ = bf16[256,768]{1,0:T(8,128)(2,1)S(1)} collective-permute-done((bf16[256,768]{1,0:T(8,128)(2,1)S(1)}, bf16[256,768]{1,0:T(8,128)(2,1)S(1)}, u32[]{:S(2)}, u32[]{:S(2)}) %collective-permute-start.21) | collective-permute-done | bytes 393248 | tf_op jit(solution)/shard_map/ppermute | solution.py:78
  68.2 3.8 %collective-permute-start.22 = (bf16[256,768]{1,0:T(8,128)(2,1)S(1)}, bf16[256,768]{1,0:T(8,128)(2,1)S(1)}, u32[]{:S(2)}, u32[]{:S(2)}) collective-permute-start(bf16[256,768]{1,0:T(8,128)(2,1)S(1)} %collective-permute-done.21.refs_11_.refs_6_), channel_id=1, source_target_pairs={{0,28},{4,0},{8,4},{12,8},{16,12},{20,16},{24,20},{28,24},{32,60},... | collective-permute-start | bytes 1179656 | tf_op jit(solution)/shard_map/ppermute | solution.py:78
  71.9 0.8 copy-done.23
  72.7 0.8 slice.24
  73.5 0.8 collective-permute-start.10
  74.3 0.9 slice.25
  75.7 0.8 collective-permute-start.11
  76.5 4.4 %collective-permute-done.22.refs_12_.refs_7_ = bf16[256,768]{1,0:T(8,128)(2,1)S(1)} collective-permute-done((bf16[256,768]{1,0:T(8,128)(2,1)S(1)}, bf16[256,768]{1,0:T(8,128)(2,1)S(1)}, u32[]{:S(2)}, u32[]{:S(2)}) %collective-permute-start.22) | collective-permute-done | bytes 393248 | tf_op jit(solution)/shard_map/ppermute | solution.py:78
  80.9 0.7 slice.27
  81.7 0.8 copy-done.11
  82.5 3.7 %collective-permute-start.23 = (bf16[128,768]{1,0:T(8,128)(2,1)}, bf16[128,768]{1,0:T(8,128)(2,1)}, u32[]{:S(2)}, u32[]{:S(2)}) collective-permute-start(bf16[128,768]{1,0:T(8,128)(2,1)} %slice.27), channel_id=1, source_target_pairs={{0,28},{4,0},{8,4},{12,8},{16,12},{20,16},{24,20},{28,24},{32,60},... | collective-permute-start | bytes 589832 | tf_op jit(solution)/shard_map/ppermute | solution.py:85
  87.0 2.4 %collective-permute-done.19.refs_9_.refs_4_ = bf16[128,768]{1,0:T(8,128)(2,1)S(1)} collective-permute-done((bf16[128,768]{1,0:T(8,128)(2,1)S(1)}, bf16[128,768]{1,0:T(8,128)(2,1)S(1)}, u32[]{:S(2)}, u32[]{:S(2)}) %collective-permute-start.19) | collective-permute-done | bytes 196640 | tf_op jit(solution)/shard_map/ppermute | solution.py:82
  89.3 1.2 collective-permute-done.23.refs_13_.refs_8_
  90.5 1.0 copy-done.7
  91.5 1.1 copy-done.12
  92.6 1.0 copy-done.15
  93.6 1.0 copy-done.18
  94.6 1.0 copy-done.21
  95.6 1.0 copy-done.24
  96.6 10.5 %weight_term.3 = bf16[768,640]{1,0:T(8,128)(2,1)} custom-call(s32[3]{0:T(128)S(1)} %pad_add_fusion.where, bf16[256,768]{1,0:T(8,128)(2,1)S(1)} %copy-done.7, bf16[256,768]{1,0:T(8,128)(2,1)S(1)} %copy-done.15, bf16[256,768]{1,0:T(8,128)(2,1)S(1)} %copy-done.21, bf16[256,768]{1,0:T(8,128)(2,1)S(1)} %collective-permute-done.18.refs_8_.refs_3_, ...), custom_call_target="tpu_custom_call" | custom-call | flops 2013265920 | bytes 6750208 | tf_op jit(solution)/shard_map/weight_term/pallas_call | solution.py:134
  107.1 0.9 collective-permute-start.31
  108.0 10.3 %weight_term.2 = bf16[1024,640]{1,0:T(8,128)(2,1)} custom-call(s32[3]{0:T(128)S(1)} %pad_add_fusion.where, bf16[512,1024]{1,0:T(8,128)(2,1)S(1)} %copy-done.10, bf16[512,1024]{1,0:T(8,128)(2,1)S(1)} %collective-permute-done.8.refs_1_, bf16[512,1024]{1,0:T(8,128)(2,1)} %copy-done.26, bf16[256,1024]{1,0:T(8,128)(2,1)} %collective-permute-done.10.refs_3_, ...), custom_call_target="tpu_custom_call" | custom-call | flops 2684354560 | bytes 8126464 | tf_op jit(solution)/shard_map/weight_term/pallas_call | solution.py:134
  118.3 1.5 collective-permute-start.30
  119.9 10.2 %act_parts.1 = (bf16[512,640]{1,0:T(8,128)(2,1)S(1)}, bf16[512,640]{1,0:T(8,128)(2,1)S(1)}, bf16[512,640]{1,0:T(8,128)(2,1)S(1)}, bf16[512,640]{1,0:T(8,128)(2,1)}) custom-call(s32[3]{0:T(128)S(1)} %pad_add_fusion.where, f32[1]{0:T(128)S(6)} %copy.18.weight_scale, bf16[1792,640]{1,0:T(8,128)(2,1)} %codes.1, bf16[512,1024]{1,0:T(8,128)(2,1)} %copy-done.9, ...), custom_call_target="tpu_custom_call" | custom-call | flops 4697620480 | bytes 12255232 | tf_op jit(solution)/shard_map/act_parts/pallas_call | solution.py:183
  130.9 1.5 collective-permute-done.31
  132.4 1.7 %convert_add_fusion.1 = f32[768,640]{1,0:T(8,128)S(1)} fusion(bf16[768,640]{1,0:T(8,128)(2,1)} %collective-permute-done.31, bf16[768,640]{1,0:T(8,128)(2,1)} %weight_term.3), kind=kLoop, calls=%fused_computation.2 | loop fusion | flops 1474560 | bytes 3932160 | tf_op jit(solution)/shard_map/add | solution.py:263
  134.3 0.7 collective-permute-start.26
  135.0 23.2 %collective-permute-done.30 = bf16[1024,640]{1,0:T(8,128)(2,1)} collective-permute-done((bf16[1024,640]{1,0:T(8,128)(2,1)}, bf16[1024,640]{1,0:T(8,128)(2,1)}, u32[]{:S(2)}, u32[]{:S(2)}) %collective-permute-start.30) | collective-permute-done | bytes 1310752 | tf_op jit(solution)/shard_map/ppermute | solution.py:262
  158.2 1.6 convert_add_fusion
  159.8 2.4 %pad_maximum_fusion = f32[1792,640]{1,0:T(8,128)} fusion(f32[768,640]{1,0:T(8,128)S(1)} %convert_add_fusion.1, f32[1024,640]{1,0:T(8,128)S(1)} %convert_add_fusion), kind=kLoop, calls=%fused_computation | loop fusion | flops 1146880 | bytes 9175040 | tf_op jit(solution)/shard_map/concatenate | solution.py:264
  162.2 1.7 %finish.1 = bf16[512,640]{1,0:T(8,128)(2,1)} custom-call(bf16[512,640]{1,0:T(8,128)(2,1)S(1)} %get-tuple-element.6.own, bf16[512,640]{1,0:T(8,128)(2,1)S(1)} %collective-permute-done.24.sibling, bf16[512,640]{1,0:T(8,128)(2,1)S(1)} %collective-permute-done.26.other, bf16[512,640]{1,0:T(8,128)(2,1)S(1)} %copy-done, f32[512,1]{1,0:T(8,128)S(1)} %copy.7.bound, ...), custom_call_target="tpu_custom_call" | custom-call | tf_op jit(solution)/shard_map/finish/pallas_call | solution.py:216
  (103 shorter events, 4.4 us)
Async XLA Ops:
  0.6 43.5 %copy-start.27 = (f32[512]{0:T(512)S(1)}, f32[512]{0:T(512)}, u32[]{:S(2)}) copy-start(f32[512]{0:T(512)} %param.9) | copy-start | bytes 6148
  0.6 43.5 %copy-start = (bf16[512,640]{1,0:T(8,128)(2,1)S(1)}, bf16[512,640]{1,0:T(8,128)(2,1)}, u32[]{:S(2)}) copy-start(bf16[512,640]{1,0:T(8,128)(2,1)} %rotated.1) | copy-start | bytes 1966084
  1.6 2.9 %collective-permute-start = (bf16[64,1024]{1,0:T(8,128)(2,1)S(1)}, bf16[64,1024]{1,0:T(8,128)(2,1)S(1)}, u32[]{:S(2)}, u32[]{:S(2)}) collective-permute-start(bf16[64,1024]{1,0:T(8,128)(2,1)S(1)} %slice.18), channel_id=1, source_target_pairs={{0,0},{1,1},{2,130},{3,131},{4,4},{5,5},{6,134},{7,135},{8,8},{9,9... | collective-permute-start | bytes 393224 | tf_op jit(solution)/shard_map/ppermute | solution.py:244
  3.2 3.3 %collective-permute-start.12 = (bf16[64,768]{1,0:T(8,128)(2,1)S(1)}, bf16[64,768]{1,0:T(8,128)(2,1)S(1)}, u32[]{:S(2)}, u32[]{:S(2)}) collective-permute-start(bf16[64,768]{1,0:T(8,128)(2,1)S(1)} %slice.21), channel_id=1, source_target_pairs={{0,0},{1,1},{2,130},{3,131},{4,4},{5,5},{6,134},{7,135},{8,8},{9,9... | collective-permute-start | bytes 294920 | tf_op jit(solution)/shard_map/ppermute | solution.py:244
  4.6 18.2 %collective-permute-start.1 = (bf16[64,1024]{1,0:T(8,128)(2,1)S(1)}, bf16[64,1024]{1,0:T(8,128)(2,1)S(1)}, u32[]{:S(2)}, u32[]{:S(2)}) collective-permute-start(bf16[64,1024]{1,0:T(8,128)(2,1)S(1)} %collective-permute-done), channel_id=1, source_target_pairs={{0,4},{4,8},{8,12},{12,16},{16,20},{20,24},{24,28},{28,0},{32,36},... | collective-permute-start | bytes 393224 | tf_op jit(solution)/shard_map/ppermute | solution.py:41
  6.5 16.3 %collective-permute-start.13 = (bf16[64,768]{1,0:T(8,128)(2,1)S(1)}, bf16[64,768]{1,0:T(8,128)(2,1)S(1)}, u32[]{:S(2)}, u32[]{:S(2)}) collective-permute-start(bf16[64,768]{1,0:T(8,128)(2,1)S(1)} %collective-permute-done.12), channel_id=1, source_target_pairs={{0,32},{4,36},{8,40},{12,44},{16,48},{20,52},{24,56},{28,60},{32,6... | collective-permute-start | bytes 294920 | tf_op jit(solution)/shard_map/ppermute | solution.py:66
  14.1 8.7 %collective-permute-start.14 = (bf16[64,768]{1,0:T(8,128)(2,1)S(1)}, bf16[64,768]{1,0:T(8,128)(2,1)S(1)}, u32[]{:S(2)}, u32[]{:S(2)}) collective-permute-start(bf16[64,768]{1,0:T(8,128)(2,1)S(1)} %collective-permute-done.12), channel_id=1, source_target_pairs={{0,96},{4,100},{8,104},{12,108},{16,112},{20,116},{24,120},{28,124... | collective-permute-start | bytes 294920 | tf_op jit(solution)/shard_map/ppermute | solution.py:67
  14.1 14.9 %collective-permute-start.15 = (bf16[64,768]{1,0:T(8,128)(2,1)S(1)}, bf16[64,768]{1,0:T(8,128)(2,1)S(1)}, u32[]{:S(2)}, u32[]{:S(2)}) collective-permute-start(bf16[64,768]{1,0:T(8,128)(2,1)S(1)} %collective-permute-done.12), channel_id=1, source_target_pairs={{0,64},{4,68},{8,72},{12,76},{16,80},{20,84},{24,88},{28,92},{32,9... | collective-permute-start | bytes 294920 | tf_op jit(solution)/shard_map/ppermute | solution.py:68
  16.9 12.3 %collective-permute-start.5 = (bf16[64,1024]{1,0:T(8,128)(2,1)S(1)}, bf16[64,1024]{1,0:T(8,128)(2,1)S(1)}, u32[]{:S(2)}, u32[]{:S(2)}) collective-permute-start(bf16[64,1024]{1,0:T(8,128)(2,1)S(1)} %collective-permute-done), channel_id=1, source_target_pairs={{0,28},{4,0},{8,4},{12,8},{16,12},{20,16},{24,20},{28,24},{32,60},... | collective-permute-start | bytes 393224 | tf_op jit(solution)/shard_map/ppermute | solution.py:43
  22.7 6.3 %collective-permute-start.2 = (bf16[64,1024]{1,0:T(8,128)(2,1)S(1)}, bf16[64,1024]{1,0:T(8,128)(2,1)S(1)}, u32[]{:S(2)}, u32[]{:S(2)}) collective-permute-start(bf16[64,1024]{1,0:T(8,128)(2,1)S(1)} %collective-permute-done.1), channel_id=1, source_target_pairs={{0,4},{4,8},{8,12},{12,16},{16,20},{20,24},{24,28},{28,0},{32,36},... | collective-permute-start | bytes 393224 | tf_op jit(solution)/shard_map/ppermute | solution.py:41
  29.0 7.6 %collective-permute-start.3 = (bf16[64,1024]{1,0:T(8,128)(2,1)S(1)}, bf16[64,1024]{1,0:T(8,128)(2,1)S(1)}, u32[]{:S(2)}, u32[]{:S(2)}) collective-permute-start(bf16[64,1024]{1,0:T(8,128)(2,1)S(1)} %collective-permute-done.2), channel_id=1, source_target_pairs={{0,4},{4,8},{8,12},{12,16},{16,20},{20,24},{24,28},{28,0},{32,36},... | collective-permute-start | bytes 393224 | tf_op jit(solution)/shard_map/ppermute | solution.py:41
  29.0 33.8 %copy-start.6 = (bf16[256,768]{1,0:T(8,128)(2,1)}, bf16[256,768]{1,0:T(8,128)(2,1)S(1)}, u32[]{:S(2)}) copy-start(bf16[256,768]{1,0:T(8,128)(2,1)S(1)} %constant_dynamic-update-slice_fusion.8.refs_5_.refs_0_) | copy-start | bytes 1179652
  29.0 20.9 %collective-permute-start.16 = (bf16[256,768]{1,0:T(8,128)(2,1)S(1)}, bf16[256,768]{1,0:T(8,128)(2,1)S(1)}, u32[]{:S(2)}, u32[]{:S(2)}) collective-permute-start(bf16[256,768]{1,0:T(8,128)(2,1)S(1)} %constant_dynamic-update-slice_fusion.8.refs_5_.refs_0_), channel_id=1, source_target_pairs={{0,4},{4,8},{8,12},{12,16},{16,20},{20,24},{24,28},{28,0},{32,36},... | collective-permute-start | bytes 1179656 | tf_op jit(solution)/shard_map/ppermute | solution.py:78
  29.1 7.5 %collective-permute-start.6 = (bf16[64,1024]{1,0:T(8,128)(2,1)S(1)}, bf16[64,1024]{1,0:T(8,128)(2,1)S(1)}, u32[]{:S(2)}, u32[]{:S(2)}) collective-permute-start(bf16[64,1024]{1,0:T(8,128)(2,1)S(1)} %collective-permute-done.5), channel_id=1, source_target_pairs={{0,28},{4,0},{8,4},{12,8},{16,12},{20,16},{24,20},{28,24},{32,60},... | collective-permute-start | bytes 393224 | tf_op jit(solution)/shard_map/ppermute | solution.py:43
  36.6 6.4 %collective-permute-start.4 = (bf16[64,1024]{1,0:T(8,128)(2,1)S(1)}, bf16[64,1024]{1,0:T(8,128)(2,1)S(1)}, u32[]{:S(2)}, u32[]{:S(2)}) collective-permute-start(bf16[64,1024]{1,0:T(8,128)(2,1)S(1)} %collective-permute-done.3), channel_id=1, source_target_pairs={{0,4},{4,8},{8,12},{12,16},{16,20},{20,24},{24,28},{28,0},{32,36},... | collective-permute-start | bytes 393224 | tf_op jit(solution)/shard_map/ppermute | solution.py:41
  36.7 6.4 %collective-permute-start.7 = (bf16[64,1024]{1,0:T(8,128)(2,1)S(1)}, bf16[64,1024]{1,0:T(8,128)(2,1)S(1)}, u32[]{:S(2)}, u32[]{:S(2)}) collective-permute-start(bf16[64,1024]{1,0:T(8,128)(2,1)S(1)} %collective-permute-done.6), channel_id=1, source_target_pairs={{0,28},{4,0},{8,4},{12,8},{16,12},{20,16},{24,20},{28,24},{32,60},... | collective-permute-start | bytes 393224 | tf_op jit(solution)/shard_map/ppermute | solution.py:43
  43.1 38.6 %copy-start.9 = (bf16[512,1024]{1,0:T(8,128)(2,1)}, bf16[512,1024]{1,0:T(8,128)(2,1)S(1)}, u32[]{:S(2)}) copy-start(bf16[512,1024]{1,0:T(8,128)(2,1)S(1)} %constant_dynamic-update-slice_fusion.refs_0_) | copy-start | bytes 3145732
  43.1 25.0 %collective-permute-start.8 = (bf16[512,1024]{1,0:T(8,128)(2,1)S(1)}, bf16[512,1024]{1,0:T(8,128)(2,1)S(1)}, u32[]{:S(2)}, u32[]{:S(2)}) collective-permute-start(bf16[512,1024]{1,0:T(8,128)(2,1)S(1)} %constant_dynamic-update-slice_fusion.refs_0_), channel_id=1, source_target_pairs={{0,32},{4,36},{8,40},{12,44},{16,48},{20,52},{24,56},{28,60},{32,6... | collective-permute-start | bytes 3145736 | tf_op jit(solution)/shard_map/ppermute | solution.py:47
  44.4 18.5 %collective-permute-start.28 = (bf16[512,640]{1,0:T(8,128)(2,1)S(1)}, bf16[512,640]{1,0:T(8,128)(2,1)}, u32[]{:S(2)}, u32[]{:S(2)}) collective-permute-start(bf16[512,640]{1,0:T(8,128)(2,1)S(1)} %minimum_convert_fusion.refs_5_.refs_9_), channel_id=1, source_target_pairs={{0,130},{1,131},{2,128},{3,129},{128,2},{129,3},{130,0},{131,1},{4... | collective-permute-start | bytes 1966088 | tf_op jit(solution)/shard_map/ppermute | solution.py:251
  46.5 12.7 %collective-permute-start.20 = (bf16[256,768]{1,0:T(8,128)(2,1)S(1)}, bf16[256,768]{1,0:T(8,128)(2,1)S(1)}, u32[]{:S(2)}, u32[]{:S(2)}) collective-permute-start(bf16[256,768]{1,0:T(8,128)(2,1)S(1)} %constant_dynamic-update-slice_fusion.8.refs_5_.refs_0_), channel_id=1, source_target_pairs={{0,28},{4,0},{8,4},{12,8},{16,12},{20,16},{24,20},{28,24},{32,60},... | collective-permute-start | bytes 1179656 | tf_op jit(solution)/shard_map/ppermute | solution.py:78
  50.0 23.6 %collective-permute-start.9 = (bf16[512,1024]{1,0:T(8,128)(2,1)S(1)}, bf16[512,1024]{1,0:T(8,128)(2,1)S(1)}, u32[]{:S(2)}, u32[]{:S(2)}) collective-permute-start(bf16[512,1024]{1,0:T(8,128)(2,1)S(1)} %constant_dynamic-update-slice_fusion.refs_0_), channel_id=1, source_target_pairs={{0,96},{4,100},{8,104},{12,108},{16,112},{20,116},{24,120},{28,124... | collective-permute-start | bytes 3145736 | tf_op jit(solution)/shard_map/ppermute | solution.py:48
  50.0 12.9 %collective-permute-start.17 = (bf16[256,768]{1,0:T(8,128)(2,1)S(1)}, bf16[256,768]{1,0:T(8,128)(2,1)S(1)}, u32[]{:S(2)}, u32[]{:S(2)}) collective-permute-start(bf16[256,768]{1,0:T(8,128)(2,1)S(1)} %collective-permute-done.16.refs_6_.refs_1_), channel_id=1, source_target_pairs={{0,4},{4,8},{8,12},{12,16},{16,20},{20,24},{24,28},{28,0},{32,36},... | collective-permute-start | bytes 1179656 | tf_op jit(solution)/shard_map/ppermute | solution.py:78
  59.2 22.5 %copy-start.17 = (bf16[256,768]{1,0:T(8,128)(2,1)}, bf16[256,768]{1,0:T(8,128)(2,1)S(1)}, u32[]{:S(2)}) copy-start(bf16[256,768]{1,0:T(8,128)(2,1)S(1)} %collective-permute-done.20.refs_10_.refs_5_) | copy-start | bytes 1179652
  59.2 9.0 %collective-permute-start.21 = (bf16[256,768]{1,0:T(8,128)(2,1)S(1)}, bf16[256,768]{1,0:T(8,128)(2,1)S(1)}, u32[]{:S(2)}, u32[]{:S(2)}) collective-permute-start(bf16[256,768]{1,0:T(8,128)(2,1)S(1)} %collective-permute-done.20.refs_10_.refs_5_), channel_id=1, source_target_pairs={{0,28},{4,0},{8,4},{12,8},{16,12},{20,16},{24,20},{28,24},{32,60},... | collective-permute-start | bytes 1179656 | tf_op jit(solution)/shard_map/ppermute | solution.py:78
  62.9 18.8 %collective-permute-start.27 = (bf16[512,640]{1,0:T(8,128)(2,1)S(1)}, bf16[512,640]{1,0:T(8,128)(2,1)S(1)}, u32[]{:S(2)}, u32[]{:S(2)}) collective-permute-start(bf16[512,640]{1,0:T(8,128)(2,1)S(1)} %minimum_convert_fusion.refs_5_.refs_9_), channel_id=1, source_target_pairs={{0,1},{1,0},{2,3},{3,2},{4,5},{5,4},{6,7},{7,6},{8,9},{9,8},{10,11... | collective-permute-start | bytes 1966088 | tf_op jit(solution)/shard_map/ppermute | solution.py:254
  62.9 23.3 %copy-start.20 = (bf16[256,768]{1,0:T(8,128)(2,1)}, bf16[256,768]{1,0:T(8,128)(2,1)S(1)}, u32[]{:S(2)}) copy-start(bf16[256,768]{1,0:T(8,128)(2,1)S(1)} %collective-permute-done.17.refs_7_.refs_2_) | copy-start | bytes 1179652
  62.9 12.8 %collective-permute-start.18 = (bf16[256,768]{1,0:T(8,128)(2,1)S(1)}, bf16[256,768]{1,0:T(8,128)(2,1)S(1)}, u32[]{:S(2)}, u32[]{:S(2)}) collective-permute-start(bf16[256,768]{1,0:T(8,128)(2,1)S(1)} %collective-permute-done.17.refs_7_.refs_2_), channel_id=1, source_target_pairs={{0,4},{4,8},{8,12},{12,16},{16,20},{20,24},{24,28},{28,0},{32,36},... | collective-permute-start | bytes 1179656 | tf_op jit(solution)/shard_map/ppermute | solution.py:78
  68.2 18.8 %collective-permute-start.29 = (bf16[512,640]{1,0:T(8,128)(2,1)}, bf16[512,640]{1,0:T(8,128)(2,1)}, u32[]{:S(2)}, u32[]{:S(2)}) collective-permute-start(bf16[512,640]{1,0:T(8,128)(2,1)} %collective-permute-done.28.refs_7_.refs_11_), channel_id=1, source_target_pairs={{0,1},{1,0},{2,3},{3,2},{4,5},{5,4},{6,7},{7,6},{8,9},{9,8},{10,11... | collective-permute-start | bytes 1966088 | tf_op jit(solution)/shard_map/ppermute | solution.py:256
  68.2 39.8 %copy-start.1 = (bf16[512,1024]{1,0:T(8,128)(2,1)}, bf16[512,1024]{1,0:T(8,128)(2,1)S(1)}, u32[]{:S(2)}) copy-start(bf16[512,1024]{1,0:T(8,128)(2,1)S(1)} %collective-permute-done.8.refs_1_) | copy-start | bytes 3145732
  68.2 12.8 %collective-permute-start.22 = (bf16[256,768]{1,0:T(8,128)(2,1)S(1)}, bf16[256,768]{1,0:T(8,128)(2,1)S(1)}, u32[]{:S(2)}, u32[]{:S(2)}) collective-permute-start(bf16[256,768]{1,0:T(8,128)(2,1)S(1)} %collective-permute-done.21.refs_11_.refs_6_), channel_id=1, source_target_pairs={{0,28},{4,0},{8,4},{12,8},{16,12},{20,16},{24,20},{28,24},{32,60},... | collective-permute-start | bytes 1179656 | tf_op jit(solution)/shard_map/ppermute | solution.py:78
  73.5 12.7 %copy-start.26 = (bf16[512,1024]{1,0:T(8,128)(2,1)}, bf16[512,1024]{1,0:T(8,128)(2,1)S(1)}, u32[]{:S(2)}) copy-start(bf16[512,1024]{1,0:T(8,128)(2,1)S(1)} %collective-permute-done.9.refs_2_) | copy-start | bytes 3145732
  73.5 34.5 %collective-permute-start.10 = (bf16[256,1024]{1,0:T(8,128)(2,1)}, bf16[256,1024]{1,0:T(8,128)(2,1)}, u32[]{:S(2)}, u32[]{:S(2)}) collective-permute-start(bf16[256,1024]{1,0:T(8,128)(2,1)} %slice.24), channel_id=1, source_target_pairs={{0,32},{4,36},{8,40},{12,44},{16,48},{20,52},{24,56},{28,60},{32,6... | collective-permute-start | bytes 1572872 | tf_op jit(solution)/shard_map/ppermute | solution.py:49
  75.7 31.4 %copy-start.2 = (bf16[256,768]{1,0:T(8,128)(2,1)}, bf16[256,768]{1,0:T(8,128)(2,1)S(1)}, u32[]{:S(2)}) copy-start(bf16[256,768]{1,0:T(8,128)(2,1)S(1)} %collective-permute-done.18.refs_8_.refs_3_) | copy-start | bytes 1179652
  75.7 32.3 %collective-permute-start.11 = (bf16[256,1024]{1,0:T(8,128)(2,1)}, bf16[256,1024]{1,0:T(8,128)(2,1)}, u32[]{:S(2)}, u32[]{:S(2)}) collective-permute-start(bf16[256,1024]{1,0:T(8,128)(2,1)} %slice.25), channel_id=1, source_target_pairs={{0,96},{4,100},{8,104},{12,108},{16,112},{20,116},{24,120},{28,124... | collective-permute-start | bytes 1572872 | tf_op jit(solution)/shard_map/ppermute | solution.py:50
  80.9 26.1 %copy-start.4 = (bf16[256,768]{1,0:T(8,128)(2,1)}, bf16[256,768]{1,0:T(8,128)(2,1)S(1)}, u32[]{:S(2)}) copy-start(bf16[256,768]{1,0:T(8,128)(2,1)S(1)} %collective-permute-done.22.refs_12_.refs_7_) | copy-start | bytes 1179652
  80.9 8.4 %collective-permute-start.19 = (bf16[128,768]{1,0:T(8,128)(2,1)S(1)}, bf16[128,768]{1,0:T(8,128)(2,1)S(1)}, u32[]{:S(2)}, u32[]{:S(2)}) collective-permute-start(bf16[128,768]{1,0:T(8,128)(2,1)S(1)} %slice.26), channel_id=1, source_target_pairs={{0,4},{4,8},{8,12},{12,16},{16,20},{20,24},{24,28},{28,0},{32,36},... | collective-permute-start | bytes 589832 | tf_op jit(solution)/shard_map/ppermute | solution.py:82
  82.5 8.0 %collective-permute-start.23 = (bf16[128,768]{1,0:T(8,128)(2,1)}, bf16[128,768]{1,0:T(8,128)(2,1)}, u32[]{:S(2)}, u32[]{:S(2)}) collective-permute-start(bf16[128,768]{1,0:T(8,128)(2,1)} %slice.27), channel_id=1, source_target_pairs={{0,28},{4,0},{8,4},{12,8},{16,12},{20,16},{24,20},{28,24},{32,60},... | collective-permute-start | bytes 589832 | tf_op jit(solution)/shard_map/ppermute | solution.py:85
  107.1 12.8 %copy-start.8 = (bf16[256,768]{1,0:T(8,128)(2,1)S(1)}, bf16[256,768]{1,0:T(8,128)(2,1)}, u32[]{:S(2)}) copy-start(bf16[256,768]{1,0:T(8,128)(2,1)} %copy-done.6) | copy-start | bytes 1179652
  107.1 12.8 %copy-start.16 = (bf16[256,768]{1,0:T(8,128)(2,1)S(1)}, bf16[256,768]{1,0:T(8,128)(2,1)}, u32[]{:S(2)}) copy-start(bf16[256,768]{1,0:T(8,128)(2,1)} %copy-done.14) | copy-start | bytes 1179652
  107.1 12.8 %copy-start.19 = (bf16[256,768]{1,0:T(8,128)(2,1)S(1)}, bf16[256,768]{1,0:T(8,128)(2,1)}, u32[]{:S(2)}) copy-start(bf16[256,768]{1,0:T(8,128)(2,1)} %copy-done.17) | copy-start | bytes 1179652
  107.1 12.8 %copy-start.22 = (bf16[256,768]{1,0:T(8,128)(2,1)S(1)}, bf16[256,768]{1,0:T(8,128)(2,1)}, u32[]{:S(2)}) copy-start(bf16[256,768]{1,0:T(8,128)(2,1)} %copy-done.20) | copy-start | bytes 1179652
  107.1 25.3 %collective-permute-start.31 = (bf16[768,640]{1,0:T(8,128)(2,1)}, bf16[768,640]{1,0:T(8,128)(2,1)}, u32[]{:S(2)}, u32[]{:S(2)}) collective-permute-start(bf16[768,640]{1,0:T(8,128)(2,1)} %weight_term.3), channel_id=1, source_target_pairs={{0,128},{128,0},{1,129},{129,1},{2,130},{130,2},{3,131},{131,3},{4... | collective-permute-start | bytes 2949128 | tf_op jit(solution)/shard_map/ppermute | solution.py:262
  108.0 11.9 %copy-start.5 = (bf16[256,768]{1,0:T(8,128)(2,1)S(1)}, bf16[256,768]{1,0:T(8,128)(2,1)}, u32[]{:S(2)}) copy-start(bf16[256,768]{1,0:T(8,128)(2,1)} %copy-done.4) | copy-start | bytes 1179652
  118.3 39.9 %collective-permute-start.30 = (bf16[1024,640]{1,0:T(8,128)(2,1)}, bf16[1024,640]{1,0:T(8,128)(2,1)}, u32[]{:S(2)}, u32[]{:S(2)}) collective-permute-start(bf16[1024,640]{1,0:T(8,128)(2,1)} %weight_term.2), channel_id=1, source_target_pairs={{0,128},{128,0},{1,129},{129,1},{2,130},{130,2},{3,131},{131,3},{4... | collective-permute-start | bytes 3932168 | tf_op jit(solution)/shard_map/ppermute | solution.py:262
  130.0 4.1 %collective-permute-start.25 = (bf16[512,640]{1,0:T(8,128)(2,1)}, bf16[512,640]{1,0:T(8,128)(2,1)S(1)}, u32[]{:S(2)}, u32[]{:S(2)}) collective-permute-start(bf16[512,640]{1,0:T(8,128)(2,1)} %get-tuple-element.9), channel_id=1, source_target_pairs={{0,1},{1,0},{2,3},{3,2},{4,5},{5,4},{6,7},{7,6},{8,9},{9,8},{10,11... | collective-permute-start | bytes 1966088 | tf_op jit(solution)/shard_map/ppermute | solution.py:267
  130.4 31.9 %collective-permute-start.24 = (bf16[512,640]{1,0:T(8,128)(2,1)S(1)}, bf16[512,640]{1,0:T(8,128)(2,1)S(1)}, u32[]{:S(2)}, u32[]{:S(2)}) collective-permute-start(bf16[512,640]{1,0:T(8,128)(2,1)S(1)} %get-tuple-element.7), channel_id=1, source_target_pairs={{0,1},{1,0},{2,3},{3,2},{4,5},{5,4},{6,7},{7,6},{8,9},{9,8},{10,11... | collective-permute-start | bytes 1966088 | tf_op jit(solution)/shard_map/ppermute | solution.py:270
  134.1 24.1 %copy-start.25 = (bf16[1024,640]{1,0:T(8,128)(2,1)S(1)}, bf16[1024,640]{1,0:T(8,128)(2,1)}, u32[]{:S(2)}) copy-start(bf16[1024,640]{1,0:T(8,128)(2,1)} %weight_term.2) | copy-start | bytes 3932164
  134.3 27.9 %collective-permute-start.26 = (bf16[512,640]{1,0:T(8,128)(2,1)S(1)}, bf16[512,640]{1,0:T(8,128)(2,1)S(1)}, u32[]{:S(2)}, u32[]{:S(2)}) collective-permute-start(bf16[512,640]{1,0:T(8,128)(2,1)S(1)} %add_convert_fusion), channel_id=1, source_target_pairs={{0,130},{1,131},{2,128},{3,129},{128,2},{129,3},{130,0},{131,1},{4... | collective-permute-start | bytes 1966088 | tf_op jit(solution)/shard_map/ppermute | solution.py:269
  (12 other events, 43.2 us)

commit v2 on v0

v2 whole, which is shorter than its diff:
```python
import functools

import jax
import jax.numpy as jnp
from jax import lax
from jax.experimental import pallas as pl
from jax.experimental.pallas import tpu as pltpu
from jax.sharding import PartitionSpec as P

HB = 128
NY, NZ = 4, 8
SHARD = 64
BF = jnp.bfloat16
F32 = jnp.float32

WIDTHS = (1024, 768)
VMEM = 60 * 2**20
SMALL = 16 * 2**20
HALF = 512
LITTLE = pl.CostEstimate(flops=1, bytes_accessed=1, transcendentals=0)

NEAR = (-2, -1, 0, 1)
FAR = (-4, -3, 2, 3)
Y_ORDER = (0, -1, 1, -2)
PIECES = 10


def z_pairs(k):
    return [(y * NZ + z, y * NZ + (z + k) % NZ) for y in range(NY) for z in range(NZ)]


def y_pairs(k):
    return [(y * NZ + z, (y + k) % NY * NZ + z) for y in range(NY) for z in range(NZ)]


CORE = [(r, r ^ 1) for r in range(4)]
DP = [(0, 1), (1, 0)]
PARTNER = [(d * 4 + r, (1 - d) * 4 + (r ^ 2)) for d in range(2) for r in range(4)]


def pairs_for(steps, swap=False):
    pairs = []
    for d in range(2):
        for y in range(NY):
            for z in range(NZ):
                for r in range(4):
                    step = steps[r % 2]
                    if step is None:
                        continue
                    there = d ^ (y // 2 != r // 2) if swap else d
                    target = (y + step[0]) % NY * NZ + (z + step[1]) % NZ
                    pairs.append((((d * 32) + y * NZ + z) * 4 + r, (there * 32 + target) * 4 + r))
    return pairs


def move(value, core0, core1, swap=False):
    return lax.ppermute(value, ("dp", "col", "row"), pairs_for((core0, core1), swap))


def join_kernel(*refs):
    for at, shard in enumerate(refs[:4]):
        lo = 0
        for out in refs[4:]:
            width = out.shape[1]
            out[at * SHARD:(at + 1) * SHARD, :] = shard[:, lo:lo + width]
            lo += width


def join(*shards):
    vmem = pl.BlockSpec(memory_space=pltpu.VMEM)
    return list(pl.pallas_call(
        join_kernel,
        out_shape=[jax.ShapeDtypeStruct((4 * SHARD, width), BF) for width in WIDTHS],
        in_specs=[vmem] * 4,
        out_specs=[vmem] * len(WIDTHS),
        compiler_params=pltpu.CompilerParams(vmem_limit_bytes=SMALL),
        cost_estimate=LITTLE,
        name="join",
    )(*shards))


def gather(own, first_core, before_second, before_third):
    a = move(own, (0, 1), (1, 0))
    b = move(own, (0, -1), (-1, 0))
    c = move(own, (0, 2), (2, 0))
    near = join(c, a, own, b)
    up1 = [move(part, (1, 0), (0, 1)) for part in near]
    down1 = [move(part, (-1, 0), (0, -1)) for part in near]
    far_up = move(c, (0, 1), None)
    far_down = move(b, (0, -1), None)
    up1[0], down1[0], far_up, far_down = before_second(up1[0], down1[0], far_up, far_down)
    up2 = [move(part, (1, 0), (0, 1)) for part in up1]
    down2 = [move(part, None, (0, -1)) for part in down1]
    far = join(move(far_up, (0, 1), None), far_up, far_down, move(far_down, (0, -1), None))
    up2[0], down2[0], up1[1], down1[1] = before_third(up2[0], down2[0], up1[1], down1[1])
    up3 = [move(jnp.where(first_core, f, part), (1, 0), (0, 1)) for f, part in zip(far, up2)]
    down3 = [move(jnp.where(first_core, f, part), (-1, 0), (0, -1)) for f, part in zip(far, down2)]
    up3[0], down3[0], up2[1], down2[1] = lax.optimization_barrier((up3[0], down3[0], up2[1], down2[1]))
    up4 = [move(part[:2 * SHARD], (1, 0), (0, 1)) for part in up3]
    down4 = [move(part[2 * SHARD:], (-1, 0), (0, -1)) for part in down3]
    return [list(group) for group in zip(near, far, up1, down1, up2, down2, up3, down3, up4, down4)]


def places_of(core):
    if core == 0:
        lines = ((0, NEAR), (0, FAR), (-1, NEAR), (1, NEAR), (-2, NEAR), (0, ()), (-1, FAR), (1, FAR),
                 (-2, FAR[:2]), (-2, FAR[2:]))
        return [[(dy, dz) for dz in line] for dy, line in lines]
    lines = ((0, NEAR), (0, ()), (-1, NEAR), (1, NEAR), (-2, NEAR), (2, NEAR), (-3, NEAR), (3, NEAR),
             (-4, NEAR[:2]), (4, NEAR[2:]))
    return [[(dy, dz) for dy in line] for dz, line in lines]


def each_shard(where, refs, do, turns=Y_ORDER):
    for core in range(2):
        @pl.when(where[2] % 2 == core)
        def _():
            for turn in turns:
                for ref, spots in zip(refs, places_of(core)):
                    for at, (dy, dz) in enumerate(spots):
                        if dy == turn:
                            do(ref.at[pl.ds(at * SHARD, SHARD)],
                               lax.rem(where[0] + dy + NY, NY), lax.rem(where[1] + dz + NZ, NZ))


def clip_kernel(rotated, bound, out):
    top = bound[...]
    for lo in range(0, rotated.shape[1], 128):
        block = jnp.clip(rotated[:, lo:lo + 128].astype(F32), -top, top)
        out[lo:lo + 128, :] = block.T.astype(BF)


def clip_turned(rotated, bound):
    vmem = pl.BlockSpec(memory_space=pltpu.VMEM)
    return pl.pallas_call(
        clip_kernel,
        out_shape=jax.ShapeDtypeStruct(rotated.shape[::-1], BF),
        in_specs=[vmem] * 2,
        out_specs=vmem,
        compiler_params=pltpu.CompilerParams(vmem_limit_bytes=SMALL),
        name="clip_turned",
    )(rotated, bound)


def weight_kernel(scale, where, *refs):
    n = PIECES
    piece_refs, (own, both, other) = refs[:n], refs[n:n + 3]
    out, held, clip_held, sem, clip_sem = refs[n + 3:]
    cols, size = own.shape
    for j, ref in enumerate((own, both.at[pl.ds(0, cols)], other, both.at[pl.ds(cols, cols)])):
        start = pl.multiple_of((where[2] ^ j) * size, size)
        pltpu.make_async_copy(ref, clip_held.at[:, pl.ds(start, size)], clip_sem).start()
    width = out.shape[1]
    windows = ((0, HALF), (HALF, width))
    for i, (lo, hi) in enumerate(windows):
        window = pl.ds(lo, hi - lo)

        def load(ref, y, z):
            spot = pl.ds(pl.multiple_of((y * NZ + z) * SHARD, SHARD), SHARD)
            pltpu.make_async_copy(ref.at[:, window], held.at[spot, window], sem.at[i]).start()

        each_shard(where, piece_refs, load)
    pltpu.make_async_copy(clip_held, clip_held, clip_sem).wait()
    for i, (lo, hi) in enumerate(windows):
        part = held.at[:, pl.ds(lo, hi - lo)]
        pltpu.make_async_copy(part, part, sem.at[i]).wait()
        for first in range(lo, hi, 256):
            step = min(256, hi - first)
            out[:, first:first + step] = (
                jnp.dot(clip_held[...], held[:, first:first + step], preferred_element_type=F32) * scale
            ).astype(BF)


def weight_term(where, pieces, clips, scale):
    width = pieces[0].shape[1]
    cols, part = clips[0].shape
    tokens = 4 * part
    anywhere = pl.BlockSpec(memory_space=pltpu.HBM)
    return pl.pallas_call(
        functools.partial(weight_kernel, scale),
        out_shape=jax.ShapeDtypeStruct((cols, width), BF),
        in_specs=[pl.BlockSpec(memory_space=pltpu.SMEM)] + [anywhere] * (len(pieces) + 3),
        out_specs=pl.BlockSpec(memory_space=pltpu.VMEM),
        scratch_shapes=[
            pltpu.VMEM((tokens, width), BF),
            pltpu.VMEM((cols, tokens), BF),
            pltpu.SemaphoreType.DMA((2,)),
            pltpu.SemaphoreType.DMA,
        ],
        compiler_params=pltpu.CompilerParams(vmem_limit_bytes=VMEM),
        cost_estimate=LITTLE,
        name="weight_term",
    )(where, *pieces, *clips)


def sum_kernel(lo, mine, theirs, *refs):
    out, held, sem = refs[-3:]
    width = mine.shape[1]
    copies = []
    for at in range(0, width, 128):
        both = mine[:, at:at + 128].astype(F32) + theirs[:, at:at + 128].astype(F32)
        held[at:at + 128, :] = both.T
        copies.append(pltpu.make_async_copy(
            held.at[pl.ds(at, 128)], out.at[pl.ds(lo + at, 128)], sem.at[at // 128]))
        copies[-1].start()
    for copy in copies:
        copy.wait()


def sum_terms(lo, mine, theirs, whole, depth):
    cols, width = mine.shape
    vmem = pl.BlockSpec(memory_space=pltpu.VMEM)
    anywhere = pl.BlockSpec(memory_space=pltpu.HBM)
    before = [] if whole is None else [whole]
    return pl.pallas_call(
        functools.partial(sum_kernel, lo),
        out_shape=jax.ShapeDtypeStruct((depth, cols), F32),
        in_specs=[vmem] * 2 + [anywhere] * len(before),
        out_specs=anywhere,
        scratch_shapes=[pltpu.VMEM((width, cols), F32), pltpu.SemaphoreType.DMA((width // 128,))],
        input_output_aliases={2: 0} if before else {},
        compiler_params=pltpu.CompilerParams(vmem_limit_bytes=SMALL),
        name="sum_terms",
    )(mine, theirs, *before)


def act_kernel(where, weight_scale, codes, *refs):
    n = PIECES * len(WIDTHS)
    piece_refs, (out, held, code_held, sem, code_sem) = refs[:n], refs[n:]
    code_copy = pltpu.make_async_copy(codes, code_held, code_sem)
    code_copy.start()
    rows = held.shape[1]
    for turn in Y_ORDER:
        lo = 0
        for i, width in enumerate(WIDTHS):
            window = pl.ds(lo, width)
            lo += width

            def load(ref, y, z):
                spot = pl.ds(pl.multiple_of(z * SHARD, SHARD), SHARD)
                pltpu.make_async_copy(ref, held.at[y, spot, window], sem.at[y]).start()

            each_shard(where, piece_refs[i * PIECES:(i + 1) * PIECES], load, (turn,))
    code_copy.wait()
    for turn in Y_ORDER:
        y = lax.rem(where[0] + turn + NY, NY)
        pltpu.make_async_copy(held.at[y], held.at[y], sem.at[y]).wait()
        total = jnp.dot(held[y], code_held[...], preferred_element_type=F32) * weight_scale[0]
        j = y ^ where[2]
        place = 2 * (1 - j % 2) + 1 - j // 2
        out[pl.ds(pl.multiple_of(place * rows, rows), rows), :] = total.astype(BF)


def act_parts(where, weight_scale, codes, groups):
    depth, cols = codes.shape
    rows = 8 * SHARD
    pieces = [piece for group in groups for piece in group]
    anywhere = pl.BlockSpec(memory_space=pltpu.HBM)
    smem = pl.BlockSpec(memory_space=pltpu.SMEM)
    return pl.pallas_call(
        act_kernel,
        out_shape=jax.ShapeDtypeStruct((4 * rows, cols), BF),
        in_specs=[smem, smem] + [anywhere] * (len(pieces) + 1),
        out_specs=pl.BlockSpec(memory_space=pltpu.VMEM),
        scratch_shapes=[
            pltpu.VMEM((4, rows, depth), BF),
            pltpu.VMEM((depth, cols), BF),
            pltpu.SemaphoreType.DMA((4,)),
            pltpu.SemaphoreType.DMA,
        ],
        compiler_params=pltpu.CompilerParams(vmem_limit_bytes=VMEM),
        cost_estimate=LITTLE,
        name="act_parts",
    )(where, weight_scale, codes, *pieces)


def finish_kernel(parts, got, other, rotated, bound, signs, out):
    rows = out.shape[0]
    summed = parts[3 * rows:, :].astype(F32) + got[rows:, :].astype(F32) + other[...].astype(F32)
    masked = jnp.where(jnp.abs(rotated[...].astype(F32)) <= bound[...], summed, 0.0)
    high = masked.astype(BF)
    low = (masked - high.astype(F32)).astype(BF)
    table = signs[...]
    for lo in range(0, out.shape[1], HB):
        turned = jnp.dot(high[:, lo:lo + HB], table, preferred_element_type=F32)
        turned += jnp.dot(low[:, lo:lo + HB], table, preferred_element_type=F32)
        out[:, lo:lo + HB] = (turned * (HB ** -0.5)).astype(BF)


def finish(parts, got, other, rotated, bound, signs):
    vmem = pl.BlockSpec(memory_space=pltpu.VMEM)
    return pl.pallas_call(
        finish_kernel,
        out_shape=jax.ShapeDtypeStruct(other.shape, BF),
        in_specs=[vmem] * 6,
        out_specs=vmem,
        compiler_params=pltpu.CompilerParams(vmem_limit_bytes=SMALL),
        name="finish",
    )(parts, got, other, rotated, bound, signs)


def hadamard_signs(length):
    indices = jnp.arange(length, dtype=jnp.int32)
    common = indices[:, None] & indices[None, :]
    parity = jnp.zeros((length, length), jnp.int32)
    for bit in range(length.bit_length() - 1):
        parity = parity ^ (common >> bit)
    return (1 - 2 * (parity & 1)).astype(BF)


def body(cotangent, codes, weight_scale, rotated, clip_level):
    col = lax.axis_index("col")
    row = lax.axis_index("row")
    where = jnp.stack([col // NZ, col % NZ, row]).astype(jnp.int32)
    token_total = cotangent.shape[0] * lax.axis_size("col") * lax.axis_size("dp")
    grad_norm = token_total ** (-0.5)

    bound = clip_level[:, None]
    clipped = clip_turned(rotated, bound)
    other = lax.ppermute(clipped, ("dp", "row"), PARTNER)

    tie = lax.optimization_barrier
    first_core = row % 2 == 0
    both = None

    def before_second(*arrays):
        nonlocal other, both
        *arrays, other = tie((*arrays, other))
        both = lax.ppermute(jnp.concatenate([clipped, other], axis=0), "row", CORE)
        return arrays

    def before_third(*arrays):
        nonlocal both
        *arrays, both = tie((*arrays, both))
        return arrays

    own = move(cotangent, (0, 0), (0, 0), True)
    groups = gather(own, first_core, before_second, before_third)
    clips = [clipped, both, other]
    mine0 = weight_term(where, groups[0], clips, grad_norm)
    theirs0 = lax.ppermute(mine0, "dp", DP)
    mine0, groups[0][0] = tie((mine0, groups[0][0]))
    rows = clipped.shape[1]
    parts = act_parts(where, weight_scale, codes, groups)
    parts, groups[1][0] = tie((parts, groups[1][0]))
    mine1 = weight_term(where, groups[1], clips, grad_norm)
    got = lax.ppermute(parts[:2 * rows], "row", CORE)
    mine1, theirs0 = tie((mine1, theirs0))
    theirs1 = lax.ppermute(mine1, "dp", DP)
    outward = (parts[2 * rows:3 * rows].astype(F32) + got[:rows].astype(F32)).astype(BF)
    inward = lax.ppermute(outward, ("dp", "row"), PARTNER)
    weight_grad = sum_terms(0, mine0, theirs0, None, codes.shape[0])
    input_grad = finish(parts, got, inward, rotated, bound, hadamard_signs(HB))
    input_grad, theirs1 = tie((input_grad, theirs1))
    weight_grad = sum_terms(WIDTHS[0], mine1, theirs1, weight_grad, codes.shape[0])
    return (input_grad, weight_grad)


def solution(mesh):
    placed = (
        P(("dp", "col"), "row"),
        P("row", "col"),
        P(),
        P(("dp", "row"), "col"),
        P(("dp", "row")),
    )
    return jax.shard_map(
        body,
        mesh=mesh,
        in_specs=placed,
        out_specs=(P(("dp", "row"), "col"), P("row", "col")),
        check_vma=False,
    )
```

time: 295 us -> 149 us (0.51)
  waiting for transfers between devices: 244 us -> 28.8 us
  starting transfers between devices: 0.16 us -> 72.1 us
  Pallas kernels: 0 us -> 34.1 us
  matrix products: 22.1 us -> 0 us
  between operations: 14.5 us -> 1.82 us
    all_gather x2 -> x0, waiting for transfers between devices: 130 us -> none  [the longest x1 94.6 us: body(): gathered = lax.all_gather(cotangent, 'col', axis=0, tiled=True)]
    ppermute x0 -> x30, starting transfers between devices: none -> 72.1 us  [the longest x24 45 us: move(): lax.ppermute(value, ('dp', 'col', 'row'), pairs_for((core0, core1), swap))]
    psum x1 -> x0, waiting for transfers between devices: 66.6 us -> none  [body(): lax.psum(weight_part.astype(jnp.bfloat16), 'dp').astype(jnp.float32)]
    reduce_scatter x1 -> x0, waiting for transfers between devices: 46 us -> none  [body(): lax.psum_scatter(partial_value.astype(jnp.bfloat16), 'row', scatter_dimen...]
    pallas_call x0 -> x9, Pallas kernels: none -> 34.1 us  [the longest x2 14.7 us: weight_term(): pl.pallas_call(functools.partial(weight_kernel, scale), out_shape=jax.Sha...]
    ppermute x0 -> x30, waiting for transfers between devices: none -> 28.8 us  [the longest x1 11.5 us: body(): inward = lax.ppermute(outward, ('dp', 'row'), PARTNER)]
    dot_general x3 -> x0, matrix products: 22.1 us -> none  [the longest x1 10.3 us: body(): jnp.dot(gathered.T, clip_all, preferred_element_type=jnp.float32)]
    slice x0 -> x5, local copies, waits for them, and re-layouts: none -> 4.1 us  [the longest x1 2.51 us: body(): got = lax.ppermute(parts[:2 * rows], 'row', CORE)]
  transfers between devices with their start and end apart: 4 -> 30, of which waited for: 4 -> 12; matrix products, arithmetic and copies ran while one was open for 5% -> 5% of each run, Pallas kernels for 0% -> 22%
where the time goes in v2:
time: 149 us
  starting transfers between devices  72.1 us (48%)
  Pallas kernels  34.1 us (23%)
  waiting for transfers between devices  28.8 us (19%)
  local copies, waits for them, and re-layouts  8.84 us (6%)
  other arithmetic  3.15 us (2%)
  between operations  1.82 us (1%)
    ppermute x24, starting transfers between devices, move(): lax.ppermute(value, ('dp', 'col', 'row'), pairs_for((core0, core1), swap))  45 us
    pallas_call x2, Pallas kernels, weight_term(): pl.pallas_call(functools.partial(weight_kernel, scale), out_shape=jax.Sha...  14.7 us
    pallas_call x1, Pallas kernels, act_parts(): pl.pallas_call(act_kernel, out_shape=jax.ShapeDtypeStruct((4 * rows, cols...  12.5 us
    ppermute x1, waiting for transfers between devices, body(): inward = lax.ppermute(outward, ('dp', 'row'), PARTNER)  11.5 us
    ppermute x1, starting transfers between devices, before_second(): both = lax.ppermute(jnp.concatenate([clipped, other], axis=0), 'row', CORE)  10.3 us
    ppermute x1, starting transfers between devices, body(): got = lax.ppermute(parts[:2 * rows], 'row', CORE)  10.1 us
    ppermute x24, waiting for transfers between devices, move(): lax.ppermute(value, ('dp', 'col', 'row'), pairs_for((core0, core1), swap))  8.48 us
    ppermute x1, waiting for transfers between devices, body(): other = lax.ppermute(clipped, ('dp', 'row'), PARTNER)  5.4 us
  transfers between devices with their start and end apart: 30, of which 12 were waited for; matrix products, arithmetic and copies ran while one was open for 5% of the time, Pallas kernels for 22%

profile of v2, /device:TPU:1, one launch (start us, length us, event | category | flops | bytes accessed | tf_op | source)
XLA Modules:
  0.0 148.8 jit_solution(2495485138747890589)
XLA Ops:
  0.6 1.6 %collective-permute-start = (bf16[64,1792]{1,0:T(8,128)(2,1)}, bf16[64,1792]{1,0:T(8,128)(2,1)S(1)}, u32[]{:S(2)}, u32[]{:S(2)}) collective-permute-start(bf16[64,1792]{1,0:T(8,128)(2,1)} %param.5), channel_id=1, source_target_pairs={{0,0},{1,1},{2,130},{3,131},{4,4},{5,5},{6,134},{7,135},{8,8},{9,9... | collective-permute-start | bytes 688136 | tf_op jit(solution)/shard_map/ppermute | solution.py:57
  2.2 10.7 %collective-permute-start.1 = (bf16[64,1792]{1,0:T(8,128)(2,1)S(1)}, bf16[64,1792]{1,0:T(8,128)(2,1)S(1)}, u32[]{:S(2)}, u32[]{:S(2)}) collective-permute-start(bf16[64,1792]{1,0:T(8,128)(2,1)S(1)} %collective-permute-done.refs_2_), channel_id=1, source_target_pairs={{0,8},{1,65},{2,10},{3,67},{4,12},{5,69},{6,14},{7,71},{8,16},{9,7... | collective-permute-start | bytes 688136 | tf_op jit(solution)/shard_map/ppermute | solution.py:57
  13.0 1.5 collective-permute-start.2
  14.4 0.8 copy.8.bound
  15.3 1.1 copy-done.6
  16.8 1.9 %collective-permute-start.8 = (bf16[640,512]{1,0:T(8,128)(2,1)S(1)}, bf16[640,512]{1,0:T(8,128)(2,1)S(1)}, u32[]{:S(2)}, u32[]{:S(2)}) collective-permute-start(bf16[640,512]{1,0:T(8,128)(2,1)S(1)} %clip_turned.1.refs_10_), channel_id=1, source_target_pairs={{0,130},{1,131},{2,128},{3,129},{128,2},{129,3},{130,0},{131,1},{4... | collective-permute-start | bytes 1966088 | tf_op jit(solution)/shard_map/ppermute | solution.py:320
  19.3 1.7 %collective-permute-start.4 = (bf16[256,1024]{1,0:T(8,128)(2,1)S(1)}, bf16[256,1024]{1,0:T(8,128)(2,1)}, u32[]{:S(2)}, u32[]{:S(2)}) collective-permute-start(bf16[256,1024]{1,0:T(8,128)(2,1)S(1)} %get-tuple-element.41.refs_0_), channel_id=1, source_target_pairs={{0,32},{1,5},{2,34},{3,7},{4,36},{5,9},{6,38},{7,11},{8,40},{9,13}... | collective-permute-start | bytes 1572872 | tf_op jit(solution)/shard_map/ppermute | solution.py:57
  21.1 4.0 %collective-permute-start.5 = (bf16[256,1024]{1,0:T(8,128)(2,1)S(1)}, bf16[256,1024]{1,0:T(8,128)(2,1)}, u32[]{:S(2)}, u32[]{:S(2)}) collective-permute-start(bf16[256,1024]{1,0:T(8,128)(2,1)S(1)} %get-tuple-element.41.refs_0_), channel_id=1, source_target_pairs={{0,96},{1,29},{2,98},{3,31},{4,100},{5,1},{6,102},{7,3},{8,104},{9... | collective-permute-start | bytes 1572872 | tf_op jit(solution)/shard_map/ppermute | solution.py:57
  25.1 0.7 collective-permute-start.6
  25.8 0.7 collective-permute-start.7
  26.4 5.4 %collective-permute-done.8.refs_12_ = bf16[640,512]{1,0:T(8,128)(2,1)S(1)} collective-permute-done((bf16[640,512]{1,0:T(8,128)(2,1)S(1)}, bf16[640,512]{1,0:T(8,128)(2,1)S(1)}, u32[]{:S(2)}, u32[]{:S(2)}) %collective-permute-start.8) | collective-permute-done | bytes 655392 | tf_op jit(solution)/shard_map/ppermute | solution.py:320
  32.0 1.1 pad_maximum_fusion
  33.1 10.3 %collective-permute-start.15 = (bf16[1280,512]{1,0:T(8,128)(2,1)}, bf16[1280,512]{1,0:T(8,128)(2,1)}, u32[]{:S(2)}, u32[]{:S(2)}) collective-permute-start(bf16[1280,512]{1,0:T(8,128)(2,1)} %pad_maximum_fusion), channel_id=1, source_target_pairs={{0,1},{1,0},{2,3},{3,2},{4,5},{5,4},{6,7},{7,6},{8,9},{9,8},{10,11... | collective-permute-start | bytes 3932168 | tf_op jit(solution)/shard_map/ppermute | solution.py:329
  43.4 2.2 %collective-permute-start.13 = (bf16[256,768]{1,0:T(8,128)(2,1)S(1)}, bf16[256,768]{1,0:T(8,128)(2,1)}, u32[]{:S(2)}, u32[]{:S(2)}) collective-permute-start(bf16[256,768]{1,0:T(8,128)(2,1)S(1)} %get-tuple-element.48.refs_10_.refs_0_), channel_id=1, source_target_pairs={{0,32},{1,5},{2,34},{3,7},{4,36},{5,9},{6,38},{7,11},{8,40},{9,13}... | collective-permute-start | bytes 1179656 | tf_op jit(solution)/shard_map/ppermute | solution.py:57
  46.1 1.3 collective-permute-start.11
  47.3 3.3 %collective-permute-start.12 = (bf16[256,1024]{1,0:T(8,128)(2,1)}, bf16[256,1024]{1,0:T(8,128)(2,1)S(1)}, u32[]{:S(2)}, u32[]{:S(2)}) collective-permute-start(bf16[256,1024]{1,0:T(8,128)(2,1)} %collective-permute-done.5.refs_3_), channel_id=1, source_target_pairs={{1,29},{3,31},{5,1},{7,3},{9,5},{11,7},{13,9},{15,11},{17,13},{19,... | collective-permute-start | bytes 1572872 | tf_op jit(solution)/shard_map/ppermute | solution.py:57
  50.7 1.0 collective-permute-done.13.refs_12_.refs_2_
  51.6 0.7 collective-permute-start.10
  52.8 0.7 collective-permute-start.9
  53.5 1.8 %collective-permute-start.18 = (bf16[256,768]{1,0:T(8,128)(2,1)}, bf16[256,768]{1,0:T(8,128)(2,1)S(1)}, u32[]{:S(2)}, u32[]{:S(2)}) collective-permute-start(bf16[256,768]{1,0:T(8,128)(2,1)} %collective-permute-done.13.refs_12_.refs_2_), channel_id=1, source_target_pairs={{0,32},{1,5},{2,34},{3,7},{4,36},{5,9},{6,38},{7,11},{8,40},{9,13}... | collective-permute-start | bytes 1179656 | tf_op jit(solution)/shard_map/ppermute | solution.py:57
  55.3 2.9 %collective-permute-start.19 = (bf16[256,768]{1,0:T(8,128)(2,1)}, bf16[256,768]{1,0:T(8,128)(2,1)}, u32[]{:S(2)}, u32[]{:S(2)}) collective-permute-start(bf16[256,768]{1,0:T(8,128)(2,1)} %collective-permute-done.14.refs_13_.refs_3_), channel_id=1, source_target_pairs={{1,29},{3,31},{5,1},{7,3},{9,5},{11,7},{13,9},{15,11},{17,13},{19,... | collective-permute-start | bytes 1179656 | tf_op jit(solution)/shard_map/ppermute | solution.py:57
  59.5 1.6 %collective-permute-start.16 = (bf16[256,1024]{1,0:T(8,128)(2,1)S(1)}, bf16[256,1024]{1,0:T(8,128)(2,1)S(1)}, u32[]{:S(2)}, u32[]{:S(2)}) collective-permute-start(bf16[256,1024]{1,0:T(8,128)(2,1)S(1)} %get-tuple-element.55), channel_id=1, source_target_pairs={{0,32},{1,5},{2,34},{3,7},{4,36},{5,9},{6,38},{7,11},{8,40},{9,13}... | collective-permute-start | bytes 1572872 | tf_op jit(solution)/shard_map/ppermute | solution.py:57
  61.1 1.1 collective-permute-start.17
  62.2 2.9 %collective-permute-done.19.refs_15_.refs_5_ = bf16[256,768]{1,0:T(8,128)(2,1)} collective-permute-done((bf16[256,768]{1,0:T(8,128)(2,1)}, bf16[256,768]{1,0:T(8,128)(2,1)}, u32[]{:S(2)}, u32[]{:S(2)}) %collective-permute-start.19) | collective-permute-done | bytes 393248 | tf_op jit(solution)/shard_map/ppermute | solution.py:57
  65.1 1.1 broadcast_select_fusion.2
  66.2 1.6 %collective-permute-start.22 = (bf16[256,768]{1,0:T(8,128)(2,1)S(1)}, bf16[256,768]{1,0:T(8,128)(2,1)S(1)}, u32[]{:S(2)}, u32[]{:S(2)}) collective-permute-start(bf16[256,768]{1,0:T(8,128)(2,1)S(1)} %get-tuple-element.57), channel_id=1, source_target_pairs={{0,32},{1,5},{2,34},{3,7},{4,36},{5,9},{6,38},{7,11},{8,40},{9,13}... | collective-permute-start | bytes 1179656 | tf_op jit(solution)/shard_map/ppermute | solution.py:57
  67.7 1.2 collective-permute-start.23
  68.9 1.7 %collective-permute-done.16.refs_6_ = bf16[256,1024]{1,0:T(8,128)(2,1)S(1)} collective-permute-done((bf16[256,1024]{1,0:T(8,128)(2,1)S(1)}, bf16[256,1024]{1,0:T(8,128)(2,1)S(1)}, u32[]{:S(2)}, u32[]{:S(2)}) %collective-permute-start.16) | collective-permute-done | bytes 524320 | tf_op jit(solution)/shard_map/ppermute | solution.py:57
  70.7 0.8 slice.21
  71.6 1.6 %collective-permute-start.20 = (bf16[128,1024]{1,0:T(8,128)(2,1)}, bf16[128,1024]{1,0:T(8,128)(2,1)S(1)}, u32[]{:S(2)}, u32[]{:S(2)}) collective-permute-start(bf16[128,1024]{1,0:T(8,128)(2,1)} %slice.21), channel_id=1, source_target_pairs={{0,32},{1,5},{2,34},{3,7},{4,36},{5,9},{6,38},{7,11},{8,40},{9,13}... | collective-permute-start | bytes 786440 | tf_op jit(solution)/shard_map/ppermute | solution.py:57
  73.2 0.7 slice.22
  73.9 1.0 collective-permute-start.21
  75.5 2.3 %collective-permute-start.25 = (bf16[128,768]{1,0:T(8,128)(2,1)S(1)}, bf16[128,768]{1,0:T(8,128)(2,1)S(1)}, u32[]{:S(2)}, u32[]{:S(2)}) collective-permute-start(bf16[128,768]{1,0:T(8,128)(2,1)S(1)} %slice.29), channel_id=1, source_target_pairs={{0,96},{1,29},{2,98},{3,31},{4,100},{5,1},{6,102},{7,3},{8,104},{9... | collective-permute-start | bytes 589832 | tf_op jit(solution)/shard_map/ppermute | solution.py:57
  78.5 1.2 collective-permute-done.21.refs_9_
  79.7 0.7 copy-done.21
  80.4 7.1 %weight_term.2.mine = bf16[640,1024]{1,0:T(8,128)(2,1)} custom-call(s32[3]{0:T(128)} %pad_add_fusion.where, bf16[256,1024]{1,0:T(8,128)(2,1)} %copy-done.10, bf16[256,1024]{1,0:T(8,128)(2,1)} %copy-done.3, bf16[256,1024]{1,0:T(8,128)(2,1)} %collective-permute-done.4.refs_2_, bf16[256,1024]{1,0:T(8,128)(2,1)} %collective-permute-done.5.refs_3_, ...), custom_call_target="tpu_custom_call" | custom-call | flops 1 | bytes 1 | tf_op jit(solution)/shard_map/weight_term/pallas_call | solution.py:179
  87.5 1.3 collective-permute-start.28
  90.2 0.7 copy-done.23
  90.9 12.5 %act_parts.1.parts = bf16[2048,640]{1,0:T(8,128)(2,1)} custom-call(s32[3]{0:T(128)} %pad_add_fusion.where, f32[1]{0:T(128)S(6)} %copy.11.weight_scale, bf16[1792,640]{1,0:T(8,128)(2,1)} %codes.1, bf16[256,1024]{1,0:T(8,128)(2,1)} %copy-done.10, bf16[256,1024]{1,0:T(8,128)(2,1)} %copy-done.3, bf16[256,1024]{1,0:T(8,128)(2,1)} %collective-permute-done.4.refs_2_, ...), custom_call_target="tpu_custom_call" | custom-call | flops 1 | bytes 1 | tf_op jit(solution)/shard_map/act_parts/pallas_call | solution.py:260
  103.4 2.5 %slice.25 = bf16[1024,640]{1,0:T(8,128)(2,1)} slice(bf16[2048,640]{1,0:T(8,128)(2,1)} %act_parts.1.parts), slice={[0:1024], [0:640]} | slice | bytes 2621440 | tf_op jit(solution)/shard_map/slice | solution.py:347
  105.9 10.1 %collective-permute-start.26 = (bf16[1024,640]{1,0:T(8,128)(2,1)}, bf16[1024,640]{1,0:T(8,128)(2,1)S(1)}, u32[]{:S(2)}, u32[]{:S(2)}) collective-permute-start(bf16[1024,640]{1,0:T(8,128)(2,1)} %slice.25), channel_id=1, source_target_pairs={{0,1},{1,0},{2,3},{3,2},{4,5},{5,4},{6,7},{7,6},{8,9},{9,8},{10,11... | collective-permute-start | bytes 3932168 | tf_op jit(solution)/shard_map/ppermute | solution.py:347
  116.0 7.6 %weight_term.3.mine = bf16[640,768]{1,0:T(8,128)(2,1)} custom-call(s32[3]{0:T(128)} %pad_add_fusion.where, bf16[256,768]{1,0:T(8,128)(2,1)} %copy-done.11, bf16[256,768]{1,0:T(8,128)(2,1)} %copy-done.5, bf16[256,768]{1,0:T(8,128)(2,1)} %collective-permute-done.13.refs_12_.refs_2_, bf16[256,768]{1,0:T(8,128)(2,1)} %collective-permute-done.14.refs_13_.refs_3_, ...), custom_call_target="tpu_custom_call" | custom-call | flops 1 | bytes 1 | tf_op jit(solution)/shard_map/weight_term/pallas_call | solution.py:179
  124.1 3.2 %collective-permute-start.27 = (bf16[512,640]{1,0:T(8,128)(2,1)S(1)}, bf16[512,640]{1,0:T(8,128)(2,1)S(1)}, u32[]{:S(2)}, u32[]{:S(2)}) collective-permute-start(bf16[512,640]{1,0:T(8,128)(2,1)S(1)} %add_convert_fusion), channel_id=1, source_target_pairs={{0,130},{1,131},{2,128},{3,129},{128,2},{129,3},{130,0},{131,1},{4... | collective-permute-start | bytes 1966088 | tf_op jit(solution)/shard_map/ppermute | solution.py:351
  127.4 3.1 %sum_terms.2.refs_0_ = f32[1792,640]{1,0:T(8,128)} custom-call(bf16[640,1024]{1,0:T(8,128)(2,1)S(1)} %copy-done.2, bf16[640,1024]{1,0:T(8,128)(2,1)} %collective-permute-done.28.theirs), custom_call_target="tpu_custom_call" | custom-call | tf_op jit(solution)/shard_map/sum_terms/pallas_call | solution.py:215
  130.5 11.5 %collective-permute-done.27.other = bf16[512,640]{1,0:T(8,128)(2,1)S(1)} collective-permute-done((bf16[512,640]{1,0:T(8,128)(2,1)S(1)}, bf16[512,640]{1,0:T(8,128)(2,1)S(1)}, u32[]{:S(2)}, u32[]{:S(2)}) %collective-permute-start.27) | collective-permute-done | bytes 655392 | tf_op jit(solution)/shard_map/ppermute | solution.py:351
  142.0 1.7 %finish.1 = bf16[512,640]{1,0:T(8,128)(2,1)} custom-call(bf16[2048,640]{1,0:T(8,128)(2,1)S(1)} %copy-done, bf16[1024,640]{1,0:T(8,128)(2,1)S(1)} %collective-permute-done.26.got, bf16[512,640]{1,0:T(8,128)(2,1)S(1)} %collective-permute-done.27.other, bf16[512,640]{1,0:T(8,128)(2,1)S(1)} %copy-done.7, f32[512,1]{1,0:T(8,128)S(1)} %copy-done.9, ...), custom_call_target="tpu_custom_call" | custom-call | tf_op jit(solution)/shard_map/finish/pallas_call | solution.py:292
  143.7 3.4 %collective-permute-done.29.theirs = bf16[640,768]{1,0:T(8,128)(2,1)S(1)} collective-permute-done((bf16[640,768]{1,0:T(8,128)(2,1)}, bf16[640,768]{1,0:T(8,128)(2,1)S(1)}, u32[]{:S(2)}, u32[]{:S(2)}) %collective-permute-start.29) | collective-permute-done | bytes 983072 | tf_op jit(solution)/shard_map/ppermute | solution.py:349
  147.1 1.5 sum_terms.3
  (81 shorter events, 6.1 us)
Async XLA Ops:
  0.6 1.6 %collective-permute-start = (bf16[64,1792]{1,0:T(8,128)(2,1)}, bf16[64,1792]{1,0:T(8,128)(2,1)S(1)}, u32[]{:S(2)}, u32[]{:S(2)}) collective-permute-start(bf16[64,1792]{1,0:T(8,128)(2,1)} %param.5), channel_id=1, source_target_pairs={{0,0},{1,1},{2,130},{3,131},{4,4},{5,5},{6,134},{7,135},{8,8},{9,9... | collective-permute-start | bytes 688136 | tf_op jit(solution)/shard_map/ppermute | solution.py:57
  2.2 16.4 %collective-permute-start.1 = (bf16[64,1792]{1,0:T(8,128)(2,1)S(1)}, bf16[64,1792]{1,0:T(8,128)(2,1)S(1)}, u32[]{:S(2)}, u32[]{:S(2)}) collective-permute-start(bf16[64,1792]{1,0:T(8,128)(2,1)S(1)} %collective-permute-done.refs_2_), channel_id=1, source_target_pairs={{0,8},{1,65},{2,10},{3,67},{4,12},{5,69},{6,14},{7,71},{8,16},{9,7... | collective-permute-start | bytes 688136 | tf_op jit(solution)/shard_map/ppermute | solution.py:57
  12.9 6.3 %collective-permute-start.3 = (bf16[64,1792]{1,0:T(8,128)(2,1)S(1)}, bf16[64,1792]{1,0:T(8,128)(2,1)S(1)}, u32[]{:S(2)}, u32[]{:S(2)}) collective-permute-start(bf16[64,1792]{1,0:T(8,128)(2,1)S(1)} %collective-permute-done.refs_2_), channel_id=1, source_target_pairs={{0,28},{1,97},{2,30},{3,99},{4,0},{5,101},{6,2},{7,103},{8,4},{9,1... | collective-permute-start | bytes 688136 | tf_op jit(solution)/shard_map/ppermute | solution.py:57
  13.0 6.3 %collective-permute-start.2 = (bf16[64,1792]{1,0:T(8,128)(2,1)S(1)}, bf16[64,1792]{1,0:T(8,128)(2,1)S(1)}, u32[]{:S(2)}, u32[]{:S(2)}) collective-permute-start(bf16[64,1792]{1,0:T(8,128)(2,1)S(1)} %collective-permute-done.refs_2_), channel_id=1, source_target_pairs={{0,4},{1,33},{2,6},{3,35},{4,8},{5,37},{6,10},{7,39},{8,12},{9,41}... | collective-permute-start | bytes 688136 | tf_op jit(solution)/shard_map/ppermute | solution.py:57
  15.2 1.1 copy-start.6
  16.3 16.8 %copy-start.8 = (f32[512,1]{1,0:T(8,128)}, f32[512,1]{1,0:T(8,128)S(1)}, u32[]{:S(2)}) copy-start(f32[512,1]{1,0:T(8,128)S(1)} %copy.8.bound) | copy-start | bytes 6148
  16.8 16.4 %copy-start.1 = (bf16[640,512]{1,0:T(8,128)(2,1)}, bf16[640,512]{1,0:T(8,128)(2,1)S(1)}, u32[]{:S(2)}) copy-start(bf16[640,512]{1,0:T(8,128)(2,1)S(1)} %clip_turned.1.refs_10_) | copy-start | bytes 1966084
  16.8 15.1 %collective-permute-start.8 = (bf16[640,512]{1,0:T(8,128)(2,1)S(1)}, bf16[640,512]{1,0:T(8,128)(2,1)S(1)}, u32[]{:S(2)}, u32[]{:S(2)}) collective-permute-start(bf16[640,512]{1,0:T(8,128)(2,1)S(1)} %clip_turned.1.refs_10_), channel_id=1, source_target_pairs={{0,130},{1,131},{2,128},{3,129},{128,2},{129,3},{130,0},{131,1},{4... | collective-permute-start | bytes 1966088 | tf_op jit(solution)/shard_map/ppermute | solution.py:320
  19.3 13.8 %copy-start.10 = (bf16[256,1024]{1,0:T(8,128)(2,1)}, bf16[256,1024]{1,0:T(8,128)(2,1)S(1)}, u32[]{:S(2)}) copy-start(bf16[256,1024]{1,0:T(8,128)(2,1)S(1)} %get-tuple-element.41.refs_0_) | copy-start | bytes 1572868
  19.3 26.3 %copy-start.11 = (bf16[256,768]{1,0:T(8,128)(2,1)}, bf16[256,768]{1,0:T(8,128)(2,1)S(1)}, u32[]{:S(2)}) copy-start(bf16[256,768]{1,0:T(8,128)(2,1)S(1)} %get-tuple-element.48.refs_10_.refs_0_) | copy-start | bytes 1179652
  19.3 12.6 %collective-permute-start.4 = (bf16[256,1024]{1,0:T(8,128)(2,1)S(1)}, bf16[256,1024]{1,0:T(8,128)(2,1)}, u32[]{:S(2)}, u32[]{:S(2)}) collective-permute-start(bf16[256,1024]{1,0:T(8,128)(2,1)S(1)} %get-tuple-element.41.refs_0_), channel_id=1, source_target_pairs={{0,32},{1,5},{2,34},{3,7},{4,36},{5,9},{6,38},{7,11},{8,40},{9,13}... | collective-permute-start | bytes 1572872 | tf_op jit(solution)/shard_map/ppermute | solution.py:57
  21.1 10.9 %collective-permute-start.5 = (bf16[256,1024]{1,0:T(8,128)(2,1)S(1)}, bf16[256,1024]{1,0:T(8,128)(2,1)}, u32[]{:S(2)}, u32[]{:S(2)}) collective-permute-start(bf16[256,1024]{1,0:T(8,128)(2,1)S(1)} %get-tuple-element.41.refs_0_), channel_id=1, source_target_pairs={{0,96},{1,29},{2,98},{3,31},{4,100},{5,1},{6,102},{7,3},{8,104},{9... | collective-permute-start | bytes 1572872 | tf_op jit(solution)/shard_map/ppermute | solution.py:57
  25.1 6.8 %collective-permute-start.6 = (bf16[64,1792]{1,0:T(8,128)(2,1)S(1)}, bf16[64,1792]{1,0:T(8,128)(2,1)S(1)}, u32[]{:S(2)}, u32[]{:S(2)}) collective-permute-start(bf16[64,1792]{1,0:T(8,128)(2,1)S(1)} %collective-permute-done.1.refs_0_), channel_id=1, source_target_pairs={{0,4},{2,6},{4,8},{6,10},{8,12},{10,14},{12,16},{14,18},{16,20},{1... | collective-permute-start | bytes 688136 | tf_op jit(solution)/shard_map/ppermute | solution.py:57
  25.8 6.1 %collective-permute-start.7 = (bf16[64,1792]{1,0:T(8,128)(2,1)S(1)}, bf16[64,1792]{1,0:T(8,128)(2,1)S(1)}, u32[]{:S(2)}, u32[]{:S(2)}) collective-permute-start(bf16[64,1792]{1,0:T(8,128)(2,1)S(1)} %collective-permute-done.3.refs_3_), channel_id=1, source_target_pairs={{0,28},{2,30},{4,0},{6,2},{8,4},{10,6},{12,8},{14,10},{16,12},{18,... | collective-permute-start | bytes 688136 | tf_op jit(solution)/shard_map/ppermute | solution.py:57
  31.8 11.6 %copy-start.12 = (bf16[640,512]{1,0:T(8,128)(2,1)}, bf16[640,512]{1,0:T(8,128)(2,1)S(1)}, u32[]{:S(2)}) copy-start(bf16[640,512]{1,0:T(8,128)(2,1)S(1)} %collective-permute-done.8.refs_12_) | copy-start | bytes 1966084
  33.1 25.5 %collective-permute-start.15 = (bf16[1280,512]{1,0:T(8,128)(2,1)}, bf16[1280,512]{1,0:T(8,128)(2,1)}, u32[]{:S(2)}, u32[]{:S(2)}) collective-permute-start(bf16[1280,512]{1,0:T(8,128)(2,1)} %pad_maximum_fusion), channel_id=1, source_target_pairs={{0,1},{1,0},{2,3},{3,2},{4,5},{5,4},{6,7},{7,6},{8,9},{9,8},{10,11... | collective-permute-start | bytes 3932168 | tf_op jit(solution)/shard_map/ppermute | solution.py:329
  43.4 8.2 %collective-permute-start.13 = (bf16[256,768]{1,0:T(8,128)(2,1)S(1)}, bf16[256,768]{1,0:T(8,128)(2,1)}, u32[]{:S(2)}, u32[]{:S(2)}) collective-permute-start(bf16[256,768]{1,0:T(8,128)(2,1)S(1)} %get-tuple-element.48.refs_10_.refs_0_), channel_id=1, source_target_pairs={{0,32},{1,5},{2,34},{3,7},{4,36},{5,9},{6,38},{7,11},{8,40},{9,13}... | collective-permute-start | bytes 1179656 | tf_op jit(solution)/shard_map/ppermute | solution.py:57
  45.6 7.2 %collective-permute-start.14 = (bf16[256,768]{1,0:T(8,128)(2,1)S(1)}, bf16[256,768]{1,0:T(8,128)(2,1)}, u32[]{:S(2)}, u32[]{:S(2)}) collective-permute-start(bf16[256,768]{1,0:T(8,128)(2,1)S(1)} %get-tuple-element.48.refs_10_.refs_0_), channel_id=1, source_target_pairs={{0,96},{1,29},{2,98},{3,31},{4,100},{5,1},{6,102},{7,3},{8,104},{9... | collective-permute-start | bytes 1179656 | tf_op jit(solution)/shard_map/ppermute | solution.py:57
  46.1 12.2 %collective-permute-start.11 = (bf16[256,1024]{1,0:T(8,128)(2,1)}, bf16[256,1024]{1,0:T(8,128)(2,1)S(1)}, u32[]{:S(2)}, u32[]{:S(2)}) collective-permute-start(bf16[256,1024]{1,0:T(8,128)(2,1)} %collective-permute-done.4.refs_2_), channel_id=1, source_target_pairs={{0,32},{1,5},{2,34},{3,7},{4,36},{5,9},{6,38},{7,11},{8,40},{9,13}... | collective-permute-start | bytes 1572872 | tf_op jit(solution)/shard_map/ppermute | solution.py:57
  47.3 11.3 %collective-permute-start.12 = (bf16[256,1024]{1,0:T(8,128)(2,1)}, bf16[256,1024]{1,0:T(8,128)(2,1)S(1)}, u32[]{:S(2)}, u32[]{:S(2)}) collective-permute-start(bf16[256,1024]{1,0:T(8,128)(2,1)} %collective-permute-done.5.refs_3_), channel_id=1, source_target_pairs={{1,29},{3,31},{5,1},{7,3},{9,5},{11,7},{13,9},{15,11},{17,13},{19,... | collective-permute-start | bytes 1572872 | tf_op jit(solution)/shard_map/ppermute | solution.py:57
  51.6 1.8 %collective-permute-start.10 = (bf16[64,1792]{1,0:T(8,128)(2,1)S(1)}, bf16[64,1792]{1,0:T(8,128)(2,1)S(1)}, u32[]{:S(2)}, u32[]{:S(2)}) collective-permute-start(bf16[64,1792]{1,0:T(8,128)(2,1)S(1)} %collective-permute-done.7.refs_2_), channel_id=1, source_target_pairs={{0,28},{2,30},{4,0},{6,2},{8,4},{10,6},{12,8},{14,10},{16,12},{18,... | collective-permute-start | bytes 688136 | tf_op jit(solution)/shard_map/ppermute | solution.py:57
  52.8 2.4 %collective-permute-start.9 = (bf16[64,1792]{1,0:T(8,128)(2,1)S(1)}, bf16[64,1792]{1,0:T(8,128)(2,1)S(1)}, u32[]{:S(2)}, u32[]{:S(2)}) collective-permute-start(bf16[64,1792]{1,0:T(8,128)(2,1)S(1)} %collective-permute-done.6.refs_1_), channel_id=1, source_target_pairs={{0,4},{2,6},{4,8},{6,10},{8,12},{10,14},{12,16},{14,18},{16,20},{1... | collective-permute-start | bytes 688136 | tf_op jit(solution)/shard_map/ppermute | solution.py:57
  53.5 8.7 %collective-permute-start.18 = (bf16[256,768]{1,0:T(8,128)(2,1)}, bf16[256,768]{1,0:T(8,128)(2,1)S(1)}, u32[]{:S(2)}, u32[]{:S(2)}) collective-permute-start(bf16[256,768]{1,0:T(8,128)(2,1)} %collective-permute-done.13.refs_12_.refs_2_), channel_id=1, source_target_pairs={{0,32},{1,5},{2,34},{3,7},{4,36},{5,9},{6,38},{7,11},{8,40},{9,13}... | collective-permute-start | bytes 1179656 | tf_op jit(solution)/shard_map/ppermute | solution.py:57
  55.3 9.8 %collective-permute-start.19 = (bf16[256,768]{1,0:T(8,128)(2,1)}, bf16[256,768]{1,0:T(8,128)(2,1)}, u32[]{:S(2)}, u32[]{:S(2)}) collective-permute-start(bf16[256,768]{1,0:T(8,128)(2,1)} %collective-permute-done.14.refs_13_.refs_3_), channel_id=1, source_target_pairs={{1,29},{3,31},{5,1},{7,3},{9,5},{11,7},{13,9},{15,11},{17,13},{19,... | collective-permute-start | bytes 1179656 | tf_op jit(solution)/shard_map/ppermute | solution.py:57
  58.2 6.9 %copy-start.5 = (bf16[256,768]{1,0:T(8,128)(2,1)}, bf16[256,768]{1,0:T(8,128)(2,1)S(1)}, u32[]{:S(2)}) copy-start(bf16[256,768]{1,0:T(8,128)(2,1)S(1)} %get-tuple-element.42.refs_11_.refs_1_) | copy-start | bytes 1179652
  59.5 11.1 %collective-permute-start.16 = (bf16[256,1024]{1,0:T(8,128)(2,1)S(1)}, bf16[256,1024]{1,0:T(8,128)(2,1)S(1)}, u32[]{:S(2)}, u32[]{:S(2)}) collective-permute-start(bf16[256,1024]{1,0:T(8,128)(2,1)S(1)} %get-tuple-element.55), channel_id=1, source_target_pairs={{0,32},{1,5},{2,34},{3,7},{4,36},{5,9},{6,38},{7,11},{8,40},{9,13}... | collective-permute-start | bytes 1572872 | tf_op jit(solution)/shard_map/ppermute | solution.py:57
  61.1 9.6 %collective-permute-start.17 = (bf16[256,1024]{1,0:T(8,128)(2,1)S(1)}, bf16[256,1024]{1,0:T(8,128)(2,1)S(1)}, u32[]{:S(2)}, u32[]{:S(2)}) collective-permute-start(bf16[256,1024]{1,0:T(8,128)(2,1)S(1)} %get-tuple-element.54), channel_id=1, source_target_pairs={{0,96},{1,29},{2,98},{3,31},{4,100},{5,1},{6,102},{7,3},{8,104},{9... | collective-permute-start | bytes 1572872 | tf_op jit(solution)/shard_map/ppermute | solution.py:57
  62.2 11.7 %copy-start.15 = (bf16[256,768]{1,0:T(8,128)(2,1)}, bf16[256,768]{1,0:T(8,128)(2,1)S(1)}, u32[]{:S(2)}) copy-start(bf16[256,768]{1,0:T(8,128)(2,1)S(1)} %collective-permute-done.18.refs_14_.refs_4_) | copy-start | bytes 1179652
  66.2 8.8 %collective-permute-start.22 = (bf16[256,768]{1,0:T(8,128)(2,1)S(1)}, bf16[256,768]{1,0:T(8,128)(2,1)S(1)}, u32[]{:S(2)}, u32[]{:S(2)}) collective-permute-start(bf16[256,768]{1,0:T(8,128)(2,1)S(1)} %get-tuple-element.57), channel_id=1, source_target_pairs={{0,32},{1,5},{2,34},{3,7},{4,36},{5,9},{6,38},{7,11},{8,40},{9,13}... | collective-permute-start | bytes 1179656 | tf_op jit(solution)/shard_map/ppermute | solution.py:57
  67.7 7.8 %collective-permute-start.23 = (bf16[256,768]{1,0:T(8,128)(2,1)S(1)}, bf16[256,768]{1,0:T(8,128)(2,1)S(1)}, u32[]{:S(2)}, u32[]{:S(2)}) collective-permute-start(bf16[256,768]{1,0:T(8,128)(2,1)S(1)} %get-tuple-element.56), channel_id=1, source_target_pairs={{0,96},{1,29},{2,98},{3,31},{4,100},{5,1},{6,102},{7,3},{8,104},{9... | collective-permute-start | bytes 1179656 | tf_op jit(solution)/shard_map/ppermute | solution.py:57
  70.6 9.1 %copy-start.16 = (bf16[256,1024]{1,0:T(8,128)(2,1)}, bf16[256,1024]{1,0:T(8,128)(2,1)S(1)}, u32[]{:S(2)}) copy-start(bf16[256,1024]{1,0:T(8,128)(2,1)S(1)} %collective-permute-done.16.refs_6_) | copy-start | bytes 1572868
  70.7 8.9 %copy-start.17 = (bf16[256,1024]{1,0:T(8,128)(2,1)}, bf16[256,1024]{1,0:T(8,128)(2,1)S(1)}, u32[]{:S(2)}) copy-start(bf16[256,1024]{1,0:T(8,128)(2,1)S(1)} %collective-permute-done.17.refs_7_) | copy-start | bytes 1572868
  71.6 6.9 %collective-permute-start.20 = (bf16[128,1024]{1,0:T(8,128)(2,1)}, bf16[128,1024]{1,0:T(8,128)(2,1)S(1)}, u32[]{:S(2)}, u32[]{:S(2)}) collective-permute-start(bf16[128,1024]{1,0:T(8,128)(2,1)} %slice.21), channel_id=1, source_target_pairs={{0,32},{1,5},{2,34},{3,7},{4,36},{5,9},{6,38},{7,11},{8,40},{9,13}... | collective-permute-start | bytes 786440 | tf_op jit(solution)/shard_map/ppermute | solution.py:57
  73.9 5.7 %collective-permute-start.21 = (bf16[128,1024]{1,0:T(8,128)(2,1)}, bf16[128,1024]{1,0:T(8,128)(2,1)S(1)}, u32[]{:S(2)}, u32[]{:S(2)}) collective-permute-start(bf16[128,1024]{1,0:T(8,128)(2,1)} %slice.22), channel_id=1, source_target_pairs={{0,96},{1,29},{2,98},{3,31},{4,100},{5,1},{6,102},{7,3},{8,104},{9... | collective-permute-start | bytes 786440 | tf_op jit(solution)/shard_map/ppermute | solution.py:57
  75.0 12.6 %copy-start.18 = (bf16[256,768]{1,0:T(8,128)(2,1)}, bf16[256,768]{1,0:T(8,128)(2,1)S(1)}, u32[]{:S(2)}) copy-start(bf16[256,768]{1,0:T(8,128)(2,1)S(1)} %collective-permute-done.22.refs_16_.refs_6_) | copy-start | bytes 1179652
  75.0 14.5 %collective-permute-start.24 = (bf16[128,768]{1,0:T(8,128)(2,1)S(1)}, bf16[128,768]{1,0:T(8,128)(2,1)S(1)}, u32[]{:S(2)}, u32[]{:S(2)}) collective-permute-start(bf16[128,768]{1,0:T(8,128)(2,1)S(1)} %slice.28), channel_id=1, source_target_pairs={{0,32},{1,5},{2,34},{3,7},{4,36},{5,9},{6,38},{7,11},{8,40},{9,13}... | collective-permute-start | bytes 589832 | tf_op jit(solution)/shard_map/ppermute | solution.py:57
  75.5 12.0 %copy-start.19 = (bf16[256,768]{1,0:T(8,128)(2,1)}, bf16[256,768]{1,0:T(8,128)(2,1)S(1)}, u32[]{:S(2)}) copy-start(bf16[256,768]{1,0:T(8,128)(2,1)S(1)} %collective-permute-done.23.refs_17_.refs_7_) | copy-start | bytes 1179652
  75.5 14.0 %collective-permute-start.25 = (bf16[128,768]{1,0:T(8,128)(2,1)S(1)}, bf16[128,768]{1,0:T(8,128)(2,1)S(1)}, u32[]{:S(2)}, u32[]{:S(2)}) collective-permute-start(bf16[128,768]{1,0:T(8,128)(2,1)S(1)} %slice.29), channel_id=1, source_target_pairs={{0,96},{1,29},{2,98},{3,31},{4,100},{5,1},{6,102},{7,3},{8,104},{9... | collective-permute-start | bytes 589832 | tf_op jit(solution)/shard_map/ppermute | solution.py:57
  78.5 1.2 copy-start.20
  87.5 36.1 %collective-permute-start.28 = (bf16[640,1024]{1,0:T(8,128)(2,1)}, bf16[640,1024]{1,0:T(8,128)(2,1)}, u32[]{:S(2)}, u32[]{:S(2)}) collective-permute-start(bf16[640,1024]{1,0:T(8,128)(2,1)} %weight_term.2.mine), channel_id=1, source_target_pairs={{0,128},{128,0},{1,129},{129,1},{2,130},{130,2},{3,131},{131,3},{4... | collective-permute-start | bytes 3932168 | tf_op jit(solution)/shard_map/ppermute | solution.py:341
  105.9 18.1 %copy-start = (bf16[2048,640]{1,0:T(8,128)(2,1)S(1)}, bf16[2048,640]{1,0:T(8,128)(2,1)}, u32[]{:S(2)}) copy-start(bf16[2048,640]{1,0:T(8,128)(2,1)} %act_parts.1.parts) | copy-start | bytes 7864324
  105.9 18.1 %collective-permute-start.26 = (bf16[1024,640]{1,0:T(8,128)(2,1)}, bf16[1024,640]{1,0:T(8,128)(2,1)S(1)}, u32[]{:S(2)}, u32[]{:S(2)}) collective-permute-start(bf16[1024,640]{1,0:T(8,128)(2,1)} %slice.25), channel_id=1, source_target_pairs={{0,1},{1,0},{2,3},{3,2},{4,5},{5,4},{6,7},{7,6},{8,9},{9,8},{10,11... | collective-permute-start | bytes 3932168 | tf_op jit(solution)/shard_map/ppermute | solution.py:347
  123.6 3.7 %copy-start.2 = (bf16[640,1024]{1,0:T(8,128)(2,1)S(1)}, bf16[640,1024]{1,0:T(8,128)(2,1)}, u32[]{:S(2)}) copy-start(bf16[640,1024]{1,0:T(8,128)(2,1)} %weight_term.2.mine) | copy-start | bytes 3932164
  123.6 23.5 %collective-permute-start.29 = (bf16[640,768]{1,0:T(8,128)(2,1)}, bf16[640,768]{1,0:T(8,128)(2,1)S(1)}, u32[]{:S(2)}, u32[]{:S(2)}) collective-permute-start(bf16[640,768]{1,0:T(8,128)(2,1)} %weight_term.3.mine), channel_id=1, source_target_pairs={{0,128},{128,0},{1,129},{129,1},{2,130},{130,2},{3,131},{131,3},{4... | collective-permute-start | bytes 2949128 | tf_op jit(solution)/shard_map/ppermute | solution.py:349
  124.1 17.9 %collective-permute-start.27 = (bf16[512,640]{1,0:T(8,128)(2,1)S(1)}, bf16[512,640]{1,0:T(8,128)(2,1)S(1)}, u32[]{:S(2)}, u32[]{:S(2)}) collective-permute-start(bf16[512,640]{1,0:T(8,128)(2,1)S(1)} %add_convert_fusion), channel_id=1, source_target_pairs={{0,130},{1,131},{2,128},{3,129},{128,2},{129,3},{130,0},{131,1},{4... | collective-permute-start | bytes 1966088 | tf_op jit(solution)/shard_map/ppermute | solution.py:351
  127.3 14.7 %copy-start.7 = (bf16[512,640]{1,0:T(8,128)(2,1)S(1)}, bf16[512,640]{1,0:T(8,128)(2,1)}, u32[]{:S(2)}) copy-start(bf16[512,640]{1,0:T(8,128)(2,1)} %rotated.3) | copy-start | bytes 1966084
  127.3 14.7 %copy-start.9 = (f32[512,1]{1,0:T(8,128)S(1)}, f32[512,1]{1,0:T(8,128)}, u32[]{:S(2)}) copy-start(f32[512,1]{1,0:T(8,128)} %copy-done.8) | copy-start | bytes 6148
  130.5 16.6 %copy-start.4 = (bf16[640,768]{1,0:T(8,128)(2,1)S(1)}, bf16[640,768]{1,0:T(8,128)(2,1)}, u32[]{:S(2)}) copy-start(bf16[640,768]{1,0:T(8,128)(2,1)} %weight_term.3.mine) | copy-start | bytes 2949124
  (6 other events, 4.8 us)

commit v3 on v2

--- a/solution.py
+++ b/solution.py
@@ -13,7 +13,7 @@
 BF = jnp.bfloat16
 F32 = jnp.float32
 
-WIDTHS = (1024, 768)
+WIDTHS = (896, 896)
 VMEM = 60 * 2**20
 SMALL = 16 * 2**20
 HALF = 512
@@ -35,6 +35,7 @@
 
 CORE = [(r, r ^ 1) for r in range(4)]
 DP = [(0, 1), (1, 0)]
+PARTNER_SIBLING = [(d * 4 + r, (1 - d) * 4 + (r ^ 3)) for d in range(2) for r in range(4)]
 PARTNER = [(d * 4 + r, (1 - d) * 4 + (r ^ 2)) for d in range(2) for r in range(4)]
 
 
@@ -57,45 +58,56 @@
     return lax.ppermute(value, ("dp", "col", "row"), pairs_for((core0, core1), swap))
 
 
-def join_kernel(*refs):
-    for at, shard in enumerate(refs[:4]):
+def near_kernel(c, a, own, b, *outs):
+    for i, shard in enumerate((c, a, own, b)):
         lo = 0
-        for out in refs[4:]:
+        for out in outs[:-2]:
             width = out.shape[1]
-            out[at * SHARD:(at + 1) * SHARD, :] = shard[:, lo:lo + width]
+            out[i * SHARD:(i + 1) * SHARD, :] = shard[:, lo:lo + width]
             lo += width
-
-
-def join(*shards):
+        outs[-2 + i // 2][i % 2 * SHARD:(i % 2 + 1) * SHARD, :] = shard[...]
+
+
+def far_kernel(low, high, *outs):
+    lo = 0
+    for out in outs:
+        width = out.shape[1]
+        out[:2 * SHARD, :] = low[:, lo:lo + width]
+        out[2 * SHARD:, :] = high[:, lo:lo + width]
+        lo += width
+
+
+def join(kernel, shards, extra):
     vmem = pl.BlockSpec(memory_space=pltpu.VMEM)
+    shapes = [(4 * SHARD, width) for width in WIDTHS] + extra
     return list(pl.pallas_call(
-        join_kernel,
-        out_shape=[jax.ShapeDtypeStruct((4 * SHARD, width), BF) for width in WIDTHS],
-        in_specs=[vmem] * 4,
-        out_specs=[vmem] * len(WIDTHS),
+        kernel,
+        out_shape=[jax.ShapeDtypeStruct(shape, BF) for shape in shapes],
+        in_specs=[vmem] * len(shards),
+        out_specs=[vmem] * len(shapes),
         compiler_params=pltpu.CompilerParams(vmem_limit_bytes=SMALL),
         cost_estimate=LITTLE,
         name="join",
     )(*shards))
 
 
-def gather(own, first_core, before_second, before_third):
+def gather(own, first_core, before_second):
     a = move(own, (0, 1), (1, 0))
     b = move(own, (0, -1), (-1, 0))
     c = move(own, (0, 2), (2, 0))
-    near = join(c, a, own, b)
-    up1 = [move(part, (1, 0), (0, 1)) for part in near]
-    down1 = [move(part, (-1, 0), (0, -1)) for part in near]
-    far_up = move(c, (0, 1), None)
-    far_down = move(b, (0, -1), None)
-    up1[0], down1[0], far_up, far_down = before_second(up1[0], down1[0], far_up, far_down)
+    *near, low, high = join(near_kernel, (c, a, own, b), [(2 * SHARD, own.shape[1])] * 2)
+    up1 = [move(near[0], (1, 0), (0, 1))]
+    down1 = [move(near[0], (-1, 0), (0, -1))]
+    low = move(low, (0, 2), None)
+    high = move(high, (0, -2), None)
+    near[1], low, high = before_second(near[1], low, high)
+    up1.append(move(near[1], (1, 0), (0, 1)))
+    down1.append(move(near[1], (-1, 0), (0, -1)))
     up2 = [move(part, (1, 0), (0, 1)) for part in up1]
     down2 = [move(part, None, (0, -1)) for part in down1]
-    far = join(move(far_up, (0, 1), None), far_up, far_down, move(far_down, (0, -1), None))
-    up2[0], down2[0], up1[1], down1[1] = before_third(up2[0], down2[0], up1[1], down1[1])
+    far = join(far_kernel, (low, high), [])
     up3 = [move(jnp.where(first_core, f, part), (1, 0), (0, 1)) for f, part in zip(far, up2)]
     down3 = [move(jnp.where(first_core, f, part), (-1, 0), (0, -1)) for f, part in zip(far, down2)]
-    up3[0], down3[0], up2[1], down2[1] = lax.optimization_barrier((up3[0], down3[0], up2[1], down2[1]))
     up4 = [move(part[:2 * SHARD], (1, 0), (0, 1)) for part in up3]
     down4 = [move(part[2 * SHARD:], (-1, 0), (0, -1)) for part in down3]
     return [list(group) for group in zip(near, far, up1, down1, up2, down2, up3, down3, up4, down4)]
@@ -144,10 +156,10 @@
 
 def weight_kernel(scale, where, *refs):
     n = PIECES
-    piece_refs, (own, both, other) = refs[:n], refs[n:n + 3]
-    out, held, clip_held, sem, clip_sem = refs[n + 3:]
-    cols, size = own.shape
-    for j, ref in enumerate((own, both.at[pl.ds(0, cols)], other, both.at[pl.ds(cols, cols)])):
+    piece_refs, clip_refs = refs[:n], refs[n:n + 4]
+    out, held, clip_held, sem, clip_sem = refs[n + 4:]
+    for j, ref in enumerate(clip_refs):
+        size = ref.shape[1]
         start = pl.multiple_of((where[2] ^ j) * size, size)
         pltpu.make_async_copy(ref, clip_held.at[:, pl.ds(start, size)], clip_sem).start()
     width = out.shape[1]
@@ -179,7 +191,7 @@
     return pl.pallas_call(
         functools.partial(weight_kernel, scale),
         out_shape=jax.ShapeDtypeStruct((cols, width), BF),
-        in_specs=[pl.BlockSpec(memory_space=pltpu.SMEM)] + [anywhere] * (len(pieces) + 3),
+        in_specs=[pl.BlockSpec(memory_space=pltpu.SMEM)] + [anywhere] * (len(pieces) + 4),
         out_specs=pl.BlockSpec(memory_space=pltpu.VMEM),
         scratch_shapes=[
             pltpu.VMEM((tokens, width), BF),
@@ -226,7 +238,7 @@
 
 def act_kernel(where, weight_scale, codes, *refs):
     n = PIECES * len(WIDTHS)
-    piece_refs, (out, held, code_held, sem, code_sem) = refs[:n], refs[n:]
+    piece_refs, (away, keep, held, code_held, sem, code_sem) = refs[:n], refs[n:]
     code_copy = pltpu.make_async_copy(codes, code_held, code_sem)
     code_copy.start()
     rows = held.shape[1]
@@ -247,8 +259,11 @@
         pltpu.make_async_copy(held.at[y], held.at[y], sem.at[y]).wait()
         total = jnp.dot(held[y], code_held[...], preferred_element_type=F32) * weight_scale[0]
         j = y ^ where[2]
-        place = 2 * (1 - j % 2) + 1 - j // 2
-        out[pl.ds(pl.multiple_of(place * rows, rows), rows), :] = total.astype(BF)
+        spot = pl.ds(pl.multiple_of((1 - j // 2) * rows, rows), rows)
+        for out, side in ((away, 1), (keep, 0)):
+            @pl.when(j % 2 == side)
+            def _():
+                out[spot, :] = total.astype(BF)
 
 
 def act_parts(where, weight_scale, codes, groups):
@@ -259,9 +274,9 @@
     smem = pl.BlockSpec(memory_space=pltpu.SMEM)
     return pl.pallas_call(
         act_kernel,
-        out_shape=jax.ShapeDtypeStruct((4 * rows, cols), BF),
+        out_shape=[jax.ShapeDtypeStruct((2 * rows, cols), BF)] * 2,
         in_specs=[smem, smem] + [anywhere] * (len(pieces) + 1),
-        out_specs=pl.BlockSpec(memory_space=pltpu.VMEM),
+        out_specs=[pl.BlockSpec(memory_space=pltpu.VMEM)] * 2,
         scratch_shapes=[
             pltpu.VMEM((4, rows, depth), BF),
             pltpu.VMEM((depth, cols), BF),
@@ -274,9 +289,9 @@
     )(where, weight_scale, codes, *pieces)
 
 
-def finish_kernel(parts, got, other, rotated, bound, signs, out):
+def finish_kernel(keep, got, other, rotated, bound, signs, out):
     rows = out.shape[0]
-    summed = parts[3 * rows:, :].astype(F32) + got[rows:, :].astype(F32) + other[...].astype(F32)
+    summed = keep[rows:, :].astype(F32) + got[rows:, :].astype(F32) + other[...].astype(F32)
     masked = jnp.where(jnp.abs(rotated[...].astype(F32)) <= bound[...], summed, 0.0)
     high = masked.astype(BF)
     low = (masked - high.astype(F32)).astype(BF)
@@ -287,7 +302,7 @@
         out[:, lo:lo + HB] = (turned * (HB ** -0.5)).astype(BF)
 
 
-def finish(parts, got, other, rotated, bound, signs):
+def finish(keep, got, other, rotated, bound, signs):
     vmem = pl.BlockSpec(memory_space=pltpu.VMEM)
     return pl.pallas_call(
         finish_kernel,
@@ -296,7 +311,7 @@
         out_specs=vmem,
         compiler_params=pltpu.CompilerParams(vmem_limit_bytes=SMALL),
         name="finish",
-    )(parts, got, other, rotated, bound, signs)
+    )(keep, got, other, rotated, bound, signs)
 
 
 def hadamard_signs(length):
@@ -317,40 +332,33 @@
 
     bound = clip_level[:, None]
     clipped = clip_turned(rotated, bound)
-    other = lax.ppermute(clipped, ("dp", "row"), PARTNER)
-
     tie = lax.optimization_barrier
     first_core = row % 2 == 0
-    both = None
+    clips = [clipped, lax.ppermute(clipped, "row", CORE)]
+    for pairs in (PARTNER, PARTNER_SIBLING):
+        clips.append(lax.ppermute(clipped, ("dp", "row"), pairs))
 
     def before_second(*arrays):
-        nonlocal other, both
-        *arrays, other = tie((*arrays, other))
-        both = lax.ppermute(jnp.concatenate([clipped, other], axis=0), "row", CORE)
-        return arrays
-
-    def before_third(*arrays):
-        nonlocal both
-        *arrays, both = tie((*arrays, both))
-        return arrays
+        arrays = tie((*arrays, *clips[1:]))
+        clips[1:] = arrays[-3:]
+        return arrays[:-3]
 
     own = move(cotangent, (0, 0), (0, 0), True)
-    groups = gather(own, first_core, before_second, before_third)
-    clips = [clipped, both, other]
+    groups = gather(own, first_core, before_second)
     mine0 = weight_term(where, groups[0], clips, grad_norm)
     theirs0 = lax.ppermute(mine0, "dp", DP)
     mine0, groups[0][0] = tie((mine0, groups[0][0]))
     rows = clipped.shape[1]
-    parts = act_parts(where, weight_scale, codes, groups)
-    parts, groups[1][0] = tie((parts, groups[1][0]))
+    away, keep = act_parts(where, weight_scale, codes, groups)
+    away, keep, groups[1][0] = tie((away, keep, groups[1][0]))
     mine1 = weight_term(where, groups[1], clips, grad_norm)
-    got = lax.ppermute(parts[:2 * rows], "row", CORE)
+    got = lax.ppermute(away, "row", CORE)
+    outward = (keep[:rows].astype(F32) + got[:rows].astype(F32)).astype(BF)
     mine1, theirs0 = tie((mine1, theirs0))
     theirs1 = lax.ppermute(mine1, "dp", DP)
-    outward = (parts[2 * rows:3 * rows].astype(F32) + got[:rows].astype(F32)).astype(BF)
     inward = lax.ppermute(outward, ("dp", "row"), PARTNER)
     weight_grad = sum_terms(0, mine0, theirs0, None, codes.shape[0])
-    input_grad = finish(parts, got, inward, rotated, bound, hadamard_signs(HB))
+    input_grad = finish(keep, got, inward, rotated, bound, hadamard_signs(HB))
     input_grad, theirs1 = tie((input_grad, theirs1))
     weight_grad = sum_terms(WIDTHS[0], mine1, theirs1, weight_grad, codes.shape[0])
     return (input_grad, weight_grad)

time: 149 us -> 146 us (0.980); the launches traced: 149 us -> 144 us
  starting transfers between devices: 72.1 us -> 62.8 us
  waiting for transfers between devices: 28.8 us -> 35.9 us
  Pallas kernels: 34.1 us -> 32.6 us
  local copies, waits for them, and re-layouts: 8.84 us -> 7.34 us
    ppermute x24 -> x22, starting transfers between devices: 45 us -> 38.6 us  [move(): lax.ppermute(value, ('dp', 'col', 'row'), pairs_for((core0, core1), swap))]
    ppermute x3 -> x4, waiting for transfers between devices: 5.4 us -> 9.66 us  [the longest x2 9.66 us: body(): clips.append(lax.ppermute(clipped, ('dp', 'row'), pairs))]
    ppermute x1, waiting for transfers between devices: 3.41 us -> 7.27 us  [body(): theirs1 = lax.ppermute(mine1, 'dp', DP)]
    ppermute x24 -> x22, waiting for transfers between devices: 8.48 us -> 5.96 us  [move(): lax.ppermute(value, ('dp', 'col', 'row'), pairs_for((core0, core1), swap))]
    slice x1 -> x0, local copies, waits for them, and re-layouts: 2.51 us -> none  [body(): got = lax.ppermute(parts[:2 * rows], 'row', CORE)]
    select_n x2, other arithmetic: 1.15 us -> 2.8 us  [gather(): jnp.where(first_core, f, part)]
    ppermute x1, waiting for transfers between devices: 11.5 us -> 13 us  [body(): inward = lax.ppermute(outward, ('dp', 'row'), PARTNER)]
    ppermute x3 -> x4, starting transfers between devices: 22.3 us -> 20.9 us  [the longest x2 10.4 us: body(): clips.append(lax.ppermute(clipped, ('dp', 'row'), pairs))]
  transfers between devices with their start and end apart: 30 -> 29, of which waited for: 12 -> 9; matrix products, arithmetic and copies ran while one was open for 5% -> 4% of each run, Pallas kernels for 22% -> 21%
where the time goes in v3:
time: 146 us; the launch traced here: 144 us
  starting transfers between devices  62.8 us (43%)
  waiting for transfers between devices  35.9 us (25%)
  Pallas kernels  32.6 us (22%)
  local copies, waits for them, and re-layouts  7.34 us (5%)
  other arithmetic  3.61 us (2%)
  between operations  1.91 us (1%)
    ppermute x22, starting transfers between devices, move(): lax.ppermute(value, ('dp', 'col', 'row'), pairs_for((core0, core1), swap))  38.6 us
    pallas_call x2, Pallas kernels, weight_term(): pl.pallas_call(functools.partial(weight_kernel, scale), out_shape=jax.Sha...  14 us
    pallas_call x1, Pallas kernels, act_parts(): pl.pallas_call(act_kernel, out_shape=[jax.ShapeDtypeStruct((2 * rows, col...  13.1 us
    ppermute x1, waiting for transfers between devices, body(): inward = lax.ppermute(outward, ('dp', 'row'), PARTNER)  13 us
    ppermute x2, starting transfers between devices, body(): clips.append(lax.ppermute(clipped, ('dp', 'row'), pairs))  10.4 us
    ppermute x2, waiting for transfers between devices, body(): clips.append(lax.ppermute(clipped, ('dp', 'row'), pairs))  9.66 us
    ppermute x1, waiting for transfers between devices, body(): theirs1 = lax.ppermute(mine1, 'dp', DP)  7.27 us
    ppermute x1, starting transfers between devices, body(): got = lax.ppermute(away, 'row', CORE)  7.24 us
  transfers between devices with their start and end apart: 29, of which 9 were waited for; matrix products, arithmetic and copies ran while one was open for 4% of the time, Pallas kernels for 21%

profile of v3, /device:TPU:1, one launch (start us, length us, event | category | flops | bytes accessed | tf_op | source)
XLA Modules:
  0.0 144.2 jit_solution(16743510838944312507)
XLA Ops:
  0.6 1.6 %collective-permute-start = (bf16[64,1792]{1,0:T(8,128)(2,1)}, bf16[64,1792]{1,0:T(8,128)(2,1)S(1)}, u32[]{:S(2)}, u32[]{:S(2)}) collective-permute-start(bf16[64,1792]{1,0:T(8,128)(2,1)} %param.5), channel_id=1, source_target_pairs={{0,0},{1,1},{2,130},{3,131},{4,4},{5,5},{6,134},{7,135},{8,8},{9,9... | collective-permute-start | bytes 688136 | tf_op jit(solution)/shard_map/ppermute | solution.py:58
  2.2 0.8 copy.8.bound
  3.1 1.1 copy-done.6
  4.1 0.4 clip_turned.1.refs_10_
  4.6 3.3 %collective-permute-start.6 = (bf16[640,512]{1,0:T(8,128)(2,1)S(1)}, bf16[640,512]{1,0:T(8,128)(2,1)S(1)}, u32[]{:S(2)}, u32[]{:S(2)}) collective-permute-start(bf16[640,512]{1,0:T(8,128)(2,1)S(1)} %clip_turned.1.refs_10_), channel_id=1, source_target_pairs={{0,1},{1,0},{2,3},{3,2},{4,5},{5,4},{6,7},{7,6},{8,9},{9,8},{10,11... | collective-permute-start | bytes 1966088 | tf_op jit(solution)/shard_map/ppermute | solution.py:337
  7.9 1.9 %collective-permute-start.7 = (bf16[640,512]{1,0:T(8,128)(2,1)S(1)}, bf16[640,512]{1,0:T(8,128)(2,1)S(1)}, u32[]{:S(2)}, u32[]{:S(2)}) collective-permute-start(bf16[640,512]{1,0:T(8,128)(2,1)S(1)} %clip_turned.1.refs_10_), channel_id=1, source_target_pairs={{0,130},{1,131},{2,128},{3,129},{128,2},{129,3},{130,0},{131,1},{4... | collective-permute-start | bytes 1966088 | tf_op jit(solution)/shard_map/ppermute | solution.py:339
  9.8 3.1 %collective-permute-start.1 = (bf16[64,1792]{1,0:T(8,128)(2,1)S(1)}, bf16[64,1792]{1,0:T(8,128)(2,1)S(1)}, u32[]{:S(2)}, u32[]{:S(2)}) collective-permute-start(bf16[64,1792]{1,0:T(8,128)(2,1)S(1)} %collective-permute-done.own), channel_id=1, source_target_pairs={{0,8},{1,65},{2,10},{3,67},{4,12},{5,69},{6,14},{7,71},{8,16},{9,7... | collective-permute-start | bytes 688136 | tf_op jit(solution)/shard_map/ppermute | solution.py:58
  13.3 2.3 %collective-permute-start.3 = (bf16[64,1792]{1,0:T(8,128)(2,1)S(1)}, bf16[64,1792]{1,0:T(8,128)(2,1)S(1)}, u32[]{:S(2)}, u32[]{:S(2)}) collective-permute-start(bf16[64,1792]{1,0:T(8,128)(2,1)S(1)} %collective-permute-done.own), channel_id=1, source_target_pairs={{0,28},{1,97},{2,30},{3,99},{4,0},{5,101},{6,2},{7,103},{8,4},{9,1... | collective-permute-start | bytes 688136 | tf_op jit(solution)/shard_map/ppermute | solution.py:58
  15.6 0.7 collective-permute-done.1.c
  16.4 8.5 %collective-permute-start.8 = (bf16[640,512]{1,0:T(8,128)(2,1)S(1)}, bf16[640,512]{1,0:T(8,128)(2,1)S(1)}, u32[]{:S(2)}, u32[]{:S(2)}) collective-permute-start(bf16[640,512]{1,0:T(8,128)(2,1)S(1)} %clip_turned.1.refs_10_), channel_id=1, source_target_pairs={{0,131},{1,130},{2,129},{3,128},{128,3},{129,2},{130,1},{131,0},{4... | collective-permute-start | bytes 1966088 | tf_op jit(solution)/shard_map/ppermute | solution.py:339
  25.0 0.7 collective-permute-start.4
  25.7 0.7 collective-permute-start.5
  26.4 2.7 %collective-permute-start.9 = (bf16[256,896]{1,0:T(8,128)(2,1)S(1)}, bf16[256,896]{1,0:T(8,128)(2,1)}, u32[]{:S(2)}, u32[]{:S(2)}) collective-permute-start(bf16[256,896]{1,0:T(8,128)(2,1)S(1)} %get-tuple-element.35.refs_0_), channel_id=1, source_target_pairs={{0,32},{1,5},{2,34},{3,7},{4,36},{5,9},{6,38},{7,11},{8,40},{9,13}... | collective-permute-start | bytes 1376264 | tf_op jit(solution)/shard_map/ppermute | solution.py:58
  29.2 1.2 collective-permute-start.10
  30.4 9.7 %collective-permute-done.8.refs_13_ = bf16[640,512]{1,0:T(8,128)(2,1)S(1)} collective-permute-done((bf16[640,512]{1,0:T(8,128)(2,1)S(1)}, bf16[640,512]{1,0:T(8,128)(2,1)S(1)}, u32[]{:S(2)}, u32[]{:S(2)}) %collective-permute-start.8) | collective-permute-done | bytes 655392 | tf_op jit(solution)/shard_map/ppermute | solution.py:339
  40.1 0.8 copy-done.10
  40.9 1.7 %collective-permute-start.17 = (bf16[256,896]{1,0:T(8,128)(2,1)S(1)}, bf16[256,896]{1,0:T(8,128)(2,1)}, u32[]{:S(2)}, u32[]{:S(2)}) collective-permute-start(bf16[256,896]{1,0:T(8,128)(2,1)S(1)} %get-tuple-element.42.refs_10_.refs_0_), channel_id=1, source_target_pairs={{0,32},{1,5},{2,34},{3,7},{4,36},{5,9},{6,38},{7,11},{8,40},{9,13}... | collective-permute-start | bytes 1376264 | tf_op jit(solution)/shard_map/ppermute | solution.py:58
  42.5 3.0 %collective-permute-start.18 = (bf16[256,896]{1,0:T(8,128)(2,1)S(1)}, bf16[256,896]{1,0:T(8,128)(2,1)}, u32[]{:S(2)}, u32[]{:S(2)}) collective-permute-start(bf16[256,896]{1,0:T(8,128)(2,1)S(1)} %get-tuple-element.42.refs_10_.refs_0_), channel_id=1, source_target_pairs={{0,96},{1,29},{2,98},{3,31},{4,100},{5,1},{6,102},{7,3},{8,104},{9... | collective-permute-start | bytes 1376264 | tf_op jit(solution)/shard_map/ppermute | solution.py:58
  45.5 0.5 collective-permute-start.11
  46.0 4.1 %collective-permute-start.12 = (bf16[256,896]{1,0:T(8,128)(2,1)}, bf16[256,896]{1,0:T(8,128)(2,1)}, u32[]{:S(2)}, u32[]{:S(2)}) collective-permute-start(bf16[256,896]{1,0:T(8,128)(2,1)} %collective-permute-done.10.refs_3_), channel_id=1, source_target_pairs={{1,29},{3,31},{5,1},{7,3},{9,5},{11,7},{13,9},{15,11},{17,13},{19,... | collective-permute-start | bytes 1376264 | tf_op jit(solution)/shard_map/ppermute | solution.py:58
  50.1 1.4 collective-permute-done.17.refs_12_.refs_2_
  51.5 5.0 %collective-permute-start.20 = (bf16[256,896]{1,0:T(8,128)(2,1)}, bf16[256,896]{1,0:T(8,128)(2,1)}, u32[]{:S(2)}, u32[]{:S(2)}) collective-permute-start(bf16[256,896]{1,0:T(8,128)(2,1)} %collective-permute-done.18.refs_13_.refs_3_), channel_id=1, source_target_pairs={{1,29},{3,31},{5,1},{7,3},{9,5},{11,7},{13,9},{15,11},{17,13},{19,... | collective-permute-start | bytes 1376264 | tf_op jit(solution)/shard_map/ppermute | solution.py:58
  56.5 1.0 copy-done.11
  57.6 1.6 %broadcast_select_fusion.2 = (bf16[256,896]{1,0:T(8,128)(2,1)S(1)}, bf16[256,896]{1,0:T(8,128)(2,1)S(1)}) fusion(bf16[256,896]{1,0:T(8,128)(2,1)S(1)} %get-tuple-element.31.refs_1_, bf16[256,896]{1,0:T(8,128)(2,1)} %collective-permute-done.12.refs_5_, pred[]{:T(512)S(6)} %eq.6, bf16[256,896]{1,0:T(8,128)(2,1)} %collective-permute-done.11.refs_4_), kind=kLoop, calls=%fused_computation.3 | loop fusion | flops 458752 | bytes 2293761 | tf_op jit(solution)/shard_map/jit(_where)/select_n | solution.py:110
  59.3 2.7 %collective-permute-start.14 = (bf16[256,896]{1,0:T(8,128)(2,1)S(1)}, bf16[256,896]{1,0:T(8,128)(2,1)S(1)}, u32[]{:S(2)}, u32[]{:S(2)}) collective-permute-start(bf16[256,896]{1,0:T(8,128)(2,1)S(1)} %get-tuple-element.50), channel_id=1, source_target_pairs={{0,96},{1,29},{2,98},{3,31},{4,100},{5,1},{6,102},{7,3},{8,104},{9... | collective-permute-start | bytes 1376264 | tf_op jit(solution)/shard_map/ppermute | solution.py:58
  62.2 1.2 broadcast_select_fusion
  63.5 2.4 %collective-permute-start.21 = (bf16[256,896]{1,0:T(8,128)(2,1)S(1)}, bf16[256,896]{1,0:T(8,128)(2,1)S(1)}, u32[]{:S(2)}, u32[]{:S(2)}) collective-permute-start(bf16[256,896]{1,0:T(8,128)(2,1)S(1)} %get-tuple-element.49), channel_id=1, source_target_pairs={{0,32},{1,5},{2,34},{3,7},{4,36},{5,9},{6,38},{7,11},{8,40},{9,13}... | collective-permute-start | bytes 1376264 | tf_op jit(solution)/shard_map/ppermute | solution.py:58
  65.8 1.4 collective-permute-start.22
  67.2 0.9 collective-permute-done.13.refs_6_
  68.7 2.3 %collective-permute-start.16 = (bf16[128,896]{1,0:T(8,128)(2,1)S(1)}, bf16[128,896]{1,0:T(8,128)(2,1)S(1)}, u32[]{:S(2)}, u32[]{:S(2)}) collective-permute-start(bf16[128,896]{1,0:T(8,128)(2,1)S(1)} %slice.25), channel_id=1, source_target_pairs={{0,96},{1,29},{2,98},{3,31},{4,100},{5,1},{6,102},{7,3},{8,104},{9... | collective-permute-start | bytes 688136 | tf_op jit(solution)/shard_map/ppermute | solution.py:58
  71.0 2.3 %collective-permute-done.21.refs_16_.refs_6_ = bf16[256,896]{1,0:T(8,128)(2,1)S(1)} collective-permute-done((bf16[256,896]{1,0:T(8,128)(2,1)S(1)}, bf16[256,896]{1,0:T(8,128)(2,1)S(1)}, u32[]{:S(2)}, u32[]{:S(2)}) %collective-permute-start.21) | collective-permute-done | bytes 458784 | tf_op jit(solution)/shard_map/ppermute | solution.py:58
  73.3 0.7 slice.26
  74.2 0.8 slice.27
  75.0 2.5 %collective-permute-start.24 = (bf16[128,896]{1,0:T(8,128)(2,1)}, bf16[128,896]{1,0:T(8,128)(2,1)}, u32[]{:S(2)}, u32[]{:S(2)}) collective-permute-start(bf16[128,896]{1,0:T(8,128)(2,1)} %slice.27), channel_id=1, source_target_pairs={{0,96},{1,29},{2,98},{3,31},{4,100},{5,1},{6,102},{7,3},{8,104},{9... | collective-permute-start | bytes 688136 | tf_op jit(solution)/shard_map/ppermute | solution.py:58
  77.5 0.6 pad_add_fusion.where
  78.1 0.7 copy-done.20
  78.8 0.7 copy-done.21
  79.5 7.0 %weight_term.2.mine = bf16[640,896]{1,0:T(8,128)(2,1)} custom-call(s32[3]{0:T(128)} %pad_add_fusion.where, bf16[256,896]{1,0:T(8,128)(2,1)} %copy-done.9, bf16[256,896]{1,0:T(8,128)(2,1)} %copy-done.4, bf16[256,896]{1,0:T(8,128)(2,1)} %collective-permute-done.9.refs_2_, bf16[256,896]{1,0:T(8,128)(2,1)} %collective-permute-done.10.refs_3_, ...), custom_call_target="tpu_custom_call" | custom-call | flops 1 | bytes 1 | tf_op jit(solution)/shard_map/weight_term/pallas_call | solution.py:191
  87.4 0.7 copy-done.19
  88.0 13.1 %act_parts.1 = (bf16[1024,640]{1,0:T(8,128)(2,1)}, bf16[1024,640]{1,0:T(8,128)(2,1)}) custom-call(s32[3]{0:T(128)} %pad_add_fusion.where, f32[1]{0:T(128)S(6)} %copy.11.weight_scale, bf16[1792,640]{1,0:T(8,128)(2,1)} %codes.1, bf16[256,896]{1,0:T(8,128)(2,1)} %copy-done.9, bf16[256,896]{1,0:T(8,128)(2,1)} %copy-done.4, ...), custom_call_target="tpu_custom_call" | custom-call | flops 1 | bytes 1 | tf_op jit(solution)/shard_map/act_parts/pallas_call | solution.py:275
  101.1 7.2 %collective-permute-start.25 = (bf16[1024,640]{1,0:T(8,128)(2,1)}, bf16[1024,640]{1,0:T(8,128)(2,1)S(1)}, u32[]{:S(2)}, u32[]{:S(2)}) collective-permute-start(bf16[1024,640]{1,0:T(8,128)(2,1)} %get-tuple-element.41), channel_id=1, source_target_pairs={{0,1},{1,0},{2,3},{3,2},{4,5},{5,4},{6,7},{7,6},{8,9},{9,8},{10,11... | collective-permute-start | bytes 3932168 | tf_op jit(solution)/shard_map/ppermute | solution.py:355
  108.4 7.0 %weight_term.3.mine = bf16[640,896]{1,0:T(8,128)(2,1)} custom-call(s32[3]{0:T(128)} %pad_add_fusion.where, bf16[256,896]{1,0:T(8,128)(2,1)} %copy-done.8, bf16[256,896]{1,0:T(8,128)(2,1)} %copy-done.3, bf16[256,896]{1,0:T(8,128)(2,1)} %collective-permute-done.17.refs_12_.refs_2_, bf16[256,896]{1,0:T(8,128)(2,1)} %collective-permute-done.18.refs_13_.refs_3_, ...), custom_call_target="tpu_custom_call" | custom-call | flops 1 | bytes 1 | tf_op jit(solution)/shard_map/weight_term/pallas_call | solution.py:191
  115.7 3.0 %collective-permute-start.26 = (bf16[512,640]{1,0:T(8,128)(2,1)S(1)}, bf16[512,640]{1,0:T(8,128)(2,1)S(1)}, u32[]{:S(2)}, u32[]{:S(2)}) collective-permute-start(bf16[512,640]{1,0:T(8,128)(2,1)S(1)} %add_convert_fusion), channel_id=1, source_target_pairs={{0,130},{1,131},{2,128},{3,129},{128,2},{129,3},{130,0},{131,1},{4... | collective-permute-start | bytes 1966088 | tf_op jit(solution)/shard_map/ppermute | solution.py:359
  118.8 1.6 %sum_terms.2.refs_0_ = f32[1792,640]{1,0:T(8,128)} custom-call(bf16[640,896]{1,0:T(8,128)(2,1)S(1)} %copy-done.1, bf16[640,896]{1,0:T(8,128)(2,1)S(1)} %collective-permute-done.27.theirs), custom_call_target="tpu_custom_call" | custom-call | tf_op jit(solution)/shard_map/sum_terms/pallas_call | solution.py:227
  120.4 13.0 %collective-permute-done.26.other = bf16[512,640]{1,0:T(8,128)(2,1)S(1)} collective-permute-done((bf16[512,640]{1,0:T(8,128)(2,1)S(1)}, bf16[512,640]{1,0:T(8,128)(2,1)S(1)}, u32[]{:S(2)}, u32[]{:S(2)}) %collective-permute-start.26) | collective-permute-done | bytes 655392 | tf_op jit(solution)/shard_map/ppermute | solution.py:359
  133.4 1.7 %finish.1 = bf16[512,640]{1,0:T(8,128)(2,1)} custom-call(bf16[1024,640]{1,0:T(8,128)(2,1)S(1)} %copy-done.5, bf16[1024,640]{1,0:T(8,128)(2,1)S(1)} %collective-permute-done.25.got, bf16[512,640]{1,0:T(8,128)(2,1)S(1)} %collective-permute-done.26.other, bf16[512,640]{1,0:T(8,128)(2,1)S(1)} %copy-done.7, f32[512,1]{1,0:T(8,128)S(1)} %copy.8.bound, ...), custom_call_target="tpu_custom_call" | custom-call | tf_op jit(solution)/shard_map/finish/pallas_call | solution.py:307
  135.1 7.3 %collective-permute-done.28.theirs = bf16[640,896]{1,0:T(8,128)(2,1)S(1)} collective-permute-done((bf16[640,896]{1,0:T(8,128)(2,1)}, bf16[640,896]{1,0:T(8,128)(2,1)S(1)}, u32[]{:S(2)}, u32[]{:S(2)}) %collective-permute-start.28) | collective-permute-done | bytes 1146912 | tf_op jit(solution)/shard_map/ppermute | solution.py:358
  142.4 1.6 %sum_terms.3 = f32[1792,640]{1,0:T(8,128)} custom-call(bf16[640,896]{1,0:T(8,128)(2,1)S(1)} %copy-done.2, bf16[640,896]{1,0:T(8,128)(2,1)S(1)} %collective-permute-done.28.theirs, f32[1792,640]{1,0:T(8,128)} %sum_terms.2.refs_0_), custom_call_target="tpu_custom_call", output_to_operand_aliasing={{}: (2, {})} | custom-call | tf_op jit(solution)/shard_map/sum_terms/pallas_call | solution.py:227
  (73 shorter events, 2.2 us)
Async XLA Ops:
  0.6 9.2 %collective-permute-start = (bf16[64,1792]{1,0:T(8,128)(2,1)}, bf16[64,1792]{1,0:T(8,128)(2,1)S(1)}, u32[]{:S(2)}, u32[]{:S(2)}) collective-permute-start(bf16[64,1792]{1,0:T(8,128)(2,1)} %param.5), channel_id=1, source_target_pairs={{0,0},{1,1},{2,130},{3,131},{4,4},{5,5},{6,134},{7,135},{8,8},{9,9... | collective-permute-start | bytes 688136 | tf_op jit(solution)/shard_map/ppermute | solution.py:58
  3.1 1.1 copy-start.6
  4.6 54.6 %copy-start = (bf16[640,512]{1,0:T(8,128)(2,1)}, bf16[640,512]{1,0:T(8,128)(2,1)S(1)}, u32[]{:S(2)}) copy-start(bf16[640,512]{1,0:T(8,128)(2,1)S(1)} %clip_turned.1.refs_10_) | copy-start | bytes 1966084
  4.6 21.8 %collective-permute-start.6 = (bf16[640,512]{1,0:T(8,128)(2,1)S(1)}, bf16[640,512]{1,0:T(8,128)(2,1)S(1)}, u32[]{:S(2)}, u32[]{:S(2)}) collective-permute-start(bf16[640,512]{1,0:T(8,128)(2,1)S(1)} %clip_turned.1.refs_10_), channel_id=1, source_target_pairs={{0,1},{1,0},{2,3},{3,2},{4,5},{5,4},{6,7},{7,6},{8,9},{9,8},{10,11... | collective-permute-start | bytes 1966088 | tf_op jit(solution)/shard_map/ppermute | solution.py:337
  7.9 21.2 %collective-permute-start.7 = (bf16[640,512]{1,0:T(8,128)(2,1)S(1)}, bf16[640,512]{1,0:T(8,128)(2,1)S(1)}, u32[]{:S(2)}, u32[]{:S(2)}) collective-permute-start(bf16[640,512]{1,0:T(8,128)(2,1)S(1)} %clip_turned.1.refs_10_), channel_id=1, source_target_pairs={{0,130},{1,131},{2,128},{3,129},{128,2},{129,3},{130,0},{131,1},{4... | collective-permute-start | bytes 1966088 | tf_op jit(solution)/shard_map/ppermute | solution.py:339
  9.8 6.5 %collective-permute-start.1 = (bf16[64,1792]{1,0:T(8,128)(2,1)S(1)}, bf16[64,1792]{1,0:T(8,128)(2,1)S(1)}, u32[]{:S(2)}, u32[]{:S(2)}) collective-permute-start(bf16[64,1792]{1,0:T(8,128)(2,1)S(1)} %collective-permute-done.own), channel_id=1, source_target_pairs={{0,8},{1,65},{2,10},{3,67},{4,12},{5,69},{6,14},{7,71},{8,16},{9,7... | collective-permute-start | bytes 688136 | tf_op jit(solution)/shard_map/ppermute | solution.py:58
  12.9 11.9 %collective-permute-start.2 = (bf16[64,1792]{1,0:T(8,128)(2,1)S(1)}, bf16[64,1792]{1,0:T(8,128)(2,1)S(1)}, u32[]{:S(2)}, u32[]{:S(2)}) collective-permute-start(bf16[64,1792]{1,0:T(8,128)(2,1)S(1)} %collective-permute-done.own), channel_id=1, source_target_pairs={{0,4},{1,33},{2,6},{3,35},{4,8},{5,37},{6,10},{7,39},{8,12},{9,41}... | collective-permute-start | bytes 688136 | tf_op jit(solution)/shard_map/ppermute | solution.py:58
  13.3 11.5 %collective-permute-start.3 = (bf16[64,1792]{1,0:T(8,128)(2,1)S(1)}, bf16[64,1792]{1,0:T(8,128)(2,1)S(1)}, u32[]{:S(2)}, u32[]{:S(2)}) collective-permute-start(bf16[64,1792]{1,0:T(8,128)(2,1)S(1)} %collective-permute-done.own), channel_id=1, source_target_pairs={{0,28},{1,97},{2,30},{3,99},{4,0},{5,101},{6,2},{7,103},{8,4},{9,1... | collective-permute-start | bytes 688136 | tf_op jit(solution)/shard_map/ppermute | solution.py:58
  16.4 23.7 %collective-permute-start.8 = (bf16[640,512]{1,0:T(8,128)(2,1)S(1)}, bf16[640,512]{1,0:T(8,128)(2,1)S(1)}, u32[]{:S(2)}, u32[]{:S(2)}) collective-permute-start(bf16[640,512]{1,0:T(8,128)(2,1)S(1)} %clip_turned.1.refs_10_), channel_id=1, source_target_pairs={{0,131},{1,130},{2,129},{3,128},{128,3},{129,2},{130,1},{131,0},{4... | collective-permute-start | bytes 1966088 | tf_op jit(solution)/shard_map/ppermute | solution.py:339
  25.0 34.2 %copy-start.8 = (bf16[256,896]{1,0:T(8,128)(2,1)}, bf16[256,896]{1,0:T(8,128)(2,1)S(1)}, u32[]{:S(2)}) copy-start(bf16[256,896]{1,0:T(8,128)(2,1)S(1)} %get-tuple-element.42.refs_10_.refs_0_) | copy-start | bytes 1376260
  25.0 34.2 %copy-start.9 = (bf16[256,896]{1,0:T(8,128)(2,1)}, bf16[256,896]{1,0:T(8,128)(2,1)S(1)}, u32[]{:S(2)}) copy-start(bf16[256,896]{1,0:T(8,128)(2,1)S(1)} %get-tuple-element.35.refs_0_) | copy-start | bytes 1376260
  25.0 15.1 %collective-permute-start.4 = (bf16[128,1792]{1,0:T(8,128)(2,1)S(1)}, bf16[128,1792]{1,0:T(8,128)(2,1)S(1)}, u32[]{:S(2)}, u32[]{:S(2)}) collective-permute-start(bf16[128,1792]{1,0:T(8,128)(2,1)S(1)} %get-tuple-element.27), channel_id=1, source_target_pairs={{0,8},{2,10},{4,12},{6,14},{8,16},{10,18},{12,20},{14,22},{16,24},... | collective-permute-start | bytes 1376264 | tf_op jit(solution)/shard_map/ppermute | solution.py:58
  25.7 14.4 %collective-permute-start.5 = (bf16[128,1792]{1,0:T(8,128)(2,1)S(1)}, bf16[128,1792]{1,0:T(8,128)(2,1)S(1)}, u32[]{:S(2)}, u32[]{:S(2)}) collective-permute-start(bf16[128,1792]{1,0:T(8,128)(2,1)S(1)} %get-tuple-element.28), channel_id=1, source_target_pairs={{0,24},{2,26},{4,28},{6,30},{8,0},{10,2},{12,4},{14,6},{16,8},{18,... | collective-permute-start | bytes 1376264 | tf_op jit(solution)/shard_map/ppermute | solution.py:58
  26.4 25.1 %copy-start.16 = (bf16[640,512]{1,0:T(8,128)(2,1)}, bf16[640,512]{1,0:T(8,128)(2,1)S(1)}, u32[]{:S(2)}) copy-start(bf16[640,512]{1,0:T(8,128)(2,1)S(1)} %collective-permute-done.6.refs_11_) | copy-start | bytes 1966084
  26.4 19.1 %collective-permute-start.9 = (bf16[256,896]{1,0:T(8,128)(2,1)S(1)}, bf16[256,896]{1,0:T(8,128)(2,1)}, u32[]{:S(2)}, u32[]{:S(2)}) collective-permute-start(bf16[256,896]{1,0:T(8,128)(2,1)S(1)} %get-tuple-element.35.refs_0_), channel_id=1, source_target_pairs={{0,32},{1,5},{2,34},{3,7},{4,36},{5,9},{6,38},{7,11},{8,40},{9,13}... | collective-permute-start | bytes 1376264 | tf_op jit(solution)/shard_map/ppermute | solution.py:58
  29.2 27.3 %copy-start.17 = (bf16[640,512]{1,0:T(8,128)(2,1)}, bf16[640,512]{1,0:T(8,128)(2,1)S(1)}, u32[]{:S(2)}) copy-start(bf16[640,512]{1,0:T(8,128)(2,1)S(1)} %collective-permute-done.7.refs_12_) | copy-start | bytes 1966084
  29.2 16.9 %collective-permute-start.10 = (bf16[256,896]{1,0:T(8,128)(2,1)S(1)}, bf16[256,896]{1,0:T(8,128)(2,1)}, u32[]{:S(2)}, u32[]{:S(2)}) collective-permute-start(bf16[256,896]{1,0:T(8,128)(2,1)S(1)} %get-tuple-element.35.refs_0_), channel_id=1, source_target_pairs={{0,96},{1,29},{2,98},{3,31},{4,100},{5,1},{6,102},{7,3},{8,104},{9... | collective-permute-start | bytes 1376264 | tf_op jit(solution)/shard_map/ppermute | solution.py:58
  40.0 16.4 %copy-start.18 = (bf16[640,512]{1,0:T(8,128)(2,1)}, bf16[640,512]{1,0:T(8,128)(2,1)S(1)}, u32[]{:S(2)}) copy-start(bf16[640,512]{1,0:T(8,128)(2,1)S(1)} %collective-permute-done.8.refs_13_) | copy-start | bytes 1966084
  40.1 0.8 copy-start.10
  40.9 10.6 %collective-permute-start.17 = (bf16[256,896]{1,0:T(8,128)(2,1)S(1)}, bf16[256,896]{1,0:T(8,128)(2,1)}, u32[]{:S(2)}, u32[]{:S(2)}) collective-permute-start(bf16[256,896]{1,0:T(8,128)(2,1)S(1)} %get-tuple-element.42.refs_10_.refs_0_), channel_id=1, source_target_pairs={{0,32},{1,5},{2,34},{3,7},{4,36},{5,9},{6,38},{7,11},{8,40},{9,13}... | collective-permute-start | bytes 1376264 | tf_op jit(solution)/shard_map/ppermute | solution.py:58
  42.5 9.0 %collective-permute-start.18 = (bf16[256,896]{1,0:T(8,128)(2,1)S(1)}, bf16[256,896]{1,0:T(8,128)(2,1)}, u32[]{:S(2)}, u32[]{:S(2)}) collective-permute-start(bf16[256,896]{1,0:T(8,128)(2,1)S(1)} %get-tuple-element.42.refs_10_.refs_0_), channel_id=1, source_target_pairs={{0,96},{1,29},{2,98},{3,31},{4,100},{5,1},{6,102},{7,3},{8,104},{9... | collective-permute-start | bytes 1376264 | tf_op jit(solution)/shard_map/ppermute | solution.py:58
  45.5 12.1 %collective-permute-start.11 = (bf16[256,896]{1,0:T(8,128)(2,1)}, bf16[256,896]{1,0:T(8,128)(2,1)}, u32[]{:S(2)}, u32[]{:S(2)}) collective-permute-start(bf16[256,896]{1,0:T(8,128)(2,1)} %collective-permute-done.9.refs_2_), channel_id=1, source_target_pairs={{0,32},{1,5},{2,34},{3,7},{4,36},{5,9},{6,38},{7,11},{8,40},{9,13}... | collective-permute-start | bytes 1376264 | tf_op jit(solution)/shard_map/ppermute | solution.py:58
  46.0 11.6 %collective-permute-start.12 = (bf16[256,896]{1,0:T(8,128)(2,1)}, bf16[256,896]{1,0:T(8,128)(2,1)}, u32[]{:S(2)}, u32[]{:S(2)}) collective-permute-start(bf16[256,896]{1,0:T(8,128)(2,1)} %collective-permute-done.10.refs_3_), channel_id=1, source_target_pairs={{1,29},{3,31},{5,1},{7,3},{9,5},{11,7},{13,9},{15,11},{17,13},{19,... | collective-permute-start | bytes 1376264 | tf_op jit(solution)/shard_map/ppermute | solution.py:58
  51.5 10.5 %collective-permute-start.19 = (bf16[256,896]{1,0:T(8,128)(2,1)}, bf16[256,896]{1,0:T(8,128)(2,1)}, u32[]{:S(2)}, u32[]{:S(2)}) collective-permute-start(bf16[256,896]{1,0:T(8,128)(2,1)} %collective-permute-done.17.refs_12_.refs_2_), channel_id=1, source_target_pairs={{0,32},{1,5},{2,34},{3,7},{4,36},{5,9},{6,38},{7,11},{8,40},{9,13}... | collective-permute-start | bytes 1376264 | tf_op jit(solution)/shard_map/ppermute | solution.py:58
  51.5 10.7 %collective-permute-start.20 = (bf16[256,896]{1,0:T(8,128)(2,1)}, bf16[256,896]{1,0:T(8,128)(2,1)}, u32[]{:S(2)}, u32[]{:S(2)}) collective-permute-start(bf16[256,896]{1,0:T(8,128)(2,1)} %collective-permute-done.18.refs_13_.refs_3_), channel_id=1, source_target_pairs={{1,29},{3,31},{5,1},{7,3},{9,5},{11,7},{13,9},{15,11},{17,13},{19,... | collective-permute-start | bytes 1376264 | tf_op jit(solution)/shard_map/ppermute | solution.py:58
  56.5 1.0 copy-start.11
  57.6 5.8 %copy-start.3 = (bf16[256,896]{1,0:T(8,128)(2,1)}, bf16[256,896]{1,0:T(8,128)(2,1)S(1)}, u32[]{:S(2)}) copy-start(bf16[256,896]{1,0:T(8,128)(2,1)S(1)} %get-tuple-element.37.refs_11_.refs_1_) | copy-start | bytes 1376260
  57.6 5.8 %copy-start.4 = (bf16[256,896]{1,0:T(8,128)(2,1)}, bf16[256,896]{1,0:T(8,128)(2,1)S(1)}, u32[]{:S(2)}) copy-start(bf16[256,896]{1,0:T(8,128)(2,1)S(1)} %get-tuple-element.31.refs_1_) | copy-start | bytes 1376260
  59.2 8.9 %collective-permute-start.13 = (bf16[256,896]{1,0:T(8,128)(2,1)S(1)}, bf16[256,896]{1,0:T(8,128)(2,1)S(1)}, u32[]{:S(2)}, u32[]{:S(2)}) collective-permute-start(bf16[256,896]{1,0:T(8,128)(2,1)S(1)} %get-tuple-element.51), channel_id=1, source_target_pairs={{0,32},{1,5},{2,34},{3,7},{4,36},{5,9},{6,38},{7,11},{8,40},{9,13}... | collective-permute-start | bytes 1376264 | tf_op jit(solution)/shard_map/ppermute | solution.py:58
  59.3 9.4 %collective-permute-start.14 = (bf16[256,896]{1,0:T(8,128)(2,1)S(1)}, bf16[256,896]{1,0:T(8,128)(2,1)S(1)}, u32[]{:S(2)}, u32[]{:S(2)}) collective-permute-start(bf16[256,896]{1,0:T(8,128)(2,1)S(1)} %get-tuple-element.50), channel_id=1, source_target_pairs={{0,96},{1,29},{2,98},{3,31},{4,100},{5,1},{6,102},{7,3},{8,104},{9... | collective-permute-start | bytes 1376264 | tf_op jit(solution)/shard_map/ppermute | solution.py:58
  63.5 9.8 %collective-permute-start.21 = (bf16[256,896]{1,0:T(8,128)(2,1)S(1)}, bf16[256,896]{1,0:T(8,128)(2,1)S(1)}, u32[]{:S(2)}, u32[]{:S(2)}) collective-permute-start(bf16[256,896]{1,0:T(8,128)(2,1)S(1)} %get-tuple-element.49), channel_id=1, source_target_pairs={{0,32},{1,5},{2,34},{3,7},{4,36},{5,9},{6,38},{7,11},{8,40},{9,13}... | collective-permute-start | bytes 1376264 | tf_op jit(solution)/shard_map/ppermute | solution.py:58
  65.8 8.4 %collective-permute-start.22 = (bf16[256,896]{1,0:T(8,128)(2,1)S(1)}, bf16[256,896]{1,0:T(8,128)(2,1)S(1)}, u32[]{:S(2)}, u32[]{:S(2)}) collective-permute-start(bf16[256,896]{1,0:T(8,128)(2,1)S(1)} %get-tuple-element.48), channel_id=1, source_target_pairs={{0,96},{1,29},{2,98},{3,31},{4,100},{5,1},{6,102},{7,3},{8,104},{9... | collective-permute-start | bytes 1376264 | tf_op jit(solution)/shard_map/ppermute | solution.py:58
  68.1 9.9 %copy-start.13 = (bf16[256,896]{1,0:T(8,128)(2,1)}, bf16[256,896]{1,0:T(8,128)(2,1)S(1)}, u32[]{:S(2)}) copy-start(bf16[256,896]{1,0:T(8,128)(2,1)S(1)} %collective-permute-done.13.refs_6_) | copy-start | bytes 1376260
  68.2 9.9 %collective-permute-start.15 = (bf16[128,896]{1,0:T(8,128)(2,1)S(1)}, bf16[128,896]{1,0:T(8,128)(2,1)S(1)}, u32[]{:S(2)}, u32[]{:S(2)}) collective-permute-start(bf16[128,896]{1,0:T(8,128)(2,1)S(1)} %slice.24), channel_id=1, source_target_pairs={{0,32},{1,5},{2,34},{3,7},{4,36},{5,9},{6,38},{7,11},{8,40},{9,13}... | collective-permute-start | bytes 688136 | tf_op jit(solution)/shard_map/ppermute | solution.py:58
  68.7 9.4 %copy-start.15 = (bf16[256,896]{1,0:T(8,128)(2,1)}, bf16[256,896]{1,0:T(8,128)(2,1)S(1)}, u32[]{:S(2)}) copy-start(bf16[256,896]{1,0:T(8,128)(2,1)S(1)} %collective-permute-done.14.refs_7_) | copy-start | bytes 1376260
  68.7 9.4 %collective-permute-start.16 = (bf16[128,896]{1,0:T(8,128)(2,1)S(1)}, bf16[128,896]{1,0:T(8,128)(2,1)S(1)}, u32[]{:S(2)}, u32[]{:S(2)}) collective-permute-start(bf16[128,896]{1,0:T(8,128)(2,1)S(1)} %slice.25), channel_id=1, source_target_pairs={{0,96},{1,29},{2,98},{3,31},{4,100},{5,1},{6,102},{7,3},{8,104},{9... | collective-permute-start | bytes 688136 | tf_op jit(solution)/shard_map/ppermute | solution.py:58
  73.3 13.2 %copy-start.12 = (bf16[256,896]{1,0:T(8,128)(2,1)}, bf16[256,896]{1,0:T(8,128)(2,1)S(1)}, u32[]{:S(2)}) copy-start(bf16[256,896]{1,0:T(8,128)(2,1)S(1)} %collective-permute-done.21.refs_16_.refs_6_) | copy-start | bytes 1376260
  74.0 13.3 %collective-permute-start.23 = (bf16[128,896]{1,0:T(8,128)(2,1)}, bf16[128,896]{1,0:T(8,128)(2,1)S(1)}, u32[]{:S(2)}, u32[]{:S(2)}) collective-permute-start(bf16[128,896]{1,0:T(8,128)(2,1)} %slice.26), channel_id=1, source_target_pairs={{0,32},{1,5},{2,34},{3,7},{4,36},{5,9},{6,38},{7,11},{8,40},{9,13}... | collective-permute-start | bytes 688136 | tf_op jit(solution)/shard_map/ppermute | solution.py:58
  74.2 12.2 %copy-start.14 = (bf16[256,896]{1,0:T(8,128)(2,1)}, bf16[256,896]{1,0:T(8,128)(2,1)S(1)}, u32[]{:S(2)}) copy-start(bf16[256,896]{1,0:T(8,128)(2,1)S(1)} %collective-permute-done.22.refs_17_.refs_7_) | copy-start | bytes 1376260
  75.0 12.4 %collective-permute-start.24 = (bf16[128,896]{1,0:T(8,128)(2,1)}, bf16[128,896]{1,0:T(8,128)(2,1)}, u32[]{:S(2)}, u32[]{:S(2)}) collective-permute-start(bf16[128,896]{1,0:T(8,128)(2,1)} %slice.27), channel_id=1, source_target_pairs={{0,96},{1,29},{2,98},{3,31},{4,100},{5,1},{6,102},{7,3},{8,104},{9... | collective-permute-start | bytes 688136 | tf_op jit(solution)/shard_map/ppermute | solution.py:58
  86.5 28.9 %collective-permute-start.27 = (bf16[640,896]{1,0:T(8,128)(2,1)}, bf16[640,896]{1,0:T(8,128)(2,1)S(1)}, u32[]{:S(2)}, u32[]{:S(2)}) collective-permute-start(bf16[640,896]{1,0:T(8,128)(2,1)} %weight_term.2.mine), channel_id=1, source_target_pairs={{0,128},{128,0},{1,129},{129,1},{2,130},{130,2},{3,131},{131,3},{4... | collective-permute-start | bytes 3440648 | tf_op jit(solution)/shard_map/ppermute | solution.py:349
  101.1 14.4 %copy-start.5 = (bf16[1024,640]{1,0:T(8,128)(2,1)S(1)}, bf16[1024,640]{1,0:T(8,128)(2,1)}, u32[]{:S(2)}) copy-start(bf16[1024,640]{1,0:T(8,128)(2,1)} %get-tuple-element.40.keep) | copy-start | bytes 3932164
  101.1 14.4 %collective-permute-start.25 = (bf16[1024,640]{1,0:T(8,128)(2,1)}, bf16[1024,640]{1,0:T(8,128)(2,1)S(1)}, u32[]{:S(2)}, u32[]{:S(2)}) collective-permute-start(bf16[1024,640]{1,0:T(8,128)(2,1)} %get-tuple-element.41), channel_id=1, source_target_pairs={{0,1},{1,0},{2,3},{3,2},{4,5},{5,4},{6,7},{7,6},{8,9},{9,8},{10,11... | collective-permute-start | bytes 3932168 | tf_op jit(solution)/shard_map/ppermute | solution.py:355
  115.4 3.4 %copy-start.1 = (bf16[640,896]{1,0:T(8,128)(2,1)S(1)}, bf16[640,896]{1,0:T(8,128)(2,1)}, u32[]{:S(2)}) copy-start(bf16[640,896]{1,0:T(8,128)(2,1)} %weight_term.2.mine) | copy-start | bytes 3440644
  115.4 27.0 %collective-permute-start.28 = (bf16[640,896]{1,0:T(8,128)(2,1)}, bf16[640,896]{1,0:T(8,128)(2,1)S(1)}, u32[]{:S(2)}, u32[]{:S(2)}) collective-permute-start(bf16[640,896]{1,0:T(8,128)(2,1)} %weight_term.3.mine), channel_id=1, source_target_pairs={{0,128},{128,0},{1,129},{129,1},{2,130},{130,2},{3,131},{131,3},{4... | collective-permute-start | bytes 3440648 | tf_op jit(solution)/shard_map/ppermute | solution.py:358
  115.7 17.8 %collective-permute-start.26 = (bf16[512,640]{1,0:T(8,128)(2,1)S(1)}, bf16[512,640]{1,0:T(8,128)(2,1)S(1)}, u32[]{:S(2)}, u32[]{:S(2)}) collective-permute-start(bf16[512,640]{1,0:T(8,128)(2,1)S(1)} %add_convert_fusion), channel_id=1, source_target_pairs={{0,130},{1,131},{2,128},{3,129},{128,2},{129,3},{130,0},{131,1},{4... | collective-permute-start | bytes 1966088 | tf_op jit(solution)/shard_map/ppermute | solution.py:359
  118.8 14.7 %copy-start.7 = (bf16[512,640]{1,0:T(8,128)(2,1)S(1)}, bf16[512,640]{1,0:T(8,128)(2,1)}, u32[]{:S(2)}) copy-start(bf16[512,640]{1,0:T(8,128)(2,1)} %rotated.3) | copy-start | bytes 1966084
  120.4 22.0 %copy-start.2 = (bf16[640,896]{1,0:T(8,128)(2,1)S(1)}, bf16[640,896]{1,0:T(8,128)(2,1)}, u32[]{:S(2)}) copy-start(bf16[640,896]{1,0:T(8,128)(2,1)} %weight_term.3.mine) | copy-start | bytes 3440644
  (3 other events, 2.1 us)

commit v4 on v3

--- a/solution.py
+++ b/solution.py
@@ -200,7 +200,10 @@
             pltpu.SemaphoreType.DMA,
         ],
         compiler_params=pltpu.CompilerParams(vmem_limit_bytes=VMEM),
-        cost_estimate=LITTLE,
+        cost_estimate=pl.CostEstimate(
+            flops=2 * tokens * width * cols,
+            bytes_accessed=2 * (tokens * (width + cols) + width * cols),
+            transcendentals=0),
         name="weight_term",
     )(where, *pieces, *clips)
 
@@ -344,6 +347,7 @@
         return arrays[:-3]
 
     own = move(cotangent, (0, 0), (0, 0), True)
+    own, where = tie((own, where))
     groups = gather(own, first_core, before_second)
     mine0 = weight_term(where, groups[0], clips, grad_norm)
     theirs0 = lax.ppermute(mine0, "dp", DP)

time: 146 us -> 143 us (0.979)
  local copies, waits for them, and re-layouts: 7.34 us -> 3.46 us
  waiting for transfers between devices: 35.9 us -> 38.2 us
    ppermute x22, waiting for transfers between devices: 5.96 us -> 8.97 us  [move(): lax.ppermute(value, ('dp', 'col', 'row'), pairs_for((core0, core1), swap))]
    unnamed x44 -> x40, local copies, waits for them, and re-layouts: 4.99 us -> 2.56 us
  transfers between devices with their start and end apart: 29 -> 29, of which waited for: 9 -> 14; matrix products, arithmetic and copies ran while one was open for 4% -> 3% of each run, Pallas kernels for 21% -> 22%
where the time goes in v4:
time: 143 us; the launch traced here: 142 us
  starting transfers between devices  62.3 us (44%)
  waiting for transfers between devices  38.2 us (27%)
  Pallas kernels  32.6 us (23%)
  local copies, waits for them, and re-layouts  3.46 us (2%)
  other arithmetic  3.14 us (2%)
  between operations  1.83 us (1%)
    ppermute x22, starting transfers between devices, move(): lax.ppermute(value, ('dp', 'col', 'row'), pairs_for((core0, core1), swap))  37.8 us
    pallas_call x2, Pallas kernels, weight_term(): pl.pallas_call(functools.partial(weight_kernel, scale), out_shape=jax.Sha...  14 us
    pallas_call x1, Pallas kernels, act_parts(): pl.pallas_call(act_kernel, out_shape=[jax.ShapeDtypeStruct((2 * rows, col...  13.1 us
    ppermute x1, waiting for transfers between devices, body(): inward = lax.ppermute(outward, ('dp', 'row'), PARTNER)  13 us
    ppermute x2, starting transfers between devices, body(): clips.append(lax.ppermute(clipped, ('dp', 'row'), pairs))  9.94 us
    ppermute x2, waiting for transfers between devices, body(): clips.append(lax.ppermute(clipped, ('dp', 'row'), pairs))  9.56 us
    ppermute x22, waiting for transfers between devices, move(): lax.ppermute(value, ('dp', 'col', 'row'), pairs_for((core0, core1), swap))  8.97 us
    ppermute x1, starting transfers between devices, body(): got = lax.ppermute(away, 'row', CORE)  6.85 us
  transfers between devices with their start and end apart: 29, of which 14 were waited for; matrix products, arithmetic and copies ran while one was open for 3% of the time, Pallas kernels for 22%

profile of v4, /device:TPU:1, one launch (start us, length us, event | category | flops | bytes accessed | tf_op | source)
XLA Modules:
  0.0 141.5 jit_solution(3670759201092045054)
XLA Ops:
  0.6 1.6 %collective-permute-start = (bf16[64,1792]{1,0:T(8,128)(2,1)}, bf16[64,1792]{1,0:T(8,128)(2,1)S(1)}, u32[]{:S(2)}, u32[]{:S(2)}) collective-permute-start(bf16[64,1792]{1,0:T(8,128)(2,1)} %param.5), channel_id=1, source_target_pairs={{0,0},{1,1},{2,130},{3,131},{4,4},{5,5},{6,134},{7,135},{8,8},{9,9... | collective-permute-start | bytes 688136 | tf_op jit(solution)/shard_map/ppermute | solution.py:58
  2.2 0.8 copy.8.bound
  3.1 1.1 copy-done.1
  4.1 0.4 clip_turned.1.refs_10_
  4.6 3.3 %collective-permute-start.6 = (bf16[640,512]{1,0:T(8,128)(2,1)S(1)}, bf16[640,512]{1,0:T(8,128)(2,1)S(1)}, u32[]{:S(2)}, u32[]{:S(2)}) collective-permute-start(bf16[640,512]{1,0:T(8,128)(2,1)S(1)} %clip_turned.1.refs_10_), channel_id=1, source_target_pairs={{0,1},{1,0},{2,3},{3,2},{4,5},{5,4},{6,7},{7,6},{8,9},{9,8},{10,11... | collective-permute-start | bytes 1966088 | tf_op jit(solution)/shard_map/ppermute | solution.py:340
  7.9 1.9 %collective-permute-start.7 = (bf16[640,512]{1,0:T(8,128)(2,1)S(1)}, bf16[640,512]{1,0:T(8,128)(2,1)}, u32[]{:S(2)}, u32[]{:S(2)}) collective-permute-start(bf16[640,512]{1,0:T(8,128)(2,1)S(1)} %clip_turned.1.refs_10_), channel_id=1, source_target_pairs={{0,130},{1,131},{2,128},{3,129},{128,2},{129,3},{130,0},{131,1},{4... | collective-permute-start | bytes 1966088 | tf_op jit(solution)/shard_map/ppermute | solution.py:342
  9.8 0.6 pad_add_fusion.where
  10.4 2.5 %collective-permute-start.1 = (bf16[64,1792]{1,0:T(8,128)(2,1)S(1)}, bf16[64,1792]{1,0:T(8,128)(2,1)S(1)}, u32[]{:S(2)}, u32[]{:S(2)}) collective-permute-start(bf16[64,1792]{1,0:T(8,128)(2,1)S(1)} %collective-permute-done.own), channel_id=1, source_target_pairs={{0,8},{1,65},{2,10},{3,67},{4,12},{5,69},{6,14},{7,71},{8,16},{9,7... | collective-permute-start | bytes 688136 | tf_op jit(solution)/shard_map/ppermute | solution.py:58
  13.3 2.3 %collective-permute-start.3 = (bf16[64,1792]{1,0:T(8,128)(2,1)S(1)}, bf16[64,1792]{1,0:T(8,128)(2,1)S(1)}, u32[]{:S(2)}, u32[]{:S(2)}) collective-permute-start(bf16[64,1792]{1,0:T(8,128)(2,1)S(1)} %collective-permute-done.own), channel_id=1, source_target_pairs={{0,28},{1,97},{2,30},{3,99},{4,0},{5,101},{6,2},{7,103},{8,4},{9,1... | collective-permute-start | bytes 688136 | tf_op jit(solution)/shard_map/ppermute | solution.py:58
  15.6 1.2 collective-permute-done.1.c
  16.8 8.0 %collective-permute-start.8 = (bf16[640,512]{1,0:T(8,128)(2,1)S(1)}, bf16[640,512]{1,0:T(8,128)(2,1)S(1)}, u32[]{:S(2)}, u32[]{:S(2)}) collective-permute-start(bf16[640,512]{1,0:T(8,128)(2,1)S(1)} %clip_turned.1.refs_10_), channel_id=1, source_target_pairs={{0,131},{1,130},{2,129},{3,128},{128,3},{129,2},{130,1},{131,0},{4... | collective-permute-start | bytes 1966088 | tf_op jit(solution)/shard_map/ppermute | solution.py:342
  25.0 0.7 collective-permute-start.4
  25.7 0.7 collective-permute-start.5
  26.4 2.7 %collective-permute-start.9 = (bf16[256,896]{1,0:T(8,128)(2,1)S(1)}, bf16[256,896]{1,0:T(8,128)(2,1)}, u32[]{:S(2)}, u32[]{:S(2)}) collective-permute-start(bf16[256,896]{1,0:T(8,128)(2,1)S(1)} %get-tuple-element.39.refs_0_), channel_id=1, source_target_pairs={{0,32},{1,5},{2,34},{3,7},{4,36},{5,9},{6,38},{7,11},{8,40},{9,13}... | collective-permute-start | bytes 1376264 | tf_op jit(solution)/shard_map/ppermute | solution.py:58
  29.2 1.3 collective-permute-start.10
  30.5 9.6 %collective-permute-done.8.refs_13_ = bf16[640,512]{1,0:T(8,128)(2,1)S(1)} collective-permute-done((bf16[640,512]{1,0:T(8,128)(2,1)S(1)}, bf16[640,512]{1,0:T(8,128)(2,1)S(1)}, u32[]{:S(2)}, u32[]{:S(2)}) %collective-permute-start.8) | collective-permute-done | bytes 655392 | tf_op jit(solution)/shard_map/ppermute | solution.py:342
  40.1 2.3 %collective-permute-start.17 = (bf16[256,896]{1,0:T(8,128)(2,1)S(1)}, bf16[256,896]{1,0:T(8,128)(2,1)}, u32[]{:S(2)}, u32[]{:S(2)}) collective-permute-start(bf16[256,896]{1,0:T(8,128)(2,1)S(1)} %get-tuple-element.46.refs_10_.refs_0_), channel_id=1, source_target_pairs={{0,32},{1,5},{2,34},{3,7},{4,36},{5,9},{6,38},{7,11},{8,40},{9,13}... | collective-permute-start | bytes 1376264 | tf_op jit(solution)/shard_map/ppermute | solution.py:58
  42.4 2.5 %collective-permute-start.18 = (bf16[256,896]{1,0:T(8,128)(2,1)S(1)}, bf16[256,896]{1,0:T(8,128)(2,1)}, u32[]{:S(2)}, u32[]{:S(2)}) collective-permute-start(bf16[256,896]{1,0:T(8,128)(2,1)S(1)} %get-tuple-element.46.refs_10_.refs_0_), channel_id=1, source_target_pairs={{0,96},{1,29},{2,98},{3,31},{4,100},{5,1},{6,102},{7,3},{8,104},{9... | collective-permute-start | bytes 1376264 | tf_op jit(solution)/shard_map/ppermute | solution.py:58
  44.9 1.6 %collective-permute-start.11 = (bf16[256,896]{1,0:T(8,128)(2,1)}, bf16[256,896]{1,0:T(8,128)(2,1)}, u32[]{:S(2)}, u32[]{:S(2)}) collective-permute-start(bf16[256,896]{1,0:T(8,128)(2,1)} %collective-permute-done.9.refs_2_), channel_id=1, source_target_pairs={{0,32},{1,5},{2,34},{3,7},{4,36},{5,9},{6,38},{7,11},{8,40},{9,13}... | collective-permute-start | bytes 1376264 | tf_op jit(solution)/shard_map/ppermute | solution.py:58
  46.5 3.0 %collective-permute-start.12 = (bf16[256,896]{1,0:T(8,128)(2,1)}, bf16[256,896]{1,0:T(8,128)(2,1)}, u32[]{:S(2)}, u32[]{:S(2)}) collective-permute-start(bf16[256,896]{1,0:T(8,128)(2,1)} %collective-permute-done.10.refs_3_), channel_id=1, source_target_pairs={{1,29},{3,31},{5,1},{7,3},{9,5},{11,7},{13,9},{15,11},{17,13},{19,... | collective-permute-start | bytes 1376264 | tf_op jit(solution)/shard_map/ppermute | solution.py:58
  49.5 1.7 %collective-permute-done.17.refs_12_.refs_2_ = bf16[256,896]{1,0:T(8,128)(2,1)} collective-permute-done((bf16[256,896]{1,0:T(8,128)(2,1)S(1)}, bf16[256,896]{1,0:T(8,128)(2,1)}, u32[]{:S(2)}, u32[]{:S(2)}) %collective-permute-start.17) | collective-permute-done | bytes 458784 | tf_op jit(solution)/shard_map/ppermute | solution.py:58
  51.6 4.3 %collective-permute-start.20 = (bf16[256,896]{1,0:T(8,128)(2,1)}, bf16[256,896]{1,0:T(8,128)(2,1)}, u32[]{:S(2)}, u32[]{:S(2)}) collective-permute-start(bf16[256,896]{1,0:T(8,128)(2,1)} %collective-permute-done.18.refs_13_.refs_3_), channel_id=1, source_target_pairs={{1,29},{3,31},{5,1},{7,3},{9,5},{11,7},{13,9},{15,11},{17,13},{19,... | collective-permute-start | bytes 1376264 | tf_op jit(solution)/shard_map/ppermute | solution.py:58
  56.5 1.2 broadcast_select_fusion.2
  58.1 2.6 %collective-permute-start.14 = (bf16[256,896]{1,0:T(8,128)(2,1)S(1)}, bf16[256,896]{1,0:T(8,128)(2,1)S(1)}, u32[]{:S(2)}, u32[]{:S(2)}) collective-permute-start(bf16[256,896]{1,0:T(8,128)(2,1)S(1)} %get-tuple-element.54), channel_id=1, source_target_pairs={{0,96},{1,29},{2,98},{3,31},{4,100},{5,1},{6,102},{7,3},{8,104},{9... | collective-permute-start | bytes 1376264 | tf_op jit(solution)/shard_map/ppermute | solution.py:58
  60.7 0.7 collective-permute-done.19.refs_14_.refs_4_
  61.6 1.1 broadcast_select_fusion
  62.8 2.7 %collective-permute-start.21 = (bf16[256,896]{1,0:T(8,128)(2,1)S(1)}, bf16[256,896]{1,0:T(8,128)(2,1)S(1)}, u32[]{:S(2)}, u32[]{:S(2)}) collective-permute-start(bf16[256,896]{1,0:T(8,128)(2,1)S(1)} %get-tuple-element.53), channel_id=1, source_target_pairs={{0,32},{1,5},{2,34},{3,7},{4,36},{5,9},{6,38},{7,11},{8,40},{9,13}... | collective-permute-start | bytes 1376264 | tf_op jit(solution)/shard_map/ppermute | solution.py:58
  65.4 1.0 collective-permute-start.22
  66.8 1.1 collective-permute-start.15
  67.9 0.6 collective-permute-done.14.refs_7_
  68.5 1.4 %collective-permute-start.16 = (bf16[128,896]{1,0:T(8,128)(2,1)S(1)}, bf16[128,896]{1,0:T(8,128)(2,1)S(1)}, u32[]{:S(2)}, u32[]{:S(2)}) collective-permute-start(bf16[128,896]{1,0:T(8,128)(2,1)S(1)} %slice.25), channel_id=1, source_target_pairs={{0,96},{1,29},{2,98},{3,31},{4,100},{5,1},{6,102},{7,3},{8,104},{9... | collective-permute-start | bytes 688136 | tf_op jit(solution)/shard_map/ppermute | solution.py:58
  70.0 2.5 %collective-permute-done.21.refs_16_.refs_6_ = bf16[256,896]{1,0:T(8,128)(2,1)S(1)} collective-permute-done((bf16[256,896]{1,0:T(8,128)(2,1)S(1)}, bf16[256,896]{1,0:T(8,128)(2,1)S(1)}, u32[]{:S(2)}, u32[]{:S(2)}) %collective-permute-start.21) | collective-permute-done | bytes 458784 | tf_op jit(solution)/shard_map/ppermute | solution.py:58
  72.5 0.6 collective-permute-start.23
  73.6 1.8 %collective-permute-start.24 = (bf16[128,896]{1,0:T(8,128)(2,1)S(1)}, bf16[128,896]{1,0:T(8,128)(2,1)}, u32[]{:S(2)}, u32[]{:S(2)}) collective-permute-start(bf16[128,896]{1,0:T(8,128)(2,1)S(1)} %slice.27), channel_id=1, source_target_pairs={{0,96},{1,29},{2,98},{3,31},{4,100},{5,1},{6,102},{7,3},{8,104},{9... | collective-permute-start | bytes 688136 | tf_op jit(solution)/shard_map/ppermute | solution.py:58
  75.4 0.7 collective-permute-done.16.refs_9_
  76.1 0.7 copy-done.17
  76.8 7.0 %weight_term.2.mine = bf16[640,896]{1,0:T(8,128)(2,1)} custom-call(s32[3]{0:T(128)} %pad_add_fusion.where, bf16[256,896]{1,0:T(8,128)(2,1)} %copy-done.9, bf16[256,896]{1,0:T(8,128)(2,1)} %copy-done.4, bf16[256,896]{1,0:T(8,128)(2,1)} %collective-permute-done.9.refs_2_, bf16[256,896]{1,0:T(8,128)(2,1)} %collective-permute-done.10.refs_3_, ...), custom_call_target="tpu_custom_call" | custom-call | flops 2348810240 | bytes 7438336 | tf_op jit(solution)/shard_map/weight_term/pallas_call | solution.py:191
  83.8 0.6 collective-permute-start.27
  85.1 0.7 copy-done.15
  85.7 13.1 %act_parts.1 = (bf16[1024,640]{1,0:T(8,128)(2,1)}, bf16[1024,640]{1,0:T(8,128)(2,1)}) custom-call(s32[3]{0:T(128)} %pad_add_fusion.where, f32[1]{0:T(128)S(6)} %copy.11.weight_scale, bf16[1792,640]{1,0:T(8,128)(2,1)} %codes.1, bf16[256,896]{1,0:T(8,128)(2,1)} %copy-done.9, bf16[256,896]{1,0:T(8,128)(2,1)} %copy-done.4, ...), custom_call_target="tpu_custom_call" | custom-call | flops 1 | bytes 1 | tf_op jit(solution)/shard_map/act_parts/pallas_call | solution.py:278
  98.8 6.8 %collective-permute-start.25 = (bf16[1024,640]{1,0:T(8,128)(2,1)}, bf16[1024,640]{1,0:T(8,128)(2,1)S(1)}, u32[]{:S(2)}, u32[]{:S(2)}) collective-permute-start(bf16[1024,640]{1,0:T(8,128)(2,1)} %get-tuple-element.45), channel_id=1, source_target_pairs={{0,1},{1,0},{2,3},{3,2},{4,5},{5,4},{6,7},{7,6},{8,9},{9,8},{10,11... | collective-permute-start | bytes 3932168 | tf_op jit(solution)/shard_map/ppermute | solution.py:359
  105.7 7.0 %weight_term.3.mine = bf16[640,896]{1,0:T(8,128)(2,1)} custom-call(s32[3]{0:T(128)} %pad_add_fusion.where, bf16[256,896]{1,0:T(8,128)(2,1)} %copy-done.8, bf16[256,896]{1,0:T(8,128)(2,1)} %copy-done.3, bf16[256,896]{1,0:T(8,128)(2,1)} %collective-permute-done.17.refs_12_.refs_2_, bf16[256,896]{1,0:T(8,128)(2,1)} %collective-permute-done.18.refs_13_.refs_3_, ...), custom_call_target="tpu_custom_call" | custom-call | flops 2348810240 | bytes 7438336 | tf_op jit(solution)/shard_map/weight_term/pallas_call | solution.py:191
  113.1 3.6 %collective-permute-start.26 = (bf16[512,640]{1,0:T(8,128)(2,1)S(1)}, bf16[512,640]{1,0:T(8,128)(2,1)S(1)}, u32[]{:S(2)}, u32[]{:S(2)}) collective-permute-start(bf16[512,640]{1,0:T(8,128)(2,1)S(1)} %add_convert_fusion), channel_id=1, source_target_pairs={{0,130},{1,131},{2,128},{3,129},{128,2},{129,3},{130,0},{131,1},{4... | collective-permute-start | bytes 1966088 | tf_op jit(solution)/shard_map/ppermute | solution.py:363
  116.8 1.6 %sum_terms.2.refs_0_ = f32[1792,640]{1,0:T(8,128)} custom-call(bf16[640,896]{1,0:T(8,128)(2,1)S(1)} %copy-done.5, bf16[640,896]{1,0:T(8,128)(2,1)S(1)} %collective-permute-done.27.theirs), custom_call_target="tpu_custom_call" | custom-call | tf_op jit(solution)/shard_map/sum_terms/pallas_call | solution.py:230
  118.4 13.0 %collective-permute-done.26.other = bf16[512,640]{1,0:T(8,128)(2,1)S(1)} collective-permute-done((bf16[512,640]{1,0:T(8,128)(2,1)S(1)}, bf16[512,640]{1,0:T(8,128)(2,1)S(1)}, u32[]{:S(2)}, u32[]{:S(2)}) %collective-permute-start.26) | collective-permute-done | bytes 655392 | tf_op jit(solution)/shard_map/ppermute | solution.py:363
  131.4 1.7 %finish.1 = bf16[512,640]{1,0:T(8,128)(2,1)} custom-call(bf16[1024,640]{1,0:T(8,128)(2,1)S(1)} %copy-done, bf16[1024,640]{1,0:T(8,128)(2,1)S(1)} %collective-permute-done.25.got, bf16[512,640]{1,0:T(8,128)(2,1)S(1)} %collective-permute-done.26.other, bf16[512,640]{1,0:T(8,128)(2,1)S(1)} %copy-done.2, f32[512,1]{1,0:T(8,128)S(1)} %copy.8.bound, ...), custom_call_target="tpu_custom_call" | custom-call | tf_op jit(solution)/shard_map/finish/pallas_call | solution.py:310
  133.1 6.6 %collective-permute-done.28.theirs = bf16[640,896]{1,0:T(8,128)(2,1)S(1)} collective-permute-done((bf16[640,896]{1,0:T(8,128)(2,1)}, bf16[640,896]{1,0:T(8,128)(2,1)S(1)}, u32[]{:S(2)}, u32[]{:S(2)}) %collective-permute-start.28) | collective-permute-done | bytes 1146912 | tf_op jit(solution)/shard_map/ppermute | solution.py:362
  139.7 1.6 %sum_terms.3 = f32[1792,640]{1,0:T(8,128)} custom-call(bf16[640,896]{1,0:T(8,128)(2,1)S(1)} %copy-done.6, bf16[640,896]{1,0:T(8,128)(2,1)S(1)} %collective-permute-done.28.theirs, f32[1792,640]{1,0:T(8,128)} %sum_terms.2.refs_0_), custom_call_target="tpu_custom_call", output_to_operand_aliasing={{}: (2, {})} | custom-call | tf_op jit(solution)/shard_map/sum_terms/pallas_call | solution.py:230
  (69 shorter events, 3.4 us)
Async XLA Ops:
  0.6 9.8 %collective-permute-start = (bf16[64,1792]{1,0:T(8,128)(2,1)}, bf16[64,1792]{1,0:T(8,128)(2,1)S(1)}, u32[]{:S(2)}, u32[]{:S(2)}) collective-permute-start(bf16[64,1792]{1,0:T(8,128)(2,1)} %param.5), channel_id=1, source_target_pairs={{0,0},{1,1},{2,130},{3,131},{4,4},{5,5},{6,134},{7,135},{8,8},{9,9... | collective-permute-start | bytes 688136 | tf_op jit(solution)/shard_map/ppermute | solution.py:58
  3.1 1.1 copy-start.1
  4.6 53.2 %copy-start.7 = (bf16[640,512]{1,0:T(8,128)(2,1)}, bf16[640,512]{1,0:T(8,128)(2,1)S(1)}, u32[]{:S(2)}) copy-start(bf16[640,512]{1,0:T(8,128)(2,1)S(1)} %clip_turned.1.refs_10_) | copy-start | bytes 1966084
  4.6 21.8 %collective-permute-start.6 = (bf16[640,512]{1,0:T(8,128)(2,1)S(1)}, bf16[640,512]{1,0:T(8,128)(2,1)S(1)}, u32[]{:S(2)}, u32[]{:S(2)}) collective-permute-start(bf16[640,512]{1,0:T(8,128)(2,1)S(1)} %clip_turned.1.refs_10_), channel_id=1, source_target_pairs={{0,1},{1,0},{2,3},{3,2},{4,5},{5,4},{6,7},{7,6},{8,9},{9,8},{10,11... | collective-permute-start | bytes 1966088 | tf_op jit(solution)/shard_map/ppermute | solution.py:340
  7.9 21.2 %collective-permute-start.7 = (bf16[640,512]{1,0:T(8,128)(2,1)S(1)}, bf16[640,512]{1,0:T(8,128)(2,1)}, u32[]{:S(2)}, u32[]{:S(2)}) collective-permute-start(bf16[640,512]{1,0:T(8,128)(2,1)S(1)} %clip_turned.1.refs_10_), channel_id=1, source_target_pairs={{0,130},{1,131},{2,128},{3,129},{128,2},{129,3},{130,0},{131,1},{4... | collective-permute-start | bytes 1966088 | tf_op jit(solution)/shard_map/ppermute | solution.py:342
  10.4 6.4 %collective-permute-start.1 = (bf16[64,1792]{1,0:T(8,128)(2,1)S(1)}, bf16[64,1792]{1,0:T(8,128)(2,1)S(1)}, u32[]{:S(2)}, u32[]{:S(2)}) collective-permute-start(bf16[64,1792]{1,0:T(8,128)(2,1)S(1)} %collective-permute-done.own), channel_id=1, source_target_pairs={{0,8},{1,65},{2,10},{3,67},{4,12},{5,69},{6,14},{7,71},{8,16},{9,7... | collective-permute-start | bytes 688136 | tf_op jit(solution)/shard_map/ppermute | solution.py:58
  12.9 11.9 %collective-permute-start.2 = (bf16[64,1792]{1,0:T(8,128)(2,1)S(1)}, bf16[64,1792]{1,0:T(8,128)(2,1)S(1)}, u32[]{:S(2)}, u32[]{:S(2)}) collective-permute-start(bf16[64,1792]{1,0:T(8,128)(2,1)S(1)} %collective-permute-done.own), channel_id=1, source_target_pairs={{0,4},{1,33},{2,6},{3,35},{4,8},{5,37},{6,10},{7,39},{8,12},{9,41}... | collective-permute-start | bytes 688136 | tf_op jit(solution)/shard_map/ppermute | solution.py:58
  13.3 11.5 %collective-permute-start.3 = (bf16[64,1792]{1,0:T(8,128)(2,1)S(1)}, bf16[64,1792]{1,0:T(8,128)(2,1)S(1)}, u32[]{:S(2)}, u32[]{:S(2)}) collective-permute-start(bf16[64,1792]{1,0:T(8,128)(2,1)S(1)} %collective-permute-done.own), channel_id=1, source_target_pairs={{0,28},{1,97},{2,30},{3,99},{4,0},{5,101},{6,2},{7,103},{8,4},{9,1... | collective-permute-start | bytes 688136 | tf_op jit(solution)/shard_map/ppermute | solution.py:58
  16.8 23.2 %collective-permute-start.8 = (bf16[640,512]{1,0:T(8,128)(2,1)S(1)}, bf16[640,512]{1,0:T(8,128)(2,1)S(1)}, u32[]{:S(2)}, u32[]{:S(2)}) collective-permute-start(bf16[640,512]{1,0:T(8,128)(2,1)S(1)} %clip_turned.1.refs_10_), channel_id=1, source_target_pairs={{0,131},{1,130},{2,129},{3,128},{128,3},{129,2},{130,1},{131,0},{4... | collective-permute-start | bytes 1966088 | tf_op jit(solution)/shard_map/ppermute | solution.py:342
  25.0 32.8 %copy-start.8 = (bf16[256,896]{1,0:T(8,128)(2,1)}, bf16[256,896]{1,0:T(8,128)(2,1)S(1)}, u32[]{:S(2)}) copy-start(bf16[256,896]{1,0:T(8,128)(2,1)S(1)} %get-tuple-element.46.refs_10_.refs_0_) | copy-start | bytes 1376260
  25.0 32.8 %copy-start.9 = (bf16[256,896]{1,0:T(8,128)(2,1)}, bf16[256,896]{1,0:T(8,128)(2,1)S(1)}, u32[]{:S(2)}) copy-start(bf16[256,896]{1,0:T(8,128)(2,1)S(1)} %get-tuple-element.39.refs_0_) | copy-start | bytes 1376260
  25.0 15.1 %collective-permute-start.4 = (bf16[128,1792]{1,0:T(8,128)(2,1)S(1)}, bf16[128,1792]{1,0:T(8,128)(2,1)S(1)}, u32[]{:S(2)}, u32[]{:S(2)}) collective-permute-start(bf16[128,1792]{1,0:T(8,128)(2,1)S(1)} %get-tuple-element.31), channel_id=1, source_target_pairs={{0,8},{2,10},{4,12},{6,14},{8,16},{10,18},{12,20},{14,22},{16,24},... | collective-permute-start | bytes 1376264 | tf_op jit(solution)/shard_map/ppermute | solution.py:58
  25.7 14.4 %collective-permute-start.5 = (bf16[128,1792]{1,0:T(8,128)(2,1)S(1)}, bf16[128,1792]{1,0:T(8,128)(2,1)S(1)}, u32[]{:S(2)}, u32[]{:S(2)}) collective-permute-start(bf16[128,1792]{1,0:T(8,128)(2,1)S(1)} %get-tuple-element.32), channel_id=1, source_target_pairs={{0,24},{2,26},{4,28},{6,30},{8,0},{10,2},{12,4},{14,6},{16,8},{18,... | collective-permute-start | bytes 1376264 | tf_op jit(solution)/shard_map/ppermute | solution.py:58
  26.4 23.1 %copy-start.18 = (bf16[640,512]{1,0:T(8,128)(2,1)}, bf16[640,512]{1,0:T(8,128)(2,1)S(1)}, u32[]{:S(2)}) copy-start(bf16[640,512]{1,0:T(8,128)(2,1)S(1)} %collective-permute-done.6.refs_11_) | copy-start | bytes 1966084
  26.4 18.5 %collective-permute-start.9 = (bf16[256,896]{1,0:T(8,128)(2,1)S(1)}, bf16[256,896]{1,0:T(8,128)(2,1)}, u32[]{:S(2)}, u32[]{:S(2)}) collective-permute-start(bf16[256,896]{1,0:T(8,128)(2,1)S(1)} %get-tuple-element.39.refs_0_), channel_id=1, source_target_pairs={{0,32},{1,5},{2,34},{3,7},{4,36},{5,9},{6,38},{7,11},{8,40},{9,13}... | collective-permute-start | bytes 1376264 | tf_op jit(solution)/shard_map/ppermute | solution.py:58
  29.2 17.3 %collective-permute-start.10 = (bf16[256,896]{1,0:T(8,128)(2,1)S(1)}, bf16[256,896]{1,0:T(8,128)(2,1)}, u32[]{:S(2)}, u32[]{:S(2)}) collective-permute-start(bf16[256,896]{1,0:T(8,128)(2,1)S(1)} %get-tuple-element.39.refs_0_), channel_id=1, source_target_pairs={{0,96},{1,29},{2,98},{3,31},{4,100},{5,1},{6,102},{7,3},{8,104},{9... | collective-permute-start | bytes 1376264 | tf_op jit(solution)/shard_map/ppermute | solution.py:58
  40.0 11.6 %copy-start.19 = (bf16[640,512]{1,0:T(8,128)(2,1)}, bf16[640,512]{1,0:T(8,128)(2,1)S(1)}, u32[]{:S(2)}) copy-start(bf16[640,512]{1,0:T(8,128)(2,1)S(1)} %collective-permute-done.8.refs_13_) | copy-start | bytes 1966084
  40.1 11.2 %collective-permute-start.17 = (bf16[256,896]{1,0:T(8,128)(2,1)S(1)}, bf16[256,896]{1,0:T(8,128)(2,1)}, u32[]{:S(2)}, u32[]{:S(2)}) collective-permute-start(bf16[256,896]{1,0:T(8,128)(2,1)S(1)} %get-tuple-element.46.refs_10_.refs_0_), channel_id=1, source_target_pairs={{0,32},{1,5},{2,34},{3,7},{4,36},{5,9},{6,38},{7,11},{8,40},{9,13}... | collective-permute-start | bytes 1376264 | tf_op jit(solution)/shard_map/ppermute | solution.py:58
  42.4 9.3 %collective-permute-start.18 = (bf16[256,896]{1,0:T(8,128)(2,1)S(1)}, bf16[256,896]{1,0:T(8,128)(2,1)}, u32[]{:S(2)}, u32[]{:S(2)}) collective-permute-start(bf16[256,896]{1,0:T(8,128)(2,1)S(1)} %get-tuple-element.46.refs_10_.refs_0_), channel_id=1, source_target_pairs={{0,96},{1,29},{2,98},{3,31},{4,100},{5,1},{6,102},{7,3},{8,104},{9... | collective-permute-start | bytes 1376264 | tf_op jit(solution)/shard_map/ppermute | solution.py:58
  44.9 11.5 %collective-permute-start.11 = (bf16[256,896]{1,0:T(8,128)(2,1)}, bf16[256,896]{1,0:T(8,128)(2,1)}, u32[]{:S(2)}, u32[]{:S(2)}) collective-permute-start(bf16[256,896]{1,0:T(8,128)(2,1)} %collective-permute-done.9.refs_2_), channel_id=1, source_target_pairs={{0,32},{1,5},{2,34},{3,7},{4,36},{5,9},{6,38},{7,11},{8,40},{9,13}... | collective-permute-start | bytes 1376264 | tf_op jit(solution)/shard_map/ppermute | solution.py:58
  46.5 10.1 %collective-permute-start.12 = (bf16[256,896]{1,0:T(8,128)(2,1)}, bf16[256,896]{1,0:T(8,128)(2,1)}, u32[]{:S(2)}, u32[]{:S(2)}) collective-permute-start(bf16[256,896]{1,0:T(8,128)(2,1)} %collective-permute-done.10.refs_3_), channel_id=1, source_target_pairs={{1,29},{3,31},{5,1},{7,3},{9,5},{11,7},{13,9},{15,11},{17,13},{19,... | collective-permute-start | bytes 1376264 | tf_op jit(solution)/shard_map/ppermute | solution.py:58
  51.2 10.1 %collective-permute-start.19 = (bf16[256,896]{1,0:T(8,128)(2,1)}, bf16[256,896]{1,0:T(8,128)(2,1)S(1)}, u32[]{:S(2)}, u32[]{:S(2)}) collective-permute-start(bf16[256,896]{1,0:T(8,128)(2,1)} %collective-permute-done.17.refs_12_.refs_2_), channel_id=1, source_target_pairs={{0,32},{1,5},{2,34},{3,7},{4,36},{5,9},{6,38},{7,11},{8,40},{9,13}... | collective-permute-start | bytes 1376264 | tf_op jit(solution)/shard_map/ppermute | solution.py:58
  51.6 10.0 %collective-permute-start.20 = (bf16[256,896]{1,0:T(8,128)(2,1)}, bf16[256,896]{1,0:T(8,128)(2,1)}, u32[]{:S(2)}, u32[]{:S(2)}) collective-permute-start(bf16[256,896]{1,0:T(8,128)(2,1)} %collective-permute-done.18.refs_13_.refs_3_), channel_id=1, source_target_pairs={{1,29},{3,31},{5,1},{7,3},{9,5},{11,7},{13,9},{15,11},{17,13},{19,... | collective-permute-start | bytes 1376264 | tf_op jit(solution)/shard_map/ppermute | solution.py:58
  56.0 6.7 %copy-start.3 = (bf16[256,896]{1,0:T(8,128)(2,1)}, bf16[256,896]{1,0:T(8,128)(2,1)S(1)}, u32[]{:S(2)}) copy-start(bf16[256,896]{1,0:T(8,128)(2,1)S(1)} %get-tuple-element.41.refs_11_.refs_1_) | copy-start | bytes 1376260
  56.0 6.7 %copy-start.4 = (bf16[256,896]{1,0:T(8,128)(2,1)}, bf16[256,896]{1,0:T(8,128)(2,1)S(1)}, u32[]{:S(2)}) copy-start(bf16[256,896]{1,0:T(8,128)(2,1)S(1)} %get-tuple-element.35.refs_1_) | copy-start | bytes 1376260
  57.8 8.9 %collective-permute-start.13 = (bf16[256,896]{1,0:T(8,128)(2,1)S(1)}, bf16[256,896]{1,0:T(8,128)(2,1)S(1)}, u32[]{:S(2)}, u32[]{:S(2)}) collective-permute-start(bf16[256,896]{1,0:T(8,128)(2,1)S(1)} %get-tuple-element.55), channel_id=1, source_target_pairs={{0,32},{1,5},{2,34},{3,7},{4,36},{5,9},{6,38},{7,11},{8,40},{9,13}... | collective-permute-start | bytes 1376264 | tf_op jit(solution)/shard_map/ppermute | solution.py:58
  58.1 10.4 %collective-permute-start.14 = (bf16[256,896]{1,0:T(8,128)(2,1)S(1)}, bf16[256,896]{1,0:T(8,128)(2,1)S(1)}, u32[]{:S(2)}, u32[]{:S(2)}) collective-permute-start(bf16[256,896]{1,0:T(8,128)(2,1)S(1)} %get-tuple-element.54), channel_id=1, source_target_pairs={{0,96},{1,29},{2,98},{3,31},{4,100},{5,1},{6,102},{7,3},{8,104},{9... | collective-permute-start | bytes 1376264 | tf_op jit(solution)/shard_map/ppermute | solution.py:58
  61.3 5.4 %copy-start.10 = (bf16[256,896]{1,0:T(8,128)(2,1)}, bf16[256,896]{1,0:T(8,128)(2,1)S(1)}, u32[]{:S(2)}) copy-start(bf16[256,896]{1,0:T(8,128)(2,1)S(1)} %collective-permute-done.19.refs_14_.refs_4_) | copy-start | bytes 1376260
  62.8 9.7 %collective-permute-start.21 = (bf16[256,896]{1,0:T(8,128)(2,1)S(1)}, bf16[256,896]{1,0:T(8,128)(2,1)S(1)}, u32[]{:S(2)}, u32[]{:S(2)}) collective-permute-start(bf16[256,896]{1,0:T(8,128)(2,1)S(1)} %get-tuple-element.53), channel_id=1, source_target_pairs={{0,32},{1,5},{2,34},{3,7},{4,36},{5,9},{6,38},{7,11},{8,40},{9,13}... | collective-permute-start | bytes 1376264 | tf_op jit(solution)/shard_map/ppermute | solution.py:58
  65.4 8.1 %collective-permute-start.22 = (bf16[256,896]{1,0:T(8,128)(2,1)S(1)}, bf16[256,896]{1,0:T(8,128)(2,1)S(1)}, u32[]{:S(2)}, u32[]{:S(2)}) collective-permute-start(bf16[256,896]{1,0:T(8,128)(2,1)S(1)} %get-tuple-element.52), channel_id=1, source_target_pairs={{0,96},{1,29},{2,98},{3,31},{4,100},{5,1},{6,102},{7,3},{8,104},{9... | collective-permute-start | bytes 1376264 | tf_op jit(solution)/shard_map/ppermute | solution.py:58
  66.7 9.3 %copy-start.12 = (bf16[256,896]{1,0:T(8,128)(2,1)}, bf16[256,896]{1,0:T(8,128)(2,1)S(1)}, u32[]{:S(2)}) copy-start(bf16[256,896]{1,0:T(8,128)(2,1)S(1)} %collective-permute-done.13.refs_6_) | copy-start | bytes 1376260
  66.8 8.6 %collective-permute-start.15 = (bf16[128,896]{1,0:T(8,128)(2,1)S(1)}, bf16[128,896]{1,0:T(8,128)(2,1)S(1)}, u32[]{:S(2)}, u32[]{:S(2)}) collective-permute-start(bf16[128,896]{1,0:T(8,128)(2,1)S(1)} %slice.24), channel_id=1, source_target_pairs={{0,32},{1,5},{2,34},{3,7},{4,36},{5,9},{6,38},{7,11},{8,40},{9,13}... | collective-permute-start | bytes 688136 | tf_op jit(solution)/shard_map/ppermute | solution.py:58
  68.5 7.5 %copy-start.14 = (bf16[256,896]{1,0:T(8,128)(2,1)}, bf16[256,896]{1,0:T(8,128)(2,1)S(1)}, u32[]{:S(2)}) copy-start(bf16[256,896]{1,0:T(8,128)(2,1)S(1)} %collective-permute-done.14.refs_7_) | copy-start | bytes 1376260
  68.5 7.5 %collective-permute-start.16 = (bf16[128,896]{1,0:T(8,128)(2,1)S(1)}, bf16[128,896]{1,0:T(8,128)(2,1)S(1)}, u32[]{:S(2)}, u32[]{:S(2)}) collective-permute-start(bf16[128,896]{1,0:T(8,128)(2,1)S(1)} %slice.25), channel_id=1, source_target_pairs={{0,96},{1,29},{2,98},{3,31},{4,100},{5,1},{6,102},{7,3},{8,104},{9... | collective-permute-start | bytes 688136 | tf_op jit(solution)/shard_map/ppermute | solution.py:58
  72.5 11.3 %copy-start.11 = (bf16[256,896]{1,0:T(8,128)(2,1)}, bf16[256,896]{1,0:T(8,128)(2,1)S(1)}, u32[]{:S(2)}) copy-start(bf16[256,896]{1,0:T(8,128)(2,1)S(1)} %collective-permute-done.21.refs_16_.refs_6_) | copy-start | bytes 1376260
  72.5 12.5 %collective-permute-start.23 = (bf16[128,896]{1,0:T(8,128)(2,1)S(1)}, bf16[128,896]{1,0:T(8,128)(2,1)S(1)}, u32[]{:S(2)}, u32[]{:S(2)}) collective-permute-start(bf16[128,896]{1,0:T(8,128)(2,1)S(1)} %slice.26), channel_id=1, source_target_pairs={{0,32},{1,5},{2,34},{3,7},{4,36},{5,9},{6,38},{7,11},{8,40},{9,13}... | collective-permute-start | bytes 688136 | tf_op jit(solution)/shard_map/ppermute | solution.py:58
  73.6 10.2 %copy-start.13 = (bf16[256,896]{1,0:T(8,128)(2,1)}, bf16[256,896]{1,0:T(8,128)(2,1)S(1)}, u32[]{:S(2)}) copy-start(bf16[256,896]{1,0:T(8,128)(2,1)S(1)} %collective-permute-done.22.refs_17_.refs_7_) | copy-start | bytes 1376260
  73.6 11.5 %collective-permute-start.24 = (bf16[128,896]{1,0:T(8,128)(2,1)S(1)}, bf16[128,896]{1,0:T(8,128)(2,1)}, u32[]{:S(2)}, u32[]{:S(2)}) collective-permute-start(bf16[128,896]{1,0:T(8,128)(2,1)S(1)} %slice.27), channel_id=1, source_target_pairs={{0,96},{1,29},{2,98},{3,31},{4,100},{5,1},{6,102},{7,3},{8,104},{9... | collective-permute-start | bytes 688136 | tf_op jit(solution)/shard_map/ppermute | solution.py:58
  76.1 0.7 copy-start.17
  83.8 28.9 %collective-permute-start.27 = (bf16[640,896]{1,0:T(8,128)(2,1)}, bf16[640,896]{1,0:T(8,128)(2,1)S(1)}, u32[]{:S(2)}, u32[]{:S(2)}) collective-permute-start(bf16[640,896]{1,0:T(8,128)(2,1)} %weight_term.2.mine), channel_id=1, source_target_pairs={{0,128},{128,0},{1,129},{129,1},{2,130},{130,2},{3,131},{131,3},{4... | collective-permute-start | bytes 3440648 | tf_op jit(solution)/shard_map/ppermute | solution.py:353
  85.0 0.7 copy-start.15
  98.8 14.1 %copy-start = (bf16[1024,640]{1,0:T(8,128)(2,1)S(1)}, bf16[1024,640]{1,0:T(8,128)(2,1)}, u32[]{:S(2)}) copy-start(bf16[1024,640]{1,0:T(8,128)(2,1)} %get-tuple-element.44.keep) | copy-start | bytes 3932164
  98.8 14.1 %collective-permute-start.25 = (bf16[1024,640]{1,0:T(8,128)(2,1)}, bf16[1024,640]{1,0:T(8,128)(2,1)S(1)}, u32[]{:S(2)}, u32[]{:S(2)}) collective-permute-start(bf16[1024,640]{1,0:T(8,128)(2,1)} %get-tuple-element.45), channel_id=1, source_target_pairs={{0,1},{1,0},{2,3},{3,2},{4,5},{5,4},{6,7},{7,6},{8,9},{9,8},{10,11... | collective-permute-start | bytes 3932168 | tf_op jit(solution)/shard_map/ppermute | solution.py:359
  112.7 4.1 %copy-start.5 = (bf16[640,896]{1,0:T(8,128)(2,1)S(1)}, bf16[640,896]{1,0:T(8,128)(2,1)}, u32[]{:S(2)}) copy-start(bf16[640,896]{1,0:T(8,128)(2,1)} %weight_term.2.mine) | copy-start | bytes 3440644
  112.7 27.0 %collective-permute-start.28 = (bf16[640,896]{1,0:T(8,128)(2,1)}, bf16[640,896]{1,0:T(8,128)(2,1)S(1)}, u32[]{:S(2)}, u32[]{:S(2)}) collective-permute-start(bf16[640,896]{1,0:T(8,128)(2,1)} %weight_term.3.mine), channel_id=1, source_target_pairs={{0,128},{128,0},{1,129},{129,1},{2,130},{130,2},{3,131},{131,3},{4... | collective-permute-start | bytes 3440648 | tf_op jit(solution)/shard_map/ppermute | solution.py:362
  113.1 18.4 %collective-permute-start.26 = (bf16[512,640]{1,0:T(8,128)(2,1)S(1)}, bf16[512,640]{1,0:T(8,128)(2,1)S(1)}, u32[]{:S(2)}, u32[]{:S(2)}) collective-permute-start(bf16[512,640]{1,0:T(8,128)(2,1)S(1)} %add_convert_fusion), channel_id=1, source_target_pairs={{0,130},{1,131},{2,128},{3,129},{128,2},{129,3},{130,0},{131,1},{4... | collective-permute-start | bytes 1966088 | tf_op jit(solution)/shard_map/ppermute | solution.py:363
  116.8 14.7 %copy-start.2 = (bf16[512,640]{1,0:T(8,128)(2,1)S(1)}, bf16[512,640]{1,0:T(8,128)(2,1)}, u32[]{:S(2)}) copy-start(bf16[512,640]{1,0:T(8,128)(2,1)} %rotated.3) | copy-start | bytes 1966084
  118.4 21.3 %copy-start.6 = (bf16[640,896]{1,0:T(8,128)(2,1)S(1)}, bf16[640,896]{1,0:T(8,128)(2,1)}, u32[]{:S(2)}) copy-start(bf16[640,896]{1,0:T(8,128)(2,1)} %weight_term.3.mine) | copy-start | bytes 3440644
  (1 other events, 0.7 us)

commit v5 on v4

--- a/solution.py
+++ b/solution.py
@@ -16,7 +16,7 @@
 WIDTHS = (896, 896)
 VMEM = 60 * 2**20
 SMALL = 16 * 2**20
-HALF = 512
+HALF = 256
 LITTLE = pl.CostEstimate(flops=1, bytes_accessed=1, transcendentals=0)
 
 NEAR = (-2, -1, 0, 1)
@@ -157,7 +157,7 @@
 def weight_kernel(scale, where, *refs):
     n = PIECES
     piece_refs, clip_refs = refs[:n], refs[n:n + 4]
-    out, held, clip_held, sem, clip_sem = refs[n + 4:]
+    out, made, held, clip_held, sem, clip_sem, out_sem = refs[n + 4:]
     for j, ref in enumerate(clip_refs):
         size = ref.shape[1]
         start = pl.multiple_of((where[2] ^ j) * size, size)
@@ -172,15 +172,21 @@
             pltpu.make_async_copy(ref.at[:, window], held.at[spot, window], sem.at[i]).start()
 
         each_shard(where, piece_refs, load)
+    outward = []
     pltpu.make_async_copy(clip_held, clip_held, clip_sem).wait()
     for i, (lo, hi) in enumerate(windows):
         part = held.at[:, pl.ds(lo, hi - lo)]
         pltpu.make_async_copy(part, part, sem.at[i]).wait()
         for first in range(lo, hi, 256):
             step = min(256, hi - first)
-            out[:, first:first + step] = (
+            made[:, first:first + step] = (
                 jnp.dot(clip_held[...], held[:, first:first + step], preferred_element_type=F32) * scale
             ).astype(BF)
+            tile = pl.ds(first, step)
+            outward.append(pltpu.make_async_copy(made.at[:, tile], out.at[:, tile], out_sem.at[len(outward)]))
+            outward[-1].start()
+    for copy in outward:
+        copy.wait()
 
 
 def weight_term(where, pieces, clips, scale):
@@ -192,12 +198,14 @@
         functools.partial(weight_kernel, scale),
         out_shape=jax.ShapeDtypeStruct((cols, width), BF),
         in_specs=[pl.BlockSpec(memory_space=pltpu.SMEM)] + [anywhere] * (len(pieces) + 4),
-        out_specs=pl.BlockSpec(memory_space=pltpu.VMEM),
+        out_specs=anywhere,
         scratch_shapes=[
+            pltpu.VMEM((cols, width), BF),
             pltpu.VMEM((tokens, width), BF),
             pltpu.VMEM((cols, tokens), BF),
             pltpu.SemaphoreType.DMA((2,)),
             pltpu.SemaphoreType.DMA,
+            pltpu.SemaphoreType.DMA((width // 128,)),
         ],
         compiler_params=pltpu.CompilerParams(vmem_limit_bytes=VMEM),
         cost_estimate=pl.CostEstimate(

time: 143 us -> 145 us (1.014)
  transfers between devices with their start and end apart: 29 -> 29, of which waited for: 14 -> 14; matrix products, arithmetic and copies ran while one was open for 3% -> 3% of each run, Pallas kernels for 22% -> 23%
where the time goes in v5:
time: 145 us; the launch traced here: 143 us
  starting transfers between devices  62.3 us (43%)
  waiting for transfers between devices  38.1 us (26%)
  Pallas kernels  34 us (23%)
  local copies, waits for them, and re-layouts  3.46 us (2%)
  other arithmetic  3.14 us (2%)
  between operations  1.83 us (1%)
    ppermute x22, starting transfers between devices, move(): lax.ppermute(value, ('dp', 'col', 'row'), pairs_for((core0, core1), swap))  37.8 us
    pallas_call x2, Pallas kernels, weight_term(): pl.pallas_call(functools.partial(weight_kernel, scale), out_shape=jax.Sha...  15.4 us
    pallas_call x1, Pallas kernels, act_parts(): pl.pallas_call(act_kernel, out_shape=[jax.ShapeDtypeStruct((2 * rows, col...  13 us
    ppermute x1, waiting for transfers between devices, body(): inward = lax.ppermute(outward, ('dp', 'row'), PARTNER)  13 us
    ppermute x2, starting transfers between devices, body(): clips.append(lax.ppermute(clipped, ('dp', 'row'), pairs))  9.94 us
    ppermute x2, waiting for transfers between devices, body(): clips.append(lax.ppermute(clipped, ('dp', 'row'), pairs))  9.56 us
    ppermute x22, waiting for transfers between devices, move(): lax.ppermute(value, ('dp', 'col', 'row'), pairs_for((core0, core1), swap))  8.97 us
    ppermute x1, starting transfers between devices, body(): got = lax.ppermute(away, 'row', CORE)  6.85 us
  transfers between devices with their start and end apart: 29, of which 14 were waited for; matrix products, arithmetic and copies ran while one was open for 3% of the time, Pallas kernels for 23%

profile of v5, /device:TPU:1, one launch (start us, length us, event | category | flops | bytes accessed | tf_op | source)
XLA Modules:
  0.0 142.9 jit_solution(3270124580258311643)
XLA Ops:
  0.6 1.6 %collective-permute-start = (bf16[64,1792]{1,0:T(8,128)(2,1)}, bf16[64,1792]{1,0:T(8,128)(2,1)S(1)}, u32[]{:S(2)}, u32[]{:S(2)}) collective-permute-start(bf16[64,1792]{1,0:T(8,128)(2,1)} %param.5), channel_id=1, source_target_pairs={{0,0},{1,1},{2,130},{3,131},{4,4},{5,5},{6,134},{7,135},{8,8},{9,9... | collective-permute-start | bytes 688136 | tf_op jit(solution)/shard_map/ppermute | solution.py:58
  2.2 0.8 copy.8.bound
  3.1 1.1 copy-done.1
  4.1 0.4 clip_turned.1.refs_10_
  4.6 3.3 %collective-permute-start.6 = (bf16[640,512]{1,0:T(8,128)(2,1)S(1)}, bf16[640,512]{1,0:T(8,128)(2,1)S(1)}, u32[]{:S(2)}, u32[]{:S(2)}) collective-permute-start(bf16[640,512]{1,0:T(8,128)(2,1)S(1)} %clip_turned.1.refs_10_), channel_id=1, source_target_pairs={{0,1},{1,0},{2,3},{3,2},{4,5},{5,4},{6,7},{7,6},{8,9},{9,8},{10,11... | collective-permute-start | bytes 1966088 | tf_op jit(solution)/shard_map/ppermute | solution.py:348
  7.9 1.9 %collective-permute-start.7 = (bf16[640,512]{1,0:T(8,128)(2,1)S(1)}, bf16[640,512]{1,0:T(8,128)(2,1)}, u32[]{:S(2)}, u32[]{:S(2)}) collective-permute-start(bf16[640,512]{1,0:T(8,128)(2,1)S(1)} %clip_turned.1.refs_10_), channel_id=1, source_target_pairs={{0,130},{1,131},{2,128},{3,129},{128,2},{129,3},{130,0},{131,1},{4... | collective-permute-start | bytes 1966088 | tf_op jit(solution)/shard_map/ppermute | solution.py:350
  9.8 0.6 pad_add_fusion.where
  10.4 2.5 %collective-permute-start.1 = (bf16[64,1792]{1,0:T(8,128)(2,1)S(1)}, bf16[64,1792]{1,0:T(8,128)(2,1)S(1)}, u32[]{:S(2)}, u32[]{:S(2)}) collective-permute-start(bf16[64,1792]{1,0:T(8,128)(2,1)S(1)} %collective-permute-done.own), channel_id=1, source_target_pairs={{0,8},{1,65},{2,10},{3,67},{4,12},{5,69},{6,14},{7,71},{8,16},{9,7... | collective-permute-start | bytes 688136 | tf_op jit(solution)/shard_map/ppermute | solution.py:58
  13.3 2.3 %collective-permute-start.3 = (bf16[64,1792]{1,0:T(8,128)(2,1)S(1)}, bf16[64,1792]{1,0:T(8,128)(2,1)S(1)}, u32[]{:S(2)}, u32[]{:S(2)}) collective-permute-start(bf16[64,1792]{1,0:T(8,128)(2,1)S(1)} %collective-permute-done.own), channel_id=1, source_target_pairs={{0,28},{1,97},{2,30},{3,99},{4,0},{5,101},{6,2},{7,103},{8,4},{9,1... | collective-permute-start | bytes 688136 | tf_op jit(solution)/shard_map/ppermute | solution.py:58
  15.6 1.2 collective-permute-done.1.c
  16.8 8.0 %collective-permute-start.8 = (bf16[640,512]{1,0:T(8,128)(2,1)S(1)}, bf16[640,512]{1,0:T(8,128)(2,1)S(1)}, u32[]{:S(2)}, u32[]{:S(2)}) collective-permute-start(bf16[640,512]{1,0:T(8,128)(2,1)S(1)} %clip_turned.1.refs_10_), channel_id=1, source_target_pairs={{0,131},{1,130},{2,129},{3,128},{128,3},{129,2},{130,1},{131,0},{4... | collective-permute-start | bytes 1966088 | tf_op jit(solution)/shard_map/ppermute | solution.py:350
  25.0 0.7 collective-permute-start.4
  25.7 0.7 collective-permute-start.5
  26.4 2.7 %collective-permute-start.9 = (bf16[256,896]{1,0:T(8,128)(2,1)S(1)}, bf16[256,896]{1,0:T(8,128)(2,1)}, u32[]{:S(2)}, u32[]{:S(2)}) collective-permute-start(bf16[256,896]{1,0:T(8,128)(2,1)S(1)} %get-tuple-element.39.refs_0_), channel_id=1, source_target_pairs={{0,32},{1,5},{2,34},{3,7},{4,36},{5,9},{6,38},{7,11},{8,40},{9,13}... | collective-permute-start | bytes 1376264 | tf_op jit(solution)/shard_map/ppermute | solution.py:58
  29.2 1.3 collective-permute-start.10
  30.5 9.6 %collective-permute-done.8.refs_13_ = bf16[640,512]{1,0:T(8,128)(2,1)S(1)} collective-permute-done((bf16[640,512]{1,0:T(8,128)(2,1)S(1)}, bf16[640,512]{1,0:T(8,128)(2,1)S(1)}, u32[]{:S(2)}, u32[]{:S(2)}) %collective-permute-start.8) | collective-permute-done | bytes 655392 | tf_op jit(solution)/shard_map/ppermute | solution.py:350
  40.1 2.3 %collective-permute-start.17 = (bf16[256,896]{1,0:T(8,128)(2,1)S(1)}, bf16[256,896]{1,0:T(8,128)(2,1)}, u32[]{:S(2)}, u32[]{:S(2)}) collective-permute-start(bf16[256,896]{1,0:T(8,128)(2,1)S(1)} %get-tuple-element.46.refs_10_.refs_0_), channel_id=1, source_target_pairs={{0,32},{1,5},{2,34},{3,7},{4,36},{5,9},{6,38},{7,11},{8,40},{9,13}... | collective-permute-start | bytes 1376264 | tf_op jit(solution)/shard_map/ppermute | solution.py:58
  42.4 2.5 %collective-permute-start.18 = (bf16[256,896]{1,0:T(8,128)(2,1)S(1)}, bf16[256,896]{1,0:T(8,128)(2,1)}, u32[]{:S(2)}, u32[]{:S(2)}) collective-permute-start(bf16[256,896]{1,0:T(8,128)(2,1)S(1)} %get-tuple-element.46.refs_10_.refs_0_), channel_id=1, source_target_pairs={{0,96},{1,29},{2,98},{3,31},{4,100},{5,1},{6,102},{7,3},{8,104},{9... | collective-permute-start | bytes 1376264 | tf_op jit(solution)/shard_map/ppermute | solution.py:58
  44.9 1.6 %collective-permute-start.11 = (bf16[256,896]{1,0:T(8,128)(2,1)}, bf16[256,896]{1,0:T(8,128)(2,1)}, u32[]{:S(2)}, u32[]{:S(2)}) collective-permute-start(bf16[256,896]{1,0:T(8,128)(2,1)} %collective-permute-done.9.refs_2_), channel_id=1, source_target_pairs={{0,32},{1,5},{2,34},{3,7},{4,36},{5,9},{6,38},{7,11},{8,40},{9,13}... | collective-permute-start | bytes 1376264 | tf_op jit(solution)/shard_map/ppermute | solution.py:58
  46.5 3.0 %collective-permute-start.12 = (bf16[256,896]{1,0:T(8,128)(2,1)}, bf16[256,896]{1,0:T(8,128)(2,1)}, u32[]{:S(2)}, u32[]{:S(2)}) collective-permute-start(bf16[256,896]{1,0:T(8,128)(2,1)} %collective-permute-done.10.refs_3_), channel_id=1, source_target_pairs={{1,29},{3,31},{5,1},{7,3},{9,5},{11,7},{13,9},{15,11},{17,13},{19,... | collective-permute-start | bytes 1376264 | tf_op jit(solution)/shard_map/ppermute | solution.py:58
  49.5 1.7 %collective-permute-done.17.refs_12_.refs_2_ = bf16[256,896]{1,0:T(8,128)(2,1)} collective-permute-done((bf16[256,896]{1,0:T(8,128)(2,1)S(1)}, bf16[256,896]{1,0:T(8,128)(2,1)}, u32[]{:S(2)}, u32[]{:S(2)}) %collective-permute-start.17) | collective-permute-done | bytes 458784 | tf_op jit(solution)/shard_map/ppermute | solution.py:58
  51.6 4.3 %collective-permute-start.20 = (bf16[256,896]{1,0:T(8,128)(2,1)}, bf16[256,896]{1,0:T(8,128)(2,1)}, u32[]{:S(2)}, u32[]{:S(2)}) collective-permute-start(bf16[256,896]{1,0:T(8,128)(2,1)} %collective-permute-done.18.refs_13_.refs_3_), channel_id=1, source_target_pairs={{1,29},{3,31},{5,1},{7,3},{9,5},{11,7},{13,9},{15,11},{17,13},{19,... | collective-permute-start | bytes 1376264 | tf_op jit(solution)/shard_map/ppermute | solution.py:58
  56.5 1.2 broadcast_select_fusion.2
  58.1 2.6 %collective-permute-start.14 = (bf16[256,896]{1,0:T(8,128)(2,1)S(1)}, bf16[256,896]{1,0:T(8,128)(2,1)S(1)}, u32[]{:S(2)}, u32[]{:S(2)}) collective-permute-start(bf16[256,896]{1,0:T(8,128)(2,1)S(1)} %get-tuple-element.54), channel_id=1, source_target_pairs={{0,96},{1,29},{2,98},{3,31},{4,100},{5,1},{6,102},{7,3},{8,104},{9... | collective-permute-start | bytes 1376264 | tf_op jit(solution)/shard_map/ppermute | solution.py:58
  60.7 0.7 collective-permute-done.19.refs_14_.refs_4_
  61.6 1.1 broadcast_select_fusion
  62.8 2.7 %collective-permute-start.21 = (bf16[256,896]{1,0:T(8,128)(2,1)S(1)}, bf16[256,896]{1,0:T(8,128)(2,1)S(1)}, u32[]{:S(2)}, u32[]{:S(2)}) collective-permute-start(bf16[256,896]{1,0:T(8,128)(2,1)S(1)} %get-tuple-element.53), channel_id=1, source_target_pairs={{0,32},{1,5},{2,34},{3,7},{4,36},{5,9},{6,38},{7,11},{8,40},{9,13}... | collective-permute-start | bytes 1376264 | tf_op jit(solution)/shard_map/ppermute | solution.py:58
  65.4 1.0 collective-permute-start.22
  66.8 1.1 collective-permute-start.15
  67.9 0.6 collective-permute-done.14.refs_7_
  68.5 1.4 %collective-permute-start.16 = (bf16[128,896]{1,0:T(8,128)(2,1)S(1)}, bf16[128,896]{1,0:T(8,128)(2,1)S(1)}, u32[]{:S(2)}, u32[]{:S(2)}) collective-permute-start(bf16[128,896]{1,0:T(8,128)(2,1)S(1)} %slice.25), channel_id=1, source_target_pairs={{0,96},{1,29},{2,98},{3,31},{4,100},{5,1},{6,102},{7,3},{8,104},{9... | collective-permute-start | bytes 688136 | tf_op jit(solution)/shard_map/ppermute | solution.py:58
  70.0 2.5 %collective-permute-done.21.refs_16_.refs_6_ = bf16[256,896]{1,0:T(8,128)(2,1)S(1)} collective-permute-done((bf16[256,896]{1,0:T(8,128)(2,1)S(1)}, bf16[256,896]{1,0:T(8,128)(2,1)S(1)}, u32[]{:S(2)}, u32[]{:S(2)}) %collective-permute-start.21) | collective-permute-done | bytes 458784 | tf_op jit(solution)/shard_map/ppermute | solution.py:58
  72.5 0.6 collective-permute-start.23
  73.6 1.8 %collective-permute-start.24 = (bf16[128,896]{1,0:T(8,128)(2,1)S(1)}, bf16[128,896]{1,0:T(8,128)(2,1)}, u32[]{:S(2)}, u32[]{:S(2)}) collective-permute-start(bf16[128,896]{1,0:T(8,128)(2,1)S(1)} %slice.27), channel_id=1, source_target_pairs={{0,96},{1,29},{2,98},{3,31},{4,100},{5,1},{6,102},{7,3},{8,104},{9... | collective-permute-start | bytes 688136 | tf_op jit(solution)/shard_map/ppermute | solution.py:58
  75.4 0.7 collective-permute-done.16.refs_9_
  76.1 0.7 copy-done.17
  76.8 7.7 %weight_term.2.mine = bf16[640,896]{1,0:T(8,128)(2,1)} custom-call(s32[3]{0:T(128)} %pad_add_fusion.where, bf16[256,896]{1,0:T(8,128)(2,1)} %copy-done.9, bf16[256,896]{1,0:T(8,128)(2,1)} %copy-done.4, bf16[256,896]{1,0:T(8,128)(2,1)} %collective-permute-done.9.refs_2_, bf16[256,896]{1,0:T(8,128)(2,1)} %collective-permute-done.10.refs_3_, ...), custom_call_target="tpu_custom_call" | custom-call | flops 2348810240 | bytes 7438336 | tf_op jit(solution)/shard_map/weight_term/pallas_call | solution.py:197
  84.5 0.6 collective-permute-start.27
  85.8 0.7 copy-done.15
  86.4 13.0 %act_parts.1 = (bf16[1024,640]{1,0:T(8,128)(2,1)}, bf16[1024,640]{1,0:T(8,128)(2,1)}) custom-call(s32[3]{0:T(128)} %pad_add_fusion.where, f32[1]{0:T(128)S(6)} %copy.11.weight_scale, bf16[1792,640]{1,0:T(8,128)(2,1)} %codes.1, bf16[256,896]{1,0:T(8,128)(2,1)} %copy-done.9, bf16[256,896]{1,0:T(8,128)(2,1)} %copy-done.4, ...), custom_call_target="tpu_custom_call" | custom-call | flops 1 | bytes 1 | tf_op jit(solution)/shard_map/act_parts/pallas_call | solution.py:286
  99.5 6.8 %collective-permute-start.25 = (bf16[1024,640]{1,0:T(8,128)(2,1)}, bf16[1024,640]{1,0:T(8,128)(2,1)S(1)}, u32[]{:S(2)}, u32[]{:S(2)}) collective-permute-start(bf16[1024,640]{1,0:T(8,128)(2,1)} %get-tuple-element.45), channel_id=1, source_target_pairs={{0,1},{1,0},{2,3},{3,2},{4,5},{5,4},{6,7},{7,6},{8,9},{9,8},{10,11... | collective-permute-start | bytes 3932168 | tf_op jit(solution)/shard_map/ppermute | solution.py:367
  106.4 7.7 %weight_term.3.mine = bf16[640,896]{1,0:T(8,128)(2,1)} custom-call(s32[3]{0:T(128)} %pad_add_fusion.where, bf16[256,896]{1,0:T(8,128)(2,1)} %copy-done.8, bf16[256,896]{1,0:T(8,128)(2,1)} %copy-done.3, bf16[256,896]{1,0:T(8,128)(2,1)} %collective-permute-done.17.refs_12_.refs_2_, bf16[256,896]{1,0:T(8,128)(2,1)} %collective-permute-done.18.refs_13_.refs_3_, ...), custom_call_target="tpu_custom_call" | custom-call | flops 2348810240 | bytes 7438336 | tf_op jit(solution)/shard_map/weight_term/pallas_call | solution.py:197
  114.5 3.6 %collective-permute-start.26 = (bf16[512,640]{1,0:T(8,128)(2,1)S(1)}, bf16[512,640]{1,0:T(8,128)(2,1)S(1)}, u32[]{:S(2)}, u32[]{:S(2)}) collective-permute-start(bf16[512,640]{1,0:T(8,128)(2,1)S(1)} %add_convert_fusion), channel_id=1, source_target_pairs={{0,130},{1,131},{2,128},{3,129},{128,2},{129,3},{130,0},{131,1},{4... | collective-permute-start | bytes 1966088 | tf_op jit(solution)/shard_map/ppermute | solution.py:371
  118.2 1.6 %sum_terms.2.refs_0_ = f32[1792,640]{1,0:T(8,128)} custom-call(bf16[640,896]{1,0:T(8,128)(2,1)S(1)} %copy-done.5, bf16[640,896]{1,0:T(8,128)(2,1)S(1)} %collective-permute-done.27.theirs), custom_call_target="tpu_custom_call" | custom-call | tf_op jit(solution)/shard_map/sum_terms/pallas_call | solution.py:238
  119.8 13.0 %collective-permute-done.26.other = bf16[512,640]{1,0:T(8,128)(2,1)S(1)} collective-permute-done((bf16[512,640]{1,0:T(8,128)(2,1)S(1)}, bf16[512,640]{1,0:T(8,128)(2,1)S(1)}, u32[]{:S(2)}, u32[]{:S(2)}) %collective-permute-start.26) | collective-permute-done | bytes 655392 | tf_op jit(solution)/shard_map/ppermute | solution.py:371
  132.8 1.7 %finish.1 = bf16[512,640]{1,0:T(8,128)(2,1)} custom-call(bf16[1024,640]{1,0:T(8,128)(2,1)S(1)} %copy-done, bf16[1024,640]{1,0:T(8,128)(2,1)S(1)} %collective-permute-done.25.got, bf16[512,640]{1,0:T(8,128)(2,1)S(1)} %collective-permute-done.26.other, bf16[512,640]{1,0:T(8,128)(2,1)S(1)} %copy-done.2, f32[512,1]{1,0:T(8,128)S(1)} %copy.8.bound, ...), custom_call_target="tpu_custom_call" | custom-call | tf_op jit(solution)/shard_map/finish/pallas_call | solution.py:318
  134.5 6.6 %collective-permute-done.28.theirs = bf16[640,896]{1,0:T(8,128)(2,1)S(1)} collective-permute-done((bf16[640,896]{1,0:T(8,128)(2,1)}, bf16[640,896]{1,0:T(8,128)(2,1)S(1)}, u32[]{:S(2)}, u32[]{:S(2)}) %collective-permute-start.28) | collective-permute-done | bytes 1146912 | tf_op jit(solution)/shard_map/ppermute | solution.py:370
  141.1 1.6 %sum_terms.3 = f32[1792,640]{1,0:T(8,128)} custom-call(bf16[640,896]{1,0:T(8,128)(2,1)S(1)} %copy-done.6, bf16[640,896]{1,0:T(8,128)(2,1)S(1)} %collective-permute-done.28.theirs, f32[1792,640]{1,0:T(8,128)} %sum_terms.2.refs_0_), custom_call_target="tpu_custom_call", output_to_operand_aliasing={{}: (2, {})} | custom-call | tf_op jit(solution)/shard_map/sum_terms/pallas_call | solution.py:238
  (69 shorter events, 3.4 us)
Async XLA Ops:
  0.6 9.8 %collective-permute-start = (bf16[64,1792]{1,0:T(8,128)(2,1)}, bf16[64,1792]{1,0:T(8,128)(2,1)S(1)}, u32[]{:S(2)}, u32[]{:S(2)}) collective-permute-start(bf16[64,1792]{1,0:T(8,128)(2,1)} %param.5), channel_id=1, source_target_pairs={{0,0},{1,1},{2,130},{3,131},{4,4},{5,5},{6,134},{7,135},{8,8},{9,9... | collective-permute-start | bytes 688136 | tf_op jit(solution)/shard_map/ppermute | solution.py:58
  3.1 1.1 copy-start.1
  4.6 53.2 %copy-start.7 = (bf16[640,512]{1,0:T(8,128)(2,1)}, bf16[640,512]{1,0:T(8,128)(2,1)S(1)}, u32[]{:S(2)}) copy-start(bf16[640,512]{1,0:T(8,128)(2,1)S(1)} %clip_turned.1.refs_10_) | copy-start | bytes 1966084
  4.6 21.8 %collective-permute-start.6 = (bf16[640,512]{1,0:T(8,128)(2,1)S(1)}, bf16[640,512]{1,0:T(8,128)(2,1)S(1)}, u32[]{:S(2)}, u32[]{:S(2)}) collective-permute-start(bf16[640,512]{1,0:T(8,128)(2,1)S(1)} %clip_turned.1.refs_10_), channel_id=1, source_target_pairs={{0,1},{1,0},{2,3},{3,2},{4,5},{5,4},{6,7},{7,6},{8,9},{9,8},{10,11... | collective-permute-start | bytes 1966088 | tf_op jit(solution)/shard_map/ppermute | solution.py:348
  7.9 21.2 %collective-permute-start.7 = (bf16[640,512]{1,0:T(8,128)(2,1)S(1)}, bf16[640,512]{1,0:T(8,128)(2,1)}, u32[]{:S(2)}, u32[]{:S(2)}) collective-permute-start(bf16[640,512]{1,0:T(8,128)(2,1)S(1)} %clip_turned.1.refs_10_), channel_id=1, source_target_pairs={{0,130},{1,131},{2,128},{3,129},{128,2},{129,3},{130,0},{131,1},{4... | collective-permute-start | bytes 1966088 | tf_op jit(solution)/shard_map/ppermute | solution.py:350
  10.4 6.4 %collective-permute-start.1 = (bf16[64,1792]{1,0:T(8,128)(2,1)S(1)}, bf16[64,1792]{1,0:T(8,128)(2,1)S(1)}, u32[]{:S(2)}, u32[]{:S(2)}) collective-permute-start(bf16[64,1792]{1,0:T(8,128)(2,1)S(1)} %collective-permute-done.own), channel_id=1, source_target_pairs={{0,8},{1,65},{2,10},{3,67},{4,12},{5,69},{6,14},{7,71},{8,16},{9,7... | collective-permute-start | bytes 688136 | tf_op jit(solution)/shard_map/ppermute | solution.py:58
  12.9 11.9 %collective-permute-start.2 = (bf16[64,1792]{1,0:T(8,128)(2,1)S(1)}, bf16[64,1792]{1,0:T(8,128)(2,1)S(1)}, u32[]{:S(2)}, u32[]{:S(2)}) collective-permute-start(bf16[64,1792]{1,0:T(8,128)(2,1)S(1)} %collective-permute-done.own), channel_id=1, source_target_pairs={{0,4},{1,33},{2,6},{3,35},{4,8},{5,37},{6,10},{7,39},{8,12},{9,41}... | collective-permute-start | bytes 688136 | tf_op jit(solution)/shard_map/ppermute | solution.py:58
  13.3 11.5 %collective-permute-start.3 = (bf16[64,1792]{1,0:T(8,128)(2,1)S(1)}, bf16[64,1792]{1,0:T(8,128)(2,1)S(1)}, u32[]{:S(2)}, u32[]{:S(2)}) collective-permute-start(bf16[64,1792]{1,0:T(8,128)(2,1)S(1)} %collective-permute-done.own), channel_id=1, source_target_pairs={{0,28},{1,97},{2,30},{3,99},{4,0},{5,101},{6,2},{7,103},{8,4},{9,1... | collective-permute-start | bytes 688136 | tf_op jit(solution)/shard_map/ppermute | solution.py:58
  16.8 23.2 %collective-permute-start.8 = (bf16[640,512]{1,0:T(8,128)(2,1)S(1)}, bf16[640,512]{1,0:T(8,128)(2,1)S(1)}, u32[]{:S(2)}, u32[]{:S(2)}) collective-permute-start(bf16[640,512]{1,0:T(8,128)(2,1)S(1)} %clip_turned.1.refs_10_), channel_id=1, source_target_pairs={{0,131},{1,130},{2,129},{3,128},{128,3},{129,2},{130,1},{131,0},{4... | collective-permute-start | bytes 1966088 | tf_op jit(solution)/shard_map/ppermute | solution.py:350
  25.0 32.8 %copy-start.8 = (bf16[256,896]{1,0:T(8,128)(2,1)}, bf16[256,896]{1,0:T(8,128)(2,1)S(1)}, u32[]{:S(2)}) copy-start(bf16[256,896]{1,0:T(8,128)(2,1)S(1)} %get-tuple-element.46.refs_10_.refs_0_) | copy-start | bytes 1376260
  25.0 32.8 %copy-start.9 = (bf16[256,896]{1,0:T(8,128)(2,1)}, bf16[256,896]{1,0:T(8,128)(2,1)S(1)}, u32[]{:S(2)}) copy-start(bf16[256,896]{1,0:T(8,128)(2,1)S(1)} %get-tuple-element.39.refs_0_) | copy-start | bytes 1376260
  25.0 15.1 %collective-permute-start.4 = (bf16[128,1792]{1,0:T(8,128)(2,1)S(1)}, bf16[128,1792]{1,0:T(8,128)(2,1)S(1)}, u32[]{:S(2)}, u32[]{:S(2)}) collective-permute-start(bf16[128,1792]{1,0:T(8,128)(2,1)S(1)} %get-tuple-element.31), channel_id=1, source_target_pairs={{0,8},{2,10},{4,12},{6,14},{8,16},{10,18},{12,20},{14,22},{16,24},... | collective-permute-start | bytes 1376264 | tf_op jit(solution)/shard_map/ppermute | solution.py:58
  25.7 14.4 %collective-permute-start.5 = (bf16[128,1792]{1,0:T(8,128)(2,1)S(1)}, bf16[128,1792]{1,0:T(8,128)(2,1)S(1)}, u32[]{:S(2)}, u32[]{:S(2)}) collective-permute-start(bf16[128,1792]{1,0:T(8,128)(2,1)S(1)} %get-tuple-element.32), channel_id=1, source_target_pairs={{0,24},{2,26},{4,28},{6,30},{8,0},{10,2},{12,4},{14,6},{16,8},{18,... | collective-permute-start | bytes 1376264 | tf_op jit(solution)/shard_map/ppermute | solution.py:58
  26.4 23.1 %copy-start.18 = (bf16[640,512]{1,0:T(8,128)(2,1)}, bf16[640,512]{1,0:T(8,128)(2,1)S(1)}, u32[]{:S(2)}) copy-start(bf16[640,512]{1,0:T(8,128)(2,1)S(1)} %collective-permute-done.6.refs_11_) | copy-start | bytes 1966084
  26.4 18.5 %collective-permute-start.9 = (bf16[256,896]{1,0:T(8,128)(2,1)S(1)}, bf16[256,896]{1,0:T(8,128)(2,1)}, u32[]{:S(2)}, u32[]{:S(2)}) collective-permute-start(bf16[256,896]{1,0:T(8,128)(2,1)S(1)} %get-tuple-element.39.refs_0_), channel_id=1, source_target_pairs={{0,32},{1,5},{2,34},{3,7},{4,36},{5,9},{6,38},{7,11},{8,40},{9,13}... | collective-permute-start | bytes 1376264 | tf_op jit(solution)/shard_map/ppermute | solution.py:58
  29.2 17.3 %collective-permute-start.10 = (bf16[256,896]{1,0:T(8,128)(2,1)S(1)}, bf16[256,896]{1,0:T(8,128)(2,1)}, u32[]{:S(2)}, u32[]{:S(2)}) collective-permute-start(bf16[256,896]{1,0:T(8,128)(2,1)S(1)} %get-tuple-element.39.refs_0_), channel_id=1, source_target_pairs={{0,96},{1,29},{2,98},{3,31},{4,100},{5,1},{6,102},{7,3},{8,104},{9... | collective-permute-start | bytes 1376264 | tf_op jit(solution)/shard_map/ppermute | solution.py:58
  40.0 11.6 %copy-start.19 = (bf16[640,512]{1,0:T(8,128)(2,1)}, bf16[640,512]{1,0:T(8,128)(2,1)S(1)}, u32[]{:S(2)}) copy-start(bf16[640,512]{1,0:T(8,128)(2,1)S(1)} %collective-permute-done.8.refs_13_) | copy-start | bytes 1966084
  40.1 11.2 %collective-permute-start.17 = (bf16[256,896]{1,0:T(8,128)(2,1)S(1)}, bf16[256,896]{1,0:T(8,128)(2,1)}, u32[]{:S(2)}, u32[]{:S(2)}) collective-permute-start(bf16[256,896]{1,0:T(8,128)(2,1)S(1)} %get-tuple-element.46.refs_10_.refs_0_), channel_id=1, source_target_pairs={{0,32},{1,5},{2,34},{3,7},{4,36},{5,9},{6,38},{7,11},{8,40},{9,13}... | collective-permute-start | bytes 1376264 | tf_op jit(solution)/shard_map/ppermute | solution.py:58
  42.4 9.3 %collective-permute-start.18 = (bf16[256,896]{1,0:T(8,128)(2,1)S(1)}, bf16[256,896]{1,0:T(8,128)(2,1)}, u32[]{:S(2)}, u32[]{:S(2)}) collective-permute-start(bf16[256,896]{1,0:T(8,128)(2,1)S(1)} %get-tuple-element.46.refs_10_.refs_0_), channel_id=1, source_target_pairs={{0,96},{1,29},{2,98},{3,31},{4,100},{5,1},{6,102},{7,3},{8,104},{9... | collective-permute-start | bytes 1376264 | tf_op jit(solution)/shard_map/ppermute | solution.py:58
  44.9 11.5 %collective-permute-start.11 = (bf16[256,896]{1,0:T(8,128)(2,1)}, bf16[256,896]{1,0:T(8,128)(2,1)}, u32[]{:S(2)}, u32[]{:S(2)}) collective-permute-start(bf16[256,896]{1,0:T(8,128)(2,1)} %collective-permute-done.9.refs_2_), channel_id=1, source_target_pairs={{0,32},{1,5},{2,34},{3,7},{4,36},{5,9},{6,38},{7,11},{8,40},{9,13}... | collective-permute-start | bytes 1376264 | tf_op jit(solution)/shard_map/ppermute | solution.py:58
  46.5 10.1 %collective-permute-start.12 = (bf16[256,896]{1,0:T(8,128)(2,1)}, bf16[256,896]{1,0:T(8,128)(2,1)}, u32[]{:S(2)}, u32[]{:S(2)}) collective-permute-start(bf16[256,896]{1,0:T(8,128)(2,1)} %collective-permute-done.10.refs_3_), channel_id=1, source_target_pairs={{1,29},{3,31},{5,1},{7,3},{9,5},{11,7},{13,9},{15,11},{17,13},{19,... | collective-permute-start | bytes 1376264 | tf_op jit(solution)/shard_map/ppermute | solution.py:58
  51.2 10.1 %collective-permute-start.19 = (bf16[256,896]{1,0:T(8,128)(2,1)}, bf16[256,896]{1,0:T(8,128)(2,1)S(1)}, u32[]{:S(2)}, u32[]{:S(2)}) collective-permute-start(bf16[256,896]{1,0:T(8,128)(2,1)} %collective-permute-done.17.refs_12_.refs_2_), channel_id=1, source_target_pairs={{0,32},{1,5},{2,34},{3,7},{4,36},{5,9},{6,38},{7,11},{8,40},{9,13}... | collective-permute-start | bytes 1376264 | tf_op jit(solution)/shard_map/ppermute | solution.py:58
  51.6 10.0 %collective-permute-start.20 = (bf16[256,896]{1,0:T(8,128)(2,1)}, bf16[256,896]{1,0:T(8,128)(2,1)}, u32[]{:S(2)}, u32[]{:S(2)}) collective-permute-start(bf16[256,896]{1,0:T(8,128)(2,1)} %collective-permute-done.18.refs_13_.refs_3_), channel_id=1, source_target_pairs={{1,29},{3,31},{5,1},{7,3},{9,5},{11,7},{13,9},{15,11},{17,13},{19,... | collective-permute-start | bytes 1376264 | tf_op jit(solution)/shard_map/ppermute | solution.py:58
  56.0 6.7 %copy-start.3 = (bf16[256,896]{1,0:T(8,128)(2,1)}, bf16[256,896]{1,0:T(8,128)(2,1)S(1)}, u32[]{:S(2)}) copy-start(bf16[256,896]{1,0:T(8,128)(2,1)S(1)} %get-tuple-element.41.refs_11_.refs_1_) | copy-start | bytes 1376260
  56.0 6.7 %copy-start.4 = (bf16[256,896]{1,0:T(8,128)(2,1)}, bf16[256,896]{1,0:T(8,128)(2,1)S(1)}, u32[]{:S(2)}) copy-start(bf16[256,896]{1,0:T(8,128)(2,1)S(1)} %get-tuple-element.35.refs_1_) | copy-start | bytes 1376260
  57.8 8.9 %collective-permute-start.13 = (bf16[256,896]{1,0:T(8,128)(2,1)S(1)}, bf16[256,896]{1,0:T(8,128)(2,1)S(1)}, u32[]{:S(2)}, u32[]{:S(2)}) collective-permute-start(bf16[256,896]{1,0:T(8,128)(2,1)S(1)} %get-tuple-element.55), channel_id=1, source_target_pairs={{0,32},{1,5},{2,34},{3,7},{4,36},{5,9},{6,38},{7,11},{8,40},{9,13}... | collective-permute-start | bytes 1376264 | tf_op jit(solution)/shard_map/ppermute | solution.py:58
  58.1 10.4 %collective-permute-start.14 = (bf16[256,896]{1,0:T(8,128)(2,1)S(1)}, bf16[256,896]{1,0:T(8,128)(2,1)S(1)}, u32[]{:S(2)}, u32[]{:S(2)}) collective-permute-start(bf16[256,896]{1,0:T(8,128)(2,1)S(1)} %get-tuple-element.54), channel_id=1, source_target_pairs={{0,96},{1,29},{2,98},{3,31},{4,100},{5,1},{6,102},{7,3},{8,104},{9... | collective-permute-start | bytes 1376264 | tf_op jit(solution)/shard_map/ppermute | solution.py:58
  61.3 5.4 %copy-start.10 = (bf16[256,896]{1,0:T(8,128)(2,1)}, bf16[256,896]{1,0:T(8,128)(2,1)S(1)}, u32[]{:S(2)}) copy-start(bf16[256,896]{1,0:T(8,128)(2,1)S(1)} %collective-permute-done.19.refs_14_.refs_4_) | copy-start | bytes 1376260
  62.8 9.7 %collective-permute-start.21 = (bf16[256,896]{1,0:T(8,128)(2,1)S(1)}, bf16[256,896]{1,0:T(8,128)(2,1)S(1)}, u32[]{:S(2)}, u32[]{:S(2)}) collective-permute-start(bf16[256,896]{1,0:T(8,128)(2,1)S(1)} %get-tuple-element.53), channel_id=1, source_target_pairs={{0,32},{1,5},{2,34},{3,7},{4,36},{5,9},{6,38},{7,11},{8,40},{9,13}... | collective-permute-start | bytes 1376264 | tf_op jit(solution)/shard_map/ppermute | solution.py:58
  65.4 8.1 %collective-permute-start.22 = (bf16[256,896]{1,0:T(8,128)(2,1)S(1)}, bf16[256,896]{1,0:T(8,128)(2,1)S(1)}, u32[]{:S(2)}, u32[]{:S(2)}) collective-permute-start(bf16[256,896]{1,0:T(8,128)(2,1)S(1)} %get-tuple-element.52), channel_id=1, source_target_pairs={{0,96},{1,29},{2,98},{3,31},{4,100},{5,1},{6,102},{7,3},{8,104},{9... | collective-permute-start | bytes 1376264 | tf_op jit(solution)/shard_map/ppermute | solution.py:58
  66.7 9.3 %copy-start.12 = (bf16[256,896]{1,0:T(8,128)(2,1)}, bf16[256,896]{1,0:T(8,128)(2,1)S(1)}, u32[]{:S(2)}) copy-start(bf16[256,896]{1,0:T(8,128)(2,1)S(1)} %collective-permute-done.13.refs_6_) | copy-start | bytes 1376260
  66.8 8.6 %collective-permute-start.15 = (bf16[128,896]{1,0:T(8,128)(2,1)S(1)}, bf16[128,896]{1,0:T(8,128)(2,1)S(1)}, u32[]{:S(2)}, u32[]{:S(2)}) collective-permute-start(bf16[128,896]{1,0:T(8,128)(2,1)S(1)} %slice.24), channel_id=1, source_target_pairs={{0,32},{1,5},{2,34},{3,7},{4,36},{5,9},{6,38},{7,11},{8,40},{9,13}... | collective-permute-start | bytes 688136 | tf_op jit(solution)/shard_map/ppermute | solution.py:58
  68.5 7.5 %copy-start.14 = (bf16[256,896]{1,0:T(8,128)(2,1)}, bf16[256,896]{1,0:T(8,128)(2,1)S(1)}, u32[]{:S(2)}) copy-start(bf16[256,896]{1,0:T(8,128)(2,1)S(1)} %collective-permute-done.14.refs_7_) | copy-start | bytes 1376260
  68.5 7.5 %collective-permute-start.16 = (bf16[128,896]{1,0:T(8,128)(2,1)S(1)}, bf16[128,896]{1,0:T(8,128)(2,1)S(1)}, u32[]{:S(2)}, u32[]{:S(2)}) collective-permute-start(bf16[128,896]{1,0:T(8,128)(2,1)S(1)} %slice.25), channel_id=1, source_target_pairs={{0,96},{1,29},{2,98},{3,31},{4,100},{5,1},{6,102},{7,3},{8,104},{9... | collective-permute-start | bytes 688136 | tf_op jit(solution)/shard_map/ppermute | solution.py:58
  72.5 12.0 %copy-start.11 = (bf16[256,896]{1,0:T(8,128)(2,1)}, bf16[256,896]{1,0:T(8,128)(2,1)S(1)}, u32[]{:S(2)}) copy-start(bf16[256,896]{1,0:T(8,128)(2,1)S(1)} %collective-permute-done.21.refs_16_.refs_6_) | copy-start | bytes 1376260
  72.5 13.2 %collective-permute-start.23 = (bf16[128,896]{1,0:T(8,128)(2,1)S(1)}, bf16[128,896]{1,0:T(8,128)(2,1)S(1)}, u32[]{:S(2)}, u32[]{:S(2)}) collective-permute-start(bf16[128,896]{1,0:T(8,128)(2,1)S(1)} %slice.26), channel_id=1, source_target_pairs={{0,32},{1,5},{2,34},{3,7},{4,36},{5,9},{6,38},{7,11},{8,40},{9,13}... | collective-permute-start | bytes 688136 | tf_op jit(solution)/shard_map/ppermute | solution.py:58
  73.6 10.9 %copy-start.13 = (bf16[256,896]{1,0:T(8,128)(2,1)}, bf16[256,896]{1,0:T(8,128)(2,1)S(1)}, u32[]{:S(2)}) copy-start(bf16[256,896]{1,0:T(8,128)(2,1)S(1)} %collective-permute-done.22.refs_17_.refs_7_) | copy-start | bytes 1376260
  73.6 12.2 %collective-permute-start.24 = (bf16[128,896]{1,0:T(8,128)(2,1)S(1)}, bf16[128,896]{1,0:T(8,128)(2,1)}, u32[]{:S(2)}, u32[]{:S(2)}) collective-permute-start(bf16[128,896]{1,0:T(8,128)(2,1)S(1)} %slice.27), channel_id=1, source_target_pairs={{0,96},{1,29},{2,98},{3,31},{4,100},{5,1},{6,102},{7,3},{8,104},{9... | collective-permute-start | bytes 688136 | tf_op jit(solution)/shard_map/ppermute | solution.py:58
  76.1 0.7 copy-start.17
  84.5 29.6 %collective-permute-start.27 = (bf16[640,896]{1,0:T(8,128)(2,1)}, bf16[640,896]{1,0:T(8,128)(2,1)S(1)}, u32[]{:S(2)}, u32[]{:S(2)}) collective-permute-start(bf16[640,896]{1,0:T(8,128)(2,1)} %weight_term.2.mine), channel_id=1, source_target_pairs={{0,128},{128,0},{1,129},{129,1},{2,130},{130,2},{3,131},{131,3},{4... | collective-permute-start | bytes 3440648 | tf_op jit(solution)/shard_map/ppermute | solution.py:361
  85.7 0.7 copy-start.15
  99.5 14.8 %copy-start = (bf16[1024,640]{1,0:T(8,128)(2,1)S(1)}, bf16[1024,640]{1,0:T(8,128)(2,1)}, u32[]{:S(2)}) copy-start(bf16[1024,640]{1,0:T(8,128)(2,1)} %get-tuple-element.44.keep) | copy-start | bytes 3932164
  99.5 14.8 %collective-permute-start.25 = (bf16[1024,640]{1,0:T(8,128)(2,1)}, bf16[1024,640]{1,0:T(8,128)(2,1)S(1)}, u32[]{:S(2)}, u32[]{:S(2)}) collective-permute-start(bf16[1024,640]{1,0:T(8,128)(2,1)} %get-tuple-element.45), channel_id=1, source_target_pairs={{0,1},{1,0},{2,3},{3,2},{4,5},{5,4},{6,7},{7,6},{8,9},{9,8},{10,11... | collective-permute-start | bytes 3932168 | tf_op jit(solution)/shard_map/ppermute | solution.py:367
  114.1 4.1 %copy-start.5 = (bf16[640,896]{1,0:T(8,128)(2,1)S(1)}, bf16[640,896]{1,0:T(8,128)(2,1)}, u32[]{:S(2)}) copy-start(bf16[640,896]{1,0:T(8,128)(2,1)} %weight_term.2.mine) | copy-start | bytes 3440644
  114.1 27.0 %collective-permute-start.28 = (bf16[640,896]{1,0:T(8,128)(2,1)}, bf16[640,896]{1,0:T(8,128)(2,1)S(1)}, u32[]{:S(2)}, u32[]{:S(2)}) collective-permute-start(bf16[640,896]{1,0:T(8,128)(2,1)} %weight_term.3.mine), channel_id=1, source_target_pairs={{0,128},{128,0},{1,129},{129,1},{2,130},{130,2},{3,131},{131,3},{4... | collective-permute-start | bytes 3440648 | tf_op jit(solution)/shard_map/ppermute | solution.py:370
  114.5 18.3 %collective-permute-start.26 = (bf16[512,640]{1,0:T(8,128)(2,1)S(1)}, bf16[512,640]{1,0:T(8,128)(2,1)S(1)}, u32[]{:S(2)}, u32[]{:S(2)}) collective-permute-start(bf16[512,640]{1,0:T(8,128)(2,1)S(1)} %add_convert_fusion), channel_id=1, source_target_pairs={{0,130},{1,131},{2,128},{3,129},{128,2},{129,3},{130,0},{131,1},{4... | collective-permute-start | bytes 1966088 | tf_op jit(solution)/shard_map/ppermute | solution.py:371
  118.1 14.7 %copy-start.2 = (bf16[512,640]{1,0:T(8,128)(2,1)S(1)}, bf16[512,640]{1,0:T(8,128)(2,1)}, u32[]{:S(2)}) copy-start(bf16[512,640]{1,0:T(8,128)(2,1)} %rotated.3) | copy-start | bytes 1966084
  119.8 21.3 %copy-start.6 = (bf16[640,896]{1,0:T(8,128)(2,1)S(1)}, bf16[640,896]{1,0:T(8,128)(2,1)}, u32[]{:S(2)}) copy-start(bf16[640,896]{1,0:T(8,128)(2,1)} %weight_term.3.mine) | copy-start | bytes 3440644
  (1 other events, 0.7 us)
